TPU v7x, 128 devices: a whole 4x4x4 slice. The times are simulated.
128 devices in a mesh: dp: 8 (over x_lo, y), seq: 16 (over z, x_hi, core).
Axes of the slice: x: 4 (x_hi: 2, x_lo: 2; x = x_hi * 2 + x_lo), y: 4, z: 4, core: 2. Of those that a mesh axis runs over, the one named last changes fastest.
Arguments:
- queries: bfloat16 [16384, 1152], P(('dp', 'seq')), may hold values from -6 to 6
- keys: bfloat16 [16384, 1152], P(('dp', 'seq')), may hold values from -6 to 6
- values: bfloat16 [16384, 1152], P(('dp', 'seq')), may hold values from -6 to 6
- out_grad: bfloat16 [16384, 1152], P(('dp', 'seq')), may hold values from -24 to 24
- out_weight: bfloat16 [1152, 1152], replicated, may hold values from -0.1875 to 0.1875
- extents: int32 [8, 8], P('dp'), may hold values from 1 to 16, 32 in all within a row
Outputs:
- query_grad: bfloat16 [16384, 1152], P(('dp', 'seq'))
- key_grad: bfloat16 [16384, 1152], P(('dp', 'seq'))
- value_grad: bfloat16 [16384, 1152], P(('dp', 'seq'))
- weight_grad: float32 [1152, 1152], P('seq', 'dp')
Inputs may be any that keep to these rules, and one draw needn't show every extreme that they name: `extents`: row i lists the 8 images packed in order into sequence i, in units of 64 tokens; each row sums to 32.
All inputs are finite; a program needn't handle non-finite values.
Results may differ from a plain program's by a relative error of at most 0.034.
Values may be sent and summed in bfloat16 or wider, within the bound.
No kernel may reach another device: no remote copies, remote signals or barrier semaphores. Data moves between devices by JAX's collectives and lax.ppermute only.
A program may use at most 128 MiB of HBM per device.

v0:
```python
import math

import jax
import jax.numpy as jnp
from jax import lax
from jax.sharding import PartitionSpec as P

HEADS = 16
HEAD = 72
UNIT = 64


def local(queries, keys, values, out_grad, out_weight, extents):
    local_rows = queries.shape[0]
    model_width = queries.shape[1]
    seq_parts = lax.axis_size("seq")
    seq_length = local_rows * seq_parts
    block_len = math.gcd(seq_length, 512)
    num_blocks = seq_length // block_len
    score_scale = HEAD ** (-0.5)
    position = jnp.arange(seq_length, dtype=jnp.int32)
    image_ends = jnp.cumsum(extents[0]) * UNIT
    segment_all = jnp.sum((position[:, None] >= image_ends[None, :]).astype(jnp.int32), axis=1)
    segment_mine = lax.dynamic_slice_in_dim(
        segment_all, lax.axis_index("seq") * local_rows, local_rows
    )
    out_back = lax.dot_general(
        out_grad, out_weight, (((1,), (1,)), ((), ())), preferred_element_type=jnp.float32
    ).astype(jnp.bfloat16)
    key_all, value_all = (
        lax.all_gather(keys, "seq", axis=0, tiled=True),
        lax.all_gather(values, "seq", axis=0, tiled=True),
    )
    query_heads = queries.reshape(local_rows, HEADS, HEAD)
    key_heads = keys.reshape(local_rows, HEADS, HEAD)
    value_heads = values.reshape(local_rows, HEADS, HEAD)
    back_heads = out_back.reshape(local_rows, HEADS, HEAD)
    key_blocks = key_all.reshape(num_blocks, block_len, HEADS, HEAD)
    value_blocks = value_all.reshape(num_blocks, block_len, HEADS, HEAD)
    segment_blocks = segment_all.reshape(num_blocks, block_len)

    def mask_for(seg_block):
        return (segment_mine[:, None] == seg_block[None, :])[None]

    def query_scores(key_block):
        return (
            jnp.einsum("qhd,khd->hqk", query_heads, key_block, preferred_element_type=jnp.float32)
            * score_scale
        )

    def grow_total(carry, inputs):
        top_now, total_now = carry
        key_block, seg_block = inputs
        scores = query_scores(key_block)
        inside = mask_for(seg_block)
        top_next = jnp.maximum(top_now, jnp.max(jnp.where(inside, scores, -1e30), axis=2))
        total_next = total_now * jnp.exp(top_now - top_next) + jnp.sum(
            jnp.where(inside, jnp.exp(scores - top_next[:, :, None]), 0.0), axis=2
        )
        return ((top_next, total_next), None)

    start_top = jnp.full((HEADS, local_rows), -1e30, jnp.float32)
    start_total = jnp.zeros((HEADS, local_rows), jnp.float32)
    (top_all, total_all), unused = lax.scan(
        grow_total, (start_top, start_total), (key_blocks, segment_blocks)
    )
    log_total = top_all + jnp.log(total_all)

    def attend_block(carry, inputs):
        key_block, value_block, seg_block = inputs
        scores = query_scores(key_block)
        probs_low = jnp.where(
            mask_for(seg_block), jnp.exp(scores - log_total[:, :, None]), 0.0
        ).astype(jnp.bfloat16)
        return (
            carry
            + jnp.einsum(
                "hqk,khd->qhd", probs_low, value_block, preferred_element_type=jnp.float32
            ),
            None,
        )

    summed, unused = lax.scan(
        attend_block,
        jnp.zeros((local_rows, HEADS, HEAD), jnp.float32),
        (key_blocks, value_blocks, segment_blocks),
    )
    attended = summed.astype(jnp.bfloat16).reshape(local_rows, model_width)
    delta_rows = jnp.sum(
        (out_back.astype(jnp.float32) * attended.astype(jnp.float32)).reshape(
            local_rows, HEADS, HEAD
        ),
        axis=2,
    )
    lse_all, delta_all = (
        lax.all_gather(log_total.T, "seq", axis=0, tiled=True),
        lax.all_gather(delta_rows, "seq", axis=0, tiled=True),
    )
    query_all, back_all = (
        lax.all_gather(queries, "seq", axis=0, tiled=True),
        lax.all_gather(out_back, "seq", axis=0, tiled=True),
    )

    def query_side(carry, inputs):
        key_block, value_block, seg_block = inputs
        scores = query_scores(key_block)
        probs = jnp.where(mask_for(seg_block), jnp.exp(scores - log_total[:, :, None]), 0.0)
        dprobs = jnp.einsum(
            "qhd,khd->hqk", back_heads, value_block, preferred_element_type=jnp.float32
        )
        dscores = (probs * (dprobs - delta_rows.T[:, :, None])).astype(jnp.bfloat16)
        return (
            carry
            + jnp.einsum("hqk,khd->qhd", dscores, key_block, preferred_element_type=jnp.float32),
            None,
        )

    query_acc, unused = lax.scan(
        query_side,
        jnp.zeros((local_rows, HEADS, HEAD), jnp.float32),
        (key_blocks, value_blocks, segment_blocks),
    )
    query_grad = (query_acc * score_scale).astype(jnp.bfloat16).reshape(local_rows, model_width)
    query_blocks = query_all.reshape(num_blocks, block_len, HEADS, HEAD)
    back_blocks = back_all.reshape(num_blocks, block_len, HEADS, HEAD)
    lse_blocks = lse_all.reshape(num_blocks, block_len, HEADS)
    delta_blocks = delta_all.reshape(num_blocks, block_len, HEADS)

    def key_side(carry, inputs):
        key_acc, value_acc = carry
        query_block, back_block, lse_block, delta_block, seg_block = inputs
        scores = (
            jnp.einsum("khd,qhd->hkq", key_heads, query_block, preferred_element_type=jnp.float32)
            * score_scale
        )
        probs = jnp.where(mask_for(seg_block), jnp.exp(scores - lse_block.T[:, None, :]), 0.0)
        probs_low = probs.astype(jnp.bfloat16)
        value_acc = value_acc + jnp.einsum(
            "hkq,qhd->khd", probs_low, back_block, preferred_element_type=jnp.float32
        )
        dprobs = jnp.einsum(
            "khd,qhd->hkq", value_heads, back_block, preferred_element_type=jnp.float32
        )
        dscores = (probs * (dprobs - delta_block.T[:, None, :])).astype(jnp.bfloat16)
        key_acc = key_acc + jnp.einsum(
            "hkq,qhd->khd", dscores, query_block, preferred_element_type=jnp.float32
        )
        return ((key_acc, value_acc), None)

    start_acc = jnp.zeros((local_rows, HEADS, HEAD), jnp.float32)
    (key_acc, value_acc), unused = lax.scan(
        key_side,
        (start_acc, start_acc),
        (query_blocks, back_blocks, lse_blocks, delta_blocks, segment_blocks),
    )
    key_grad = (key_acc * score_scale).astype(jnp.bfloat16).reshape(local_rows, model_width)
    value_grad = value_acc.astype(jnp.bfloat16).reshape(local_rows, model_width)
    weight_term = lax.dot_general(
        attended, out_grad, (((0,), (0,)), ((), ())), preferred_element_type=jnp.float32
    )
    partial_sum = lax.psum_scatter(
        weight_term.astype(jnp.bfloat16), "seq", scatter_dimension=0, tiled=True
    )
    weight_grad = lax.psum_scatter(partial_sum, "dp", scatter_dimension=1, tiled=True).astype(
        jnp.float32
    )
    return (query_grad, key_grad, value_grad, weight_grad)


def solution(mesh):
    return jax.shard_map(
        local,
        mesh=mesh,
        in_specs=(
            P(("dp", "seq"), None),
            P(("dp", "seq"), None),
            P(("dp", "seq"), None),
            P(("dp", "seq"), None),
            P(),
            P("dp", None),
        ),
        out_specs=(
            P(("dp", "seq"), None),
            P(("dp", "seq"), None),
            P(("dp", "seq"), None),
            P("seq", "dp"),
        ),
        check_vma=False,
    )
```

profile of v0, /device:TPU:0, one launch (start us, length us, event | category | flops | bytes accessed | tf_op | source)
XLA Modules:
  0.0 515.4 jit_solution(4315347919527492731)
XLA Ops:
  10.9 59.8 %all-gather.5.cloned.1.call-done = bf16[2048,1152]{1,0:T(8,128)(2,1)} async-done(((bf16[128,1152]{1,0:T(8,128)(2,1)}), bf16[2048,1152]{1,0:T(8,128)(2,1)}) %all-gather.5.cloned.1.call-update) | async-done | bytes 4718608 | tf_op jit(solution)/shard_map/all_gather | solution.py:31
  70.7 17.4 %reshape.223 = bf16[4,512,16,72]{3,2,1,0:T(8,128)(2,1)} reshape(bf16[2048,1152]{1,0:T(8,128)(2,1)} %all-gather.5.cloned.1.call-done) | data formatting | bytes 9437184 | tf_op jit(solution)/shard_map/reshape | solution.py:38
  88.1 13.1 %copy.88 = bf16[4,512,16,72]{1,3,2,0:T(8,128)(2,1)} copy(bf16[4,512,16,72]{3,2,1,0:T(8,128)(2,1)} %reshape.223) | data formatting | bytes 9437184
  101.2 29.9 %while.48 = (s32[]{:T(128)}, f32[16,128]{1,0:T(8,128)S(1)}, f32[16,128]{1,0:T(8,128)S(1)}, s32[128]{0:T(128)S(1)}, s32[4,512]{1,0:T(4,128)S(1)}, /*index=5*/bf16...) while((s32[]{:T(128)}, f32[16,128]{1,0:T(8,128)S(1)}, ...), condition=%wide.region_5.6_spmd.clone, body=%wide.region_2.5_spmd.clone.sunk | while | flops 158410752 | bytes 10173048 | solution.py:64
  101.4 4.2 fusion.113
  108.8 4.2 fusion.113
  113.1 3.1 fusion.114
  116.4 4.2 fusion.113
  120.6 3.1 fusion.114
  123.8 4.2 fusion.113
  131.2 17.4 %reshape.224 = bf16[4,512,16,72]{3,2,1,0:T(8,128)(2,1)} reshape(bf16[2048,1152]{1,0:T(8,128)(2,1)} %all-gather.7.cloned.1.call-done) | data formatting | bytes 9437184 | tf_op jit(solution)/shard_map/reshape | solution.py:39
  148.6 13.1 %copy.89 = bf16[4,512,16,72]{1,3,2,0:T(8,128)(2,1)} copy(bf16[4,512,16,72]{3,2,1,0:T(8,128)(2,1)} %reshape.224) | data formatting | bytes 9437184
  161.7 17.2 %while.49 = (s32[]{:T(128)}, f32[128,16,72]{0,2,1:T(8,128)}, bf16[4,512,16,72]{1,3,2,0:T(8,128)(2,1)}, s32[128]{0:T(128)S(1)}, s32[4,512]{1,0:T(4,128)S(1)}, /*i...) while((s32[]{:T(128)}, f32[128,16,72]{0,2,1:T(8,128)}, ...), condition=%wide.region_7.8_spmd.clone, body=%wide.region_6.7_spmd.clone.sunk | while | flops 306544640 | bytes 3981434 | solution.py:83
  161.9 4.0 fusion.119
  166.1 4.2 fusion.119
  170.4 4.2 fusion.119
  174.7 4.2 fusion.119
  183.6 71.2 %reduce-scatter.9.cloned.1.call-done = bf16[72,1152]{1,0:T(8,128)(2,1)} async-done(((bf16[1152,1152]{1,0:T(8,128)(2,1)}), bf16[72,1152]{1,0:T(8,128)(2,1)}) %reduce-scatter.9.cloned.1.call-update) | async-done | bytes 165904
  265.5 37.4 %while.50 = (s32[]{:T(128)}, f32[128,16,72]{0,2,1:T(8,128)S(1)}, bf16[4,512,16,72]{1,3,2,0:T(8,128)(2,1)}, s32[128]{0:T(128)S(1)}, s32[4,512]{1,0:T(4,128)S(1)},...) while((s32[]{:T(128)}, f32[128,16,72]{0,2,1:T(8,128)S(1)}, ...), condition=%wide.region_10.11_spmd.clone, body=%wide.region_9.10_spmd.clone.sunk | while | flops 459636736 | bytes 13885610 | solution.py:118
  265.5 4.1 fusion.125
  269.7 5.0 fusion.126
  274.7 4.0 fusion.125
  278.9 5.0 fusion.126
  283.9 4.0 fusion.125
  288.1 5.5 %fusion.126 = f32[128,16,72]{0,2,1:T(8,128)S(1)} fusion(f32[16,512,128]{2,1,0:T(8,128)} %fusion.125, bf16[128,16,72]{0,2,1:T(8,128)(2,1)S(1)} %get-tuple-element.861, f32[16,128]{1,0:T(8,128)S(1)} %bitcast.250, f32[16,128]{1,0:T(8,128)S(1)} %copy-done.4, pred[128,512]{0,1:T(8,128)(4,1)S(1)} %broadcast_compare_fusion.10, ...), kind=kOutput, calls=%fused_computation.34.clone.1 | convolution fusion | flops 308576256 | bytes 8111616 | tf_op jit(solution)/shard_map/while/body/eval_jaxpr/hqk,khd->qhd/dot_general | solution.py:114
  293.6 4.0 fusion.125
  297.8 5.0 fusion.126
  303.8 10.1 %all-gather.9.cloned.1.call-done = bf16[2048,1152]{1,0:T(8,128)(2,1)} async-done(((bf16[128,1152]{1,0:T(8,128)(2,1)}), bf16[2048,1152]{1,0:T(8,128)(2,1)}) %all-gather.9.cloned.1.call-update) | async-done | bytes 4718608 | tf_op jit(solution)/shard_map/all_gather | solution.py:100
  313.9 17.4 %reshape.218 = bf16[4,512,16,72]{3,2,1,0:T(8,128)(2,1)} reshape(bf16[2048,1152]{1,0:T(8,128)(2,1)} %all-gather.9.cloned.1.call-done) | data formatting | bytes 9437184 | tf_op jit(solution)/shard_map/reshape | solution.py:124
  331.3 13.1 %copy.94 = bf16[4,512,16,72]{1,3,2,0:T(8,128)(2,1)} copy(bf16[4,512,16,72]{3,2,1,0:T(8,128)(2,1)} %reshape.218) | data formatting | bytes 9437184
  344.4 20.2 %all_gather.21 = f32[2048,16]{0,1:T(8,128)S(1)} all-gather(f32[128,16]{0,1:T(8,128)S(1)} %bitcast.251), channel_id=1, replica_groups=mesh['dp'=8,'seq'=16] {'seq'}, dimensions={0}, use_global_device_ids=true | all-gather | bytes 139264 | tf_op jit(solution)/shard_map/all_gather | solution.py:96
  364.7 22.4 %all_gather.23 = f32[2048,16]{0,1:T(8,128)S(1)} all-gather(f32[128,16]{0,1:T(8,128)S(1)} %get-tuple-element.939), channel_id=1, replica_groups=mesh['dp'=8,'seq'=16] {'seq'}, dimensions={0}, use_global_device_ids=true | all-gather | bytes 139264 | tf_op jit(solution)/shard_map/all_gather | solution.py:97
  388.8 22.9 %all-gather.11.cloned.1.call-done = bf16[2048,1152]{1,0:T(8,128)(2,1)} async-done(((bf16[128,1152]{1,0:T(8,128)(2,1)}), bf16[2048,1152]{1,0:T(8,128)(2,1)}) %all-gather.11.cloned.1.call-update) | async-done | bytes 4718608 | tf_op jit(solution)/shard_map/all_gather | solution.py:101
  411.6 17.4 %reshape.219 = bf16[4,512,16,72]{3,2,1,0:T(8,128)(2,1)} reshape(bf16[2048,1152]{1,0:T(8,128)(2,1)} %all-gather.11.cloned.1.call-done) | data formatting | bytes 9437184 | tf_op jit(solution)/shard_map/reshape | solution.py:125
  429.1 13.1 %copy.96 = bf16[4,512,16,72]{1,3,2,0:T(8,128)(2,1)} copy(bf16[4,512,16,72]{3,2,1,0:T(8,128)(2,1)} %reshape.219) | data formatting | bytes 9437184
  442.2 62.2 %while.51 = (s32[]{:T(128)}, f32[128,16,72]{0,2,1:T(8,128)}, f32[128,16,72]{0,2,1:T(8,128)}, bf16[4,512,16,72]{1,3,2,0:T(8,128)(2,1)}, s32[128]{0:T(128)S(1)}, /...) while((s32[]{:T(128)}, f32[128,16,72]{0,2,1:T(8,128)}, ...), condition=%wide.region_12.13_spmd.clone, body=%wide.region_11.12_spmd.clone.sunk | while | flops 615120896 | bytes 20816032 | solution.py:151
  442.2 4.0 fusion.134
  446.4 6.8 %fusion.135 = f32[128,16,72]{0,2,1:T(8,128)} fusion(f32[16,512,128]{2,1,0:T(8,128)} %fusion.134, bf16[128,16,72]{0,2,1:T(8,128)(2,1)S(1)} %get-tuple-element.900, f32[16,512]{1,0:T(8,128)S(1)} %bitcast.242, f32[16,512]{1,0:T(8,128)S(1)} %bitcast.240, pred[128,512]{0,1:T(8,128)(4,1)S(1)} %broadcast_compare_fusion.11, ...), kind=kOutput, calls=%fused_computation.61.clone.1 | convolution fusion | flops 308576256 | bytes 8160768 | tf_op jit(solution)/shard_map/while/body/eval_jaxpr/hkq,qhd->khd/dot_general | solution.py:145
  453.2 4.4 fusion.136
  457.6 4.0 fusion.134
  461.8 6.8 %fusion.135 = f32[128,16,72]{0,2,1:T(8,128)} fusion(f32[16,512,128]{2,1,0:T(8,128)} %fusion.134, bf16[128,16,72]{0,2,1:T(8,128)(2,1)S(1)} %get-tuple-element.900, f32[16,512]{1,0:T(8,128)S(1)} %bitcast.242, f32[16,512]{1,0:T(8,128)S(1)} %bitcast.240, pred[128,512]{0,1:T(8,128)(4,1)S(1)} %broadcast_compare_fusion.11, ...), kind=kOutput, calls=%fused_computation.61.clone.1 | convolution fusion | flops 308576256 | bytes 8160768 | tf_op jit(solution)/shard_map/while/body/eval_jaxpr/hkq,qhd->khd/dot_general | solution.py:145
  468.7 4.5 fusion.136
  473.2 4.0 fusion.134
  477.4 6.8 %fusion.135 = f32[128,16,72]{0,2,1:T(8,128)} fusion(f32[16,512,128]{2,1,0:T(8,128)} %fusion.134, bf16[128,16,72]{0,2,1:T(8,128)(2,1)S(1)} %get-tuple-element.900, f32[16,512]{1,0:T(8,128)S(1)} %bitcast.242, f32[16,512]{1,0:T(8,128)S(1)} %bitcast.240, pred[128,512]{0,1:T(8,128)(4,1)S(1)} %broadcast_compare_fusion.11, ...), kind=kOutput, calls=%fused_computation.61.clone.1 | convolution fusion | flops 308576256 | bytes 8160768 | tf_op jit(solution)/shard_map/while/body/eval_jaxpr/hkq,qhd->khd/dot_general | solution.py:145
  484.3 4.5 fusion.136
  488.8 4.0 fusion.134
  493.0 6.8 %fusion.135 = f32[128,16,72]{0,2,1:T(8,128)} fusion(f32[16,512,128]{2,1,0:T(8,128)} %fusion.134, bf16[128,16,72]{0,2,1:T(8,128)(2,1)S(1)} %get-tuple-element.900, f32[16,512]{1,0:T(8,128)S(1)} %bitcast.242, f32[16,512]{1,0:T(8,128)S(1)} %bitcast.240, pred[128,512]{0,1:T(8,128)(4,1)S(1)} %broadcast_compare_fusion.11, ...), kind=kOutput, calls=%fused_computation.61.clone.1 | convolution fusion | flops 308576256 | bytes 8160768 | tf_op jit(solution)/shard_map/while/body/eval_jaxpr/hkq,qhd->khd/dot_general | solution.py:145
  499.8 4.5 fusion.136
  (123 shorter events, 34.7 us)
Async XLA Ops:
  7.2 250.6 %copy-start = (bf16[1152,1152]{1,0:T(8,128)(2,1)S(1)}, bf16[1152,1152]{1,0:T(8,128)(2,1)}, u32[]{:S(2)}) copy-start(bf16[1152,1152]{1,0:T(8,128)(2,1)} %param.18) | copy-start | bytes 7962628
  7.2 63.5 %all-gather.5.cloned.1.call-start = ((), (), s32[]{:S(2)}) async-start(), calls=%async_computation.2 | async-start | bytes 5013504 | tf_op jit(solution)/shard_map/all_gather | solution.py:31
  7.9 123.3 %all-gather.7.cloned.1.call-start = ((), (), s32[]{:S(2)}) async-start(), calls=%async_computation.3 | async-start | bytes 5013504 | tf_op jit(solution)/shard_map/all_gather | solution.py:32
  8.7 246.1 %reduce-scatter.9.cloned.1.call-start = ((), (), s32[]{:S(2)}) async-start(), calls=%async_computation.7 | async-start | bytes 2820096
  161.7 18.9 %copy-start.2 = (bf16[128,1152]{1,0:T(8,128)(2,1)S(1)}, bf16[128,1152]{1,0:T(8,128)(2,1)}, u32[]{:S(2)}) copy-start(bf16[128,1152]{1,0:T(8,128)(2,1)} %param.17) | copy-start | bytes 884740
  178.9 0.6 copy-start.3
  183.0 130.9 %all-gather.9.cloned.1.call-start = ((), (), s32[]{:S(2)}) async-start(), calls=%async_computation.4 | async-start | bytes 5013504 | tf_op jit(solution)/shard_map/all_gather | solution.py:100
  183.6 203.7 %reduce-scatter.7.cloned.1.call-start = ((), (), s32[]{:S(2)}) async-start(), calls=%async_computation.6 | async-start | bytes 331776
  256.6 155.0 %all-gather.11.cloned.1.call-start = ((), (), s32[]{:S(2)}) async-start(), calls=%async_computation.5 | async-start | bytes 5013504 | tf_op jit(solution)/shard_map/all_gather | solution.py:101
  265.5 4.2 copy-start.4
  274.7 4.2 copy-start.4
  283.9 4.2 copy-start.4
  293.6 4.2 copy-start.4
  331.3 13.1 %copy-start.5 = (f32[16,128]{1,0:T(8,128)S(1)}, f32[16,128]{1,0:T(8,128)}, u32[]{:S(2)}) copy-start(f32[16,128]{1,0:T(8,128)} %get-tuple-element.941) | copy-start | bytes 24580
  504.4 4.2 copy-start.1
Sparse Core Ops, SparseCore 0:
  10.5 60.1 all-gather.4
  73.2 55.4 all-gather.6
  183.1 71.6 reduce-scatter.8
  257.4 56.4 all-gather.8
  316.8 35.0 reduce-scatter.6
  354.8 56.7 all-gather.10
where the time goes:
time: 520 us; the launch traced here: 515 us
  waiting for transfers between devices  166 us (32%)
  local copies, waits for them, and re-layouts  136 us (26%)
  matrix products  136 us (26%)
  blocking collectives  42.7 us (8%)
  other arithmetic  19.7 us (4%)
  between operations  14.3 us (3%)
    unnamed x8, waiting for transfers between devices  73.1 us
    unnamed x22, local copies, waits for them, and re-layouts  61.9 us
    all_gather x1, waiting for transfers between devices, local(): lax.all_gather(keys, 'seq', axis=0, tiled=True)  59.8 us
    dot_general x8, matrix products, query_scores(): jnp.einsum('qhd,khd->hqk', query_heads, key_block, preferred_element_type...  33 us
    dot_general x4, matrix products, key_side(): jnp.einsum('hkq,qhd->khd', dscores, query_block, preferred_element_type=j...  27.2 us
    all_gather x1, waiting for transfers between devices, local(): lax.all_gather(out_back, 'seq', axis=0, tiled=True)  22.9 us
    all_gather x1, blocking collectives, local(): lax.all_gather(delta_rows, 'seq', axis=0, tiled=True)  22.4 us
    dot_general x4, matrix products, query_side(): jnp.einsum('hqk,khd->qhd', dscores, key_block, preferred_element_type=jnp...  20.5 us
  transfers between devices with their start and end apart: 6, of which 4 were waited for; matrix products, arithmetic and copies ran while one was open for 28% of the time, Pallas kernels for 0%

commit v1 on v0

v1 whole, which is shorter than its diff:
```python
import functools

import jax
import jax.numpy as jnp
from jax import lax
from jax.experimental import pallas as pl
from jax.experimental.pallas import tpu as pltpu
from jax.sharding import PartitionSpec as P

HEADS = 16
HEAD = 72
IMAGES = 8
UNIT = 64
ROWS = 128
BLOCK = 256
BLOCKS = 8
PAD = 80
SCALE = HEAD**-0.5
LOG2E = 1.4426950408889634
FAR = 16384.0
F32 = jnp.float32
BF16 = jnp.bfloat16
VMEM_LIMIT = 48 * 1024 * 1024

NN = (((1,), (0,)), ((), ()))
NT = (((1,), (1,)), ((), ()))


def dot(a, b, dims):
    return lax.dot_general(a, b, dims, preferred_element_type=F32)


def pack_body(q_ref, k_ref, v_ref, g_ref, w_ref, out_ref):
    back = dot(w_ref[...], g_ref[...], NT).astype(BF16).astype(F32)
    parts = [ref[...].astype(F32).T for ref in (q_ref, k_ref, v_ref)] + [back]
    for h in range(HEADS):
        rows = slice(h * HEAD, (h + 1) * HEAD)
        out_ref[h] = jnp.concatenate([part[rows] for part in parts], axis=0).astype(BF16)


def pack(queries, keys, values, out_grad, out_weight):
    return pl.pallas_call(
        pack_body,
        out_shape=jax.ShapeDtypeStruct((HEADS, 4 * HEAD, ROWS), BF16),
        compiler_params=pltpu.CompilerParams(vmem_limit_bytes=VMEM_LIMIT),
        name="pack",
    )(queries, keys, values, out_grad, out_weight)


def attend_body(
    ext_ref, r_ref, g_ref, att_ref, q_s, b_s, k_s, v_s, kn_s, vn_s, e_s, dq_s, dk_s, dv_s
):
    ends = []
    total = jnp.int32(0)
    for i in range(IMAGES):
        total = total + ext_ref[0, i] * UNIT
        ends.append(total)

    lane = lax.broadcasted_iota(jnp.int32, (IMAGES, ROWS), 1)
    row = lax.broadcasted_iota(jnp.int32, (IMAGES, ROWS), 0)
    nothing = jnp.zeros((128 - PAD, ROWS), F32)
    ones_row = jnp.where(row == 0, 1.0, 0.0)
    zeros_rows = jnp.zeros((IMAGES, ROWS), F32)
    for s in range(HEADS):
        b, half = s // 2, s % 2
        lanes = slice(half * ROWS, (half + 1) * ROWS)
        x = r_ref[s].astype(F32)
        q, k, v, back = (x[j * HEAD : (j + 1) * HEAD] for j in range(4))
        segment = jnp.zeros((IMAGES, ROWS), jnp.int32)
        for end in ends:
            segment = segment + (lane + s * ROWS >= end).astype(jnp.int32)
        here = (segment == row).astype(F32)
        q_s[b, :, lanes] = jnp.concatenate([q, here * -FAR, nothing], axis=0).astype(BF16)
        b_s[b, :, lanes] = jnp.concatenate([back, zeros_rows], axis=0).astype(BF16)
        k_aug = jnp.concatenate([k, 1.0 - here, nothing], axis=0)
        v_aug = jnp.concatenate([v, zeros_rows, nothing], axis=0)
        k_s[b, :, lanes] = k_aug[:PAD].astype(BF16)
        v_s[b, :, lanes] = jnp.concatenate([v, ones_row], axis=0).astype(BF16)
        kn_s[b, lanes, :] = k_aug.T.astype(BF16)
        vn_s[b, lanes, :] = v_aug.T.astype(BF16)

    dk_s[...] = jnp.zeros_like(dk_s)
    dv_s[...] = jnp.zeros_like(dv_s)

    def query_block(qb, carry):
        first = qb * BLOCK
        last = first + BLOCK - 1
        start, stop = jnp.int32(0), jnp.int32(BLOCKS * BLOCK)
        for end in ends:
            start = jnp.maximum(start, jnp.where(end <= first, end, 0))
            stop = jnp.minimum(stop, jnp.where(end > last, end, BLOCKS * BLOCK))
        lo = start // BLOCK
        hi = (stop + BLOCK - 1) // BLOCK
        q = q_s[qb]

        def scores_of(c, top):
            scores = dot(kn_s[c], q, NN)
            e_s[c] = scores
            return jnp.maximum(top, jnp.max(scores.reshape(BLOCK // 8, 8, BLOCK), axis=0))

        top = lax.fori_loop(lo, hi, scores_of, jnp.full((8, BLOCK), -3e38, F32))
        top = jnp.max(top, axis=0, keepdims=True)

        def attend(c, acc):
            e = jnp.exp2((e_s[c] - top) * (SCALE * LOG2E))
            e_s[c] = e
            return acc + dot(v_s[c], e.astype(BF16), NN)

        acc = lax.fori_loop(lo, hi, attend, jnp.zeros((PAD, BLOCK), F32))
        inverse = 1.0 / acc[HEAD : HEAD + 1]
        attended = (acc[:HEAD] * inverse).astype(BF16)
        att_ref[2 * qb] = attended[:, :ROWS]
        att_ref[2 * qb + 1] = attended[:, ROWS:]
        back = b_s[qb].astype(F32)
        delta = jnp.sum(back[:HEAD] * attended.astype(F32), axis=0, keepdims=True) * inverse
        back = (back * inverse).astype(BF16)
        back_wide = jnp.concatenate([back, jnp.zeros((128 - PAD, BLOCK), BF16)], axis=0)

        def grads(c, dq):
            e = e_s[c]
            ds = (e * (dot(vn_s[c], back_wide, NN) - delta)).astype(BF16)
            dv_s[c] += dot(back, e.astype(BF16), NT)
            dk_s[c] += dot(q[:PAD], ds, NT)
            return dq + dot(k_s[c], ds, NN)

        dq_s[qb] = lax.fori_loop(lo, hi, grads, jnp.zeros((PAD, BLOCK), F32))
        return carry

    lax.fori_loop(0, BLOCKS, query_block, 0)

    for s in range(HEADS):
        b, half = s // 2, s % 2
        lanes = slice(half * ROWS, (half + 1) * ROWS)
        g_ref[s] = jnp.concatenate(
            [
                dq_s[b, :HEAD, lanes] * SCALE,
                dk_s[b, :HEAD, lanes] * SCALE,
                dv_s[b, :HEAD, lanes],
            ],
            axis=0,
        ).astype(BF16)


def attend(extents, received):
    return pl.pallas_call(
        attend_body,
        out_shape=(
            jax.ShapeDtypeStruct((HEADS, 3 * HEAD, ROWS), BF16),
            jax.ShapeDtypeStruct((HEADS, HEAD, ROWS), BF16),
        ),
        in_specs=[
            pl.BlockSpec(memory_space=pltpu.SMEM),
            pl.BlockSpec(memory_space=pltpu.VMEM),
        ],
        scratch_shapes=[
            pltpu.VMEM((BLOCKS, 128, BLOCK), BF16),
            pltpu.VMEM((BLOCKS, PAD, BLOCK), BF16),
            pltpu.VMEM((BLOCKS, PAD, BLOCK), BF16),
            pltpu.VMEM((BLOCKS, PAD, BLOCK), BF16),
            pltpu.VMEM((BLOCKS, BLOCK, 128), BF16),
            pltpu.VMEM((BLOCKS, BLOCK, 128), BF16),
            pltpu.VMEM((BLOCKS, BLOCK, BLOCK), F32),
            pltpu.VMEM((BLOCKS, PAD, BLOCK), F32),
            pltpu.VMEM((BLOCKS, PAD, BLOCK), F32),
            pltpu.VMEM((BLOCKS, PAD, BLOCK), F32),
        ],
        compiler_params=pltpu.CompilerParams(vmem_limit_bytes=VMEM_LIMIT),
        name="attend",
    )(extents, received)


def unpack_body(y_ref, dq_ref, dk_ref, dv_ref):
    for j, ref in enumerate((dq_ref, dk_ref, dv_ref)):
        rows = [y_ref[h].astype(F32)[j * HEAD : (j + 1) * HEAD] for h in range(HEADS)]
        ref[...] = jnp.concatenate(rows, axis=0).T.astype(BF16)


def unpack(returned):
    shape = jax.ShapeDtypeStruct((ROWS, HEADS * HEAD), BF16)
    return pl.pallas_call(
        unpack_body,
        out_shape=(shape, shape, shape),
        compiler_params=pltpu.CompilerParams(vmem_limit_bytes=VMEM_LIMIT),
        name="unpack",
    )(returned)


def local(queries, keys, values, out_grad, out_weight, extents):
    same_core = [[core + 2 * chip for chip in range(8)] for core in range(2)]
    swap_core = [(i, i ^ 1) for i in range(HEADS)]
    core = lax.axis_index("seq") % 2

    sent = pack(queries, keys, values, out_grad, out_weight)
    received = lax.all_to_all(sent, "seq", 0, 0, tiled=True)
    copies = jnp.broadcast_to(out_grad[None], (8,) + out_grad.shape)
    grad_all = lax.all_to_all(copies, "seq", 0, 0, tiled=True, axis_index_groups=same_core)
    grads, attended = attend(extents, received)
    returned = lax.all_to_all(grads, "seq", 0, 0, tiled=True)
    query_grad, key_grad, value_grad = unpack(returned)

    by_core = attended.reshape(8, 2, HEAD, ROWS)
    mine = lax.dynamic_index_in_dim(by_core, core, 1, keepdims=False)
    other = lax.dynamic_index_in_dim(by_core, 1 - core, 1, keepdims=False)
    other = lax.ppermute(other, "seq", swap_core)

    def term(rows):
        return jnp.einsum("shr,srd->hd", rows, grad_all, preferred_element_type=F32)

    passed = lax.ppermute(term(other).astype(BF16), "seq", swap_core)
    summed = (term(mine) + passed.astype(F32)).astype(BF16)
    tiles = summed.reshape(HEAD, 8, 144).transpose(1, 0, 2)
    tiles = lax.all_to_all(tiles, "dp", 0, 0, tiled=True)
    weight_grad = jnp.sum(tiles.astype(F32), axis=0)
    return query_grad, key_grad, value_grad, weight_grad


def solution(mesh):
    tokens = P(("dp", "seq"), None)
    return jax.shard_map(
        local,
        mesh=mesh,
        in_specs=(tokens, tokens, tokens, tokens, P(), P("dp", None)),
        out_specs=(tokens, tokens, tokens, P("seq", "dp")),
        check_vma=False,
    )
```

time: 520 us -> 105 us (0.20)
  waiting for transfers between devices: 166 us -> 24 us
  matrix products: 136 us -> 4.41 us
  local copies, waits for them, and re-layouts: 136 us -> 8.46 us
  Pallas kernels: 0 us -> 25.9 us
  other arithmetic: 19.7 us -> 0.72 us
  blocking collectives: 42.7 us -> 27.2 us
  between operations: 14.3 us -> 0.76 us
  starting transfers between devices: 0.42 us -> 13.1 us
    dot_general x30 -> x2, matrix products: 136 us -> 4.41 us  [term(): return jnp.einsum('shr,srd->hd', rows, grad_all, preferred_element_type=F32)]
    all_gather x4 -> x0, waiting for transfers between devices: 92.7 us -> none  [the longest x1 59.8 us: local(): lax.all_gather(keys, 'seq', axis=0, tiled=True)]
    unnamed x8 -> x0, waiting for transfers between devices: 73.1 us -> none
    reshape x8 -> x2, local copies, waits for them, and re-layouts: 70.8 us -> 1.15 us  [local(): tiles = summed.reshape(HEAD, 8, 144).transpose(1, 0, 2)]
    unnamed x22 -> x12, local copies, waits for them, and re-layouts: 61.9 us -> 5.59 us
    all_gather x2 -> x0, blocking collectives: 42.7 us -> none  [the longest x1 22.4 us: local(): lax.all_gather(delta_rows, 'seq', axis=0, tiled=True)]
    all_to_all x0 -> x1, blocking collectives: none -> 27.2 us  [local(): received = lax.all_to_all(sent, 'seq', 0, 0, tiled=True)]
    pallas_call x0 -> x3, Pallas kernels: none -> 25.9 us  [the longest x1 23.9 us: attend(): pl.pallas_call(attend_body, out_shape=(jax.ShapeDtypeStruct((HEADS, 3 * H...]
  transfers between devices with their start and end apart: 6 -> 5, of which waited for: 4 -> 3; matrix products, arithmetic and copies ran while one was open for 28% -> 5% of each run, Pallas kernels for 0% -> 24%
where the time goes in v1:
time: 105 us
  blocking collectives  27.2 us (26%)
  Pallas kernels  25.9 us (25%)
  waiting for transfers between devices  24 us (23%)
  starting transfers between devices  13.1 us (12%)
  local copies, waits for them, and re-layouts  8.46 us (8%)
  matrix products  4.41 us (4%)
    all_to_all x1, blocking collectives, local(): received = lax.all_to_all(sent, 'seq', 0, 0, tiled=True)  27.2 us
    pallas_call x1, Pallas kernels, attend(): pl.pallas_call(attend_body, out_shape=(jax.ShapeDtypeStruct((HEADS, 3 * H...  23.9 us
    all_to_all x1, waiting for transfers between devices, local(): returned = lax.all_to_all(grads, 'seq', 0, 0, tiled=True)  10.2 us
    all_to_all x1, waiting for transfers between devices, local(): lax.all_to_all(copies, 'seq', 0, 0, tiled=True, axis_index_groups=same_core)  7.52 us
    all_to_all x1, waiting for transfers between devices, local(): tiles = lax.all_to_all(tiles, 'dp', 0, 0, tiled=True)  6.28 us
    unnamed x12, local copies, waits for them, and re-layouts  5.59 us
    all_to_all x1, starting transfers between devices, local(): tiles = lax.all_to_all(tiles, 'dp', 0, 0, tiled=True)  4.56 us
    all_to_all x1, starting transfers between devices, local(): lax.all_to_all(copies, 'seq', 0, 0, tiled=True, axis_index_groups=same_core)  4.5 us
  transfers between devices with their start and end apart: 5, of which 3 were waited for; matrix products, arithmetic and copies ran while one was open for 5% of the time, Pallas kernels for 24%

profile of v1, /device:TPU:0, one launch (start us, length us, event | category | flops | bytes accessed | tf_op | source)
XLA Modules:
  0.0 104.5 jit_solution(2731540299107084925)
XLA Ops:
  0.6 0.0 copy-start
  0.6 1.7 %copy-done = bf16[1152,1152]{1,0:T(8,128)(2,1)S(1)} copy-done((bf16[1152,1152]{1,0:T(8,128)(2,1)S(1)}, bf16[1152,1152]{1,0:T(8,128)(2,1)}, u32[]{:S(2)}) %copy-start) | copy-done | bytes 2654232
  2.4 0.0 copy-start.1
  2.4 1.0 copy-done.1
  3.3 0.0 copy-start.2
  3.3 1.0 copy-done.2
  4.3 0.0 copy-start.3
  4.3 1.0 copy-done.3
  5.3 0.0 copy-start.4
  5.3 1.0 copy-done.4
  6.2 0.8 pack.1
  7.1 27.2 %all_to_all.20.r_ref = bf16[16,288,128]{2,1,0:T(8,128)(2,1)S(1)} all-to-all(bf16[16,288,128]{2,1,0:T(8,128)(2,1)S(1)} %pack.1), channel_id=1, replica_groups=mesh['dp'=8,'seq'=16] {'seq'}, dimensions={0} | all-to-all | bytes 2359296 | tf_op jit(solution)/shard_map/all_to_all | solution.py:194
  34.3 1.7 %broadcast_in_dim.2 = bf16[8,128,1152]{2,1,0:T(8,128)(2,1)} broadcast(bf16[128,1152]{1,0:T(8,128)(2,1)S(1)} %copy-done.1), dimensions={1,2} | broadcast | bytes 2654208 | tf_op jit(solution)/shard_map/broadcast_in_dim | solution.py:195
  36.0 0.0 copy-start.5
  36.0 4.5 %all-to-all-start.2 = ((bf16[8,128,1152]{2,1,0:T(8,128)(2,1)}), bf16[8,128,1152]{2,1,0:T(8,128)(2,1)}, u32[]{:S(2)}, u32[]{:S(2)}) async-start(bf16[8,128,1152]{2,1,0:T(8,128)(2,1)} %broadcast_in_dim.2), calls=%async_computation.2 | async-start | bytes 4718592 | tf_op jit(solution)/shard_map/all_to_all | solution.py:196
  40.5 0.0 copy-done.5
  40.5 23.9 %attend.1 = (bf16[16,216,128]{2,1,0:T(8,128)(2,1)}, bf16[16,72,128]{2,1,0:T(8,128)(2,1)S(1)}) custom-call(s32[1,8]{1,0:T(1,128)S(1)} %copy-done.5, bf16[16,288,128]{2,1,0:T(8,128)(2,1)S(1)} %all_to_all.20.r_ref), custom_call_target="tpu_custom_call" | custom-call | tf_op jit(solution)/shard_map/attend/pallas_call | solution.py:145
  64.5 0.1 collective-permute-start
  64.6 7.5 %all-to-all-done.2 = bf16[8,128,1152]{2,1,0:T(8,128)(2,1)} async-done(((bf16[8,128,1152]{2,1,0:T(8,128)(2,1)}), bf16[8,128,1152]{2,1,0:T(8,128)(2,1)}, u32[]{:S(2)}, u32[]{:S(2)}) %all-to-all-start.2) | async-done | bytes 2359328 | tf_op jit(solution)/shard_map/all_to_all | solution.py:196
  72.1 3.6 %all-to-all-start.1 = ((bf16[16,216,128]{2,1,0:T(8,128)(2,1)}), bf16[16,216,128]{2,1,0:T(8,128)(2,1)S(1)}, u32[]{:S(2)}, u32[]{:S(2)}) async-start(bf16[16,216,128]{2,1,0:T(8,128)(2,1)} %get-tuple-element.9), calls=%async_computation.1 | async-start | bytes 1769472 | tf_op jit(solution)/shard_map/all_to_all | solution.py:198
  75.8 0.0 collective-permute-done
  75.8 2.2 %fusion = bf16[72,1152]{1,0:T(8,128)(2,1)S(1)} fusion(bf16[8,72,128]{2,1,0:T(8,128)(2,1)S(1)} %collective-permute-done, bf16[8,128,1152]{2,1,0:T(8,128)(2,1)} %all-to-all-done.2), kind=kOutput, calls=%fused_computation.2 | convolution fusion | flops 169952256 | bytes 2672640 | tf_op jit(solution)/shard_map/shr,srd->hd/dot_general | solution.py:207
  78.0 0.4 collective-permute-start.1
  78.3 2.2 %convolution_bitcast_fusion.1 = f32[72,1152]{1,0:T(8,128)S(1)} fusion(bf16[8,128,1152]{2,1,0:T(8,128)(2,1)} %all-to-all-done.2, bf16[8,2,72,128]{3,2,1,0:T(8,128)(2,1)S(1)} %bitcast.19, s32[]{:T(128)S(6)} %select_n.15), kind=kOutput, calls=%fused_computation.1 | convolution fusion | flops 169869312 | bytes 2838532 | tf_op jit(solution)/shard_map/shr,srd->hd/dot_general | solution.py:207
  80.6 0.0 collective-permute-done.1
  80.6 0.4 reshape.16
  81.0 0.8 copy.12
  81.8 10.2 %all-to-all-done.1.y_ref = bf16[16,216,128]{2,1,0:T(8,128)(2,1)S(1)} async-done(((bf16[16,216,128]{2,1,0:T(8,128)(2,1)}), bf16[16,216,128]{2,1,0:T(8,128)(2,1)S(1)}, u32[]{:S(2)}, u32[]{:S(2)}) %all-to-all-start.1) | async-done | bytes 884768 | tf_op jit(solution)/shard_map/all_to_all | solution.py:198
  91.9 4.6 %all-to-all-start.3 = ((bf16[8,72,144]{2,1,0:T(8,128)(2,1)}), bf16[8,72,144]{2,1,0:T(8,128)(2,1)S(1)}, u32[]{:S(2)}, u32[]{:S(2)}) async-start(bf16[8,72,144]{2,1,0:T(8,128)(2,1)} %bitcast.17), calls=%async_computation.3 | async-start | bytes 589824 | tf_op jit(solution)/shard_map/all_to_all | solution.py:212
  96.5 1.1 %unpack.1 = (bf16[128,1152]{1,0:T(8,128)(2,1)}, bf16[128,1152]{1,0:T(8,128)(2,1)}, bf16[128,1152]{1,0:T(8,128)(2,1)}) custom-call(bf16[16,216,128]{2,1,0:T(8,128)(2,1)S(1)} %all-to-all-done.1.y_ref), custom_call_target="tpu_custom_call" | custom-call | tf_op jit(solution)/shard_map/unpack/pallas_call | solution.py:180
  97.6 6.3 %all-to-all-done.3 = bf16[8,72,144]{2,1,0:T(8,128)(2,1)S(1)} async-done(((bf16[8,72,144]{2,1,0:T(8,128)(2,1)}), bf16[8,72,144]{2,1,0:T(8,128)(2,1)S(1)}, u32[]{:S(2)}, u32[]{:S(2)}) %all-to-all-start.3) | async-done | bytes 165920 | tf_op jit(solution)/shard_map/all_to_all | solution.py:212
  103.9 0.7 convert_reduce_fusion
  (2 shorter events, 0.0 us)
Async XLA Ops:
  0.6 1.8 %copy-start = (bf16[1152,1152]{1,0:T(8,128)(2,1)S(1)}, bf16[1152,1152]{1,0:T(8,128)(2,1)}, u32[]{:S(2)}) copy-start(bf16[1152,1152]{1,0:T(8,128)(2,1)} %w_ref.1) | copy-start | bytes 7962628
  2.4 1.0 copy-start.1
  3.3 1.0 copy-start.2
  4.3 1.0 copy-start.3
  5.3 1.0 copy-start.4
  36.0 4.5 %copy-start.5 = (s32[1,8]{1,0:T(1,128)S(1)}, s32[1,8]{1,0:T(1,128)}, u32[]{:S(2)}) copy-start(s32[1,8]{1,0:T(1,128)} %ext_ref.1) | copy-start | bytes 100
  36.0 36.1 %all-to-all-start.2 = ((bf16[8,128,1152]{2,1,0:T(8,128)(2,1)}), bf16[8,128,1152]{2,1,0:T(8,128)(2,1)}, u32[]{:S(2)}, u32[]{:S(2)}) async-start(bf16[8,128,1152]{2,1,0:T(8,128)(2,1)} %broadcast_in_dim.2), calls=%async_computation.2 | async-start | bytes 4718592 | tf_op jit(solution)/shard_map/all_to_all | solution.py:196
  64.5 11.3 %collective-permute-start = (bf16[8,72,128]{2,1,0:T(8,128)(2,1)S(1)}, bf16[8,72,128]{2,1,0:T(8,128)(2,1)S(1)}, u32[]{:S(2)}, u32[]{:S(2)}) collective-permute-start(bf16[8,72,128]{2,1,0:T(8,128)(2,1)S(1)} %dynamic-slice_bitcast_fusion), channel_id=1, source_target_pairs={{0,1},{1,0},{2,3},{3,2},{4,5},{5,4},{6,7},{7,6},{8,9},{9,8},{10,11... | collective-permute-start | bytes 442376 | tf_op jit(solution)/shard_map/ppermute | solution.py:204
  72.1 19.8 %all-to-all-start.1 = ((bf16[16,216,128]{2,1,0:T(8,128)(2,1)}), bf16[16,216,128]{2,1,0:T(8,128)(2,1)S(1)}, u32[]{:S(2)}, u32[]{:S(2)}) async-start(bf16[16,216,128]{2,1,0:T(8,128)(2,1)} %get-tuple-element.9), calls=%async_computation.1 | async-start | bytes 1769472 | tf_op jit(solution)/shard_map/all_to_all | solution.py:198
  78.0 2.6 %collective-permute-start.1 = (bf16[72,1152]{1,0:T(8,128)(2,1)S(1)}, bf16[72,1152]{1,0:T(8,128)(2,1)S(1)}, u32[]{:S(2)}, u32[]{:S(2)}) collective-permute-start(bf16[72,1152]{1,0:T(8,128)(2,1)S(1)} %fusion), channel_id=1, source_target_pairs={{0,1},{1,0},{2,3},{3,2},{4,5},{5,4},{6,7},{7,6},{8,9},{9,8},{10,11... | collective-permute-start | bytes 497672 | tf_op jit(solution)/shard_map/ppermute | solution.py:209
  91.9 11.9 %all-to-all-start.3 = ((bf16[8,72,144]{2,1,0:T(8,128)(2,1)}), bf16[8,72,144]{2,1,0:T(8,128)(2,1)S(1)}, u32[]{:S(2)}, u32[]{:S(2)}) async-start(bf16[8,72,144]{2,1,0:T(8,128)(2,1)} %bitcast.17), calls=%async_computation.3 | async-start | bytes 589824 | tf_op jit(solution)/shard_map/all_to_all | solution.py:212

commit v2 on v1

v2 whole, which is shorter than its diff:
```python
import functools

import jax
import jax.numpy as jnp
from jax import lax
from jax.experimental import pallas as pl
from jax.experimental.pallas import tpu as pltpu
from jax.sharding import PartitionSpec as P

HEADS = 16
HEAD = 72
IMAGES = 8
UNIT = 64
ROWS = 128
BLOCK = 256
BLOCKS = 8
PAIRS = BLOCKS * BLOCKS + 8
PAD = 80
SCALE = HEAD**-0.5
LOG2E = 1.4426950408889634
FAR = 16384.0
F32 = jnp.float32
BF16 = jnp.bfloat16
VMEM_LIMIT = 48 << 20
VMEM_MOST = (64 << 20) - (128 << 10)

NN = (((1,), (0,)), ((), ()))
NT = (((1,), (1,)), ((), ()))


def dot(a, b, dims):
    return lax.dot_general(a, b, dims, preferred_element_type=F32)


def pack_body(q_hbm, k_hbm, v_hbm, g_hbm, w_hbm, out_ref, q_ref, k_ref, v_ref, g_ref, w_ref, sems):
    copies = [
        pltpu.make_async_copy(source, target, sems.at[i])
        for i, (source, target) in enumerate(
            [(q_hbm, q_ref), (k_hbm, k_ref), (v_hbm, v_ref), (g_hbm, g_ref), (w_hbm, w_ref)]
        )
    ]
    for copy in copies:
        copy.start()
    parts = []
    for i, ref in enumerate((q_ref, k_ref, v_ref)):
        copies[i].wait()
        parts.append(ref[...].astype(F32).T)
    copies[3].wait()
    copies[4].wait()
    parts.append(dot(w_ref[...], g_ref[...], NT).astype(BF16).astype(F32))
    for h in range(HEADS):
        rows = slice(h * HEAD, (h + 1) * HEAD)
        out_ref[h] = jnp.concatenate([part[rows] for part in parts], axis=0).astype(BF16)


def pack(queries, keys, values, out_grad, out_weight):
    width = HEADS * HEAD
    return pl.pallas_call(
        pack_body,
        out_shape=jax.ShapeDtypeStruct((HEADS, 4 * HEAD, ROWS), BF16),
        in_specs=[pl.BlockSpec(memory_space=pltpu.HBM)] * 5,
        out_specs=pl.BlockSpec(memory_space=pltpu.VMEM),
        scratch_shapes=[pltpu.VMEM((ROWS, width), BF16)] * 4
        + [pltpu.VMEM((width, width), BF16), pltpu.SemaphoreType.DMA((5,))],
        compiler_params=pltpu.CompilerParams(vmem_limit_bytes=VMEM_MOST),
        cost_estimate=pl.CostEstimate(flops=10**10, bytes_accessed=0, transcendentals=0),
        name="pack",
    )(queries, keys, values, out_grad, out_weight)


def kept(total, later):
    return jnp.where(later > 0, total, 0.0)


def attend_body(
    me_ref, ext_ref, r_ref, g_ref, att_ref, q_s, b_s, k_s, v_s, kn_s, vn_s, e_s, acc_s, dq_s, dk_s, dv_s,
    top_s, pair_top_s, delta_s, inverse_s, qb_s, kb_s, later_q_s, later_k_s
):
    ends = []
    total = jnp.int32(0)
    for i in range(IMAGES):
        total = total + ext_ref[0, i] * UNIT
        ends.append(total)

    lane = lax.broadcasted_iota(jnp.int32, (IMAGES, ROWS), 1)
    row = lax.broadcasted_iota(jnp.int32, (IMAGES, ROWS), 0)
    nothing = jnp.zeros((128 - PAD, ROWS), F32)
    ones_row = jnp.where(row == 0, 1.0, 0.0)
    zeros_rows = jnp.zeros((IMAGES, ROWS), F32)
    for s in range(HEADS):
        b, half = s // 2, s % 2
        lanes = slice(half * ROWS, (half + 1) * ROWS)
        x = r_ref[s].astype(F32)
        q, k, v, back = (x[j * HEAD : (j + 1) * HEAD] for j in range(4))
        segment = jnp.zeros((IMAGES, ROWS), jnp.int32)
        for end in ends:
            segment = segment + (lane + s * ROWS >= end).astype(jnp.int32)
        here = (segment == row).astype(F32)
        q_s[b, :, lanes] = jnp.concatenate([q, here * -FAR, nothing], axis=0).astype(BF16)
        b_s[b, :, lanes] = jnp.concatenate([back, zeros_rows], axis=0).astype(BF16)
        k_aug = jnp.concatenate([k, 1.0 - here, nothing], axis=0)
        v_aug = jnp.concatenate([v, zeros_rows, nothing], axis=0)
        k_s[b, :, lanes] = k_aug[:PAD].astype(BF16)
        v_s[b, :, lanes] = jnp.concatenate([v, ones_row], axis=0).astype(BF16)
        kn_s[b, lanes, :] = k_aug.T.astype(BF16)
        vn_s[b, lanes, :] = v_aug.T.astype(BF16)

    top_s[...] = jnp.full(top_s.shape, -3e38, F32)

    count = jnp.int32(0)
    reached = jnp.int32(0)
    for qb in range(BLOCKS):
        first, last = qb * BLOCK, qb * BLOCK + BLOCK - 1
        start, stop = jnp.int32(0), jnp.int32(BLOCKS * BLOCK)
        for end in ends:
            start = jnp.maximum(start, jnp.where(end <= first, end, 0))
            stop = jnp.minimum(stop, jnp.where(end > last, end, BLOCKS * BLOCK))
        lo = start // BLOCK
        size = (stop + BLOCK - 1) // BLOCK - lo

        def add_pair(i, carry, qb=qb, lo=lo, base=count, reached=reached):
            qb_s[base + i] = qb
            kb_s[base + i] = lo + i
            later_q_s[base + i] = i
            later_k_s[base + i] = (lo + i < reached).astype(jnp.int32)
            return carry

        lax.fori_loop(0, size, add_pair, 0)
        count = count + size
        reached = lo + size
    for u in range(8):
        qb_s[count + u] = BLOCKS
        kb_s[count + u] = BLOCKS
        later_q_s[count + u] = 0
        later_k_s[count + u] = 0

    def forward(i, carry):
        ats = [8 * i + u for u in range(8)]
        qbs = [qb_s[at] for at in ats]
        kbs = [kb_s[at] for at in ats]
        tops = []
        for at, qb, kb in zip(ats, qbs, kbs):
            scores = dot(kn_s[kb], q_s[qb], NN)
            e_s[at] = scores
            top = jnp.max(scores.reshape(BLOCK // 8, 8, BLOCK), axis=0)
            tops.append(jnp.max(top, axis=0, keepdims=True))
        terms = []
        for at, kb, top in zip(ats, kbs, tops):
            e = jnp.exp2((e_s[at] - top) * (SCALE * LOG2E))
            e_s[at] = e
            pair_top_s[at] = top
            terms.append(dot(v_s[kb], e.astype(BF16), NN))
        for at, qb, top, term in zip(ats, qbs, tops, terms):
            before = top_s[qb]
            after = jnp.maximum(before, top)
            top_s[qb] = after
            acc_s[qb] = kept(acc_s[qb], later_q_s[at]) * jnp.exp2((before - after) * (SCALE * LOG2E)) + term * jnp.exp2(
                (top - after) * (SCALE * LOG2E)
            )
        return carry

    lax.fori_loop(0, (count + 8 - 1) // 8 if True else 0, forward, 0)

    for qb in range(BLOCKS):
        acc = acc_s[qb]
        inverse = 1.0 / acc[HEAD : HEAD + 1]
        attended = (acc[:HEAD] * inverse).astype(BF16)
        for half in range(2):
            apart = (2 * qb + half) ^ me_ref[0]
            place = (apart & 3) + ((apart >> 3) << 2) + ((apart & 4) << 1)
            att_ref[place] = attended[:, half * ROWS : (half + 1) * ROWS]
        back = b_s[qb].astype(F32)
        delta_s[qb] = jnp.sum(back[:HEAD] * attended.astype(F32), axis=0, keepdims=True)
        inverse_s[qb] = inverse

    def backward(i, carry):
        ats = [8 * i + u for u in range(8)]
        qbs = [qb_s[at] for at in ats]
        kbs = [kb_s[at] for at in ats]
        backs, dss = [], []
        for at, qb, kb in zip(ats, qbs, kbs):
            factor = jnp.exp2((pair_top_s[at] - top_s[qb]) * (SCALE * LOG2E)) * inverse_s[qb]
            back = (b_s[qb].astype(F32) * factor).astype(BF16)
            back_wide = jnp.concatenate([back, jnp.zeros((128 - PAD, BLOCK), BF16)], axis=0)
            backs.append(back)
            dss.append((e_s[at] * (dot(vn_s[kb], back_wide, NN) - delta_s[qb] * factor)).astype(BF16))
        dvs, dks, dqs = [], [], []
        for at, qb, kb, back, ds in zip(ats, qbs, kbs, backs, dss):
            dvs.append(dot(back, e_s[at].astype(BF16), NT))
            dks.append(dot(q_s[qb][:PAD], ds, NT))
            dqs.append(dot(k_s[kb], ds, NN))
        for at, qb, kb, dv, dk, dq in zip(ats, qbs, kbs, dvs, dks, dqs):
            dv_s[kb] = kept(dv_s[kb], later_k_s[at]) + dv
            dk_s[kb] = kept(dk_s[kb], later_k_s[at]) + dk
            dq_s[qb] = kept(dq_s[qb], later_q_s[at]) + dq
        return carry

    lax.fori_loop(0, (count + 8 - 1) // 8 if True else 0, backward, 0)

    for s in range(HEADS):
        b, half = s // 2, s % 2
        lanes = slice(half * ROWS, (half + 1) * ROWS)
        g_ref[s] = jnp.concatenate(
            [
                dq_s[b, :HEAD, lanes] * SCALE,
                dk_s[b, :HEAD, lanes] * SCALE,
                dv_s[b, :HEAD, lanes],
            ],
            axis=0,
        ).astype(BF16)


def attend(me, extents, received):
    return pl.pallas_call(
        attend_body,
        out_shape=(
            jax.ShapeDtypeStruct((HEADS, 3 * HEAD, ROWS), BF16),
            jax.ShapeDtypeStruct((HEADS, HEAD, ROWS), BF16),
        ),
        in_specs=[
            pl.BlockSpec(memory_space=pltpu.SMEM),
            pl.BlockSpec(memory_space=pltpu.SMEM),
            pl.BlockSpec(memory_space=pltpu.VMEM),
        ],
        scratch_shapes=[
            pltpu.VMEM((BLOCKS + 1, 128, BLOCK), BF16),
            pltpu.VMEM((BLOCKS + 1, PAD, BLOCK), BF16),
            pltpu.VMEM((BLOCKS + 1, PAD, BLOCK), BF16),
            pltpu.VMEM((BLOCKS + 1, PAD, BLOCK), BF16),
            pltpu.VMEM((BLOCKS + 1, BLOCK, 128), BF16),
            pltpu.VMEM((BLOCKS + 1, BLOCK, 128), BF16),
            pltpu.VMEM((PAIRS, BLOCK, BLOCK), F32),
            pltpu.VMEM((BLOCKS + 1, PAD, BLOCK), F32),
            pltpu.VMEM((BLOCKS + 1, PAD, BLOCK), F32),
            pltpu.VMEM((BLOCKS + 1, PAD, BLOCK), F32),
            pltpu.VMEM((BLOCKS + 1, PAD, BLOCK), F32),
            pltpu.VMEM((BLOCKS + 1, 1, BLOCK), F32),
            pltpu.VMEM((PAIRS, 1, BLOCK), F32),
            pltpu.VMEM((BLOCKS + 1, 1, BLOCK), F32),
            pltpu.VMEM((BLOCKS + 1, 1, BLOCK), F32),
            pltpu.SMEM((PAIRS,), jnp.int32),
            pltpu.SMEM((PAIRS,), jnp.int32),
            pltpu.SMEM((PAIRS,), jnp.int32),
            pltpu.SMEM((PAIRS,), jnp.int32),
        ],
        compiler_params=pltpu.CompilerParams(vmem_limit_bytes=VMEM_LIMIT),
        cost_estimate=pl.CostEstimate(flops=10**10, bytes_accessed=0, transcendentals=0),
        name="attend",
    )(me, extents, received)


def unpack_body(y_ref, dq_ref, dk_ref, dv_ref):
    for j, ref in enumerate((dq_ref, dk_ref, dv_ref)):
        rows = [y_ref[h].astype(F32)[j * HEAD : (j + 1) * HEAD] for h in range(HEADS)]
        ref[...] = jnp.concatenate(rows, axis=0).T.astype(BF16)


def unpack(returned):
    shape = jax.ShapeDtypeStruct((ROWS, HEADS * HEAD), BF16)
    return pl.pallas_call(
        unpack_body,
        out_shape=(shape, shape, shape),
        compiler_params=pltpu.CompilerParams(vmem_limit_bytes=VMEM_LIMIT),
        cost_estimate=pl.CostEstimate(flops=10**11, bytes_accessed=0, transcendentals=0),
        name="unpack",
    )(returned)


def weight_body(tile_ref, mine_ref, got_ref, *refs):
    sources, out_ref, grads, sems = refs[:8], refs[8], refs[9], refs[10]
    copies = [
        pltpu.make_async_copy(source, grads.at[pl.ds(i * ROWS, ROWS)], sems.at[i])
        for i, source in enumerate(sources)
    ]
    for copy in copies:
        copy.start()
    total = jnp.zeros((2 * HEAD, HEADS * HEAD), F32)
    for i in range(0, 8, 2):
        left = jnp.concatenate(
            [
                jnp.concatenate([mine_ref[j], got_ref[j]], axis=0) for j in (i, i + 1)
            ],
            axis=1,
        )
        copies[i].wait()
        copies[i + 1].wait()
        total = total + dot(left, grads[i * ROWS : (i + 2) * ROWS], NN)
    for tile in range(8):
        out_ref[tile_ref[tile]] = total[:, tile * 144 : (tile + 1) * 144].astype(BF16)


def weight_terms(places, mine, got, grads):
    return pl.pallas_call(
        weight_body,
        out_shape=jax.ShapeDtypeStruct((8, 2 * HEAD, 144), BF16),
        in_specs=[pl.BlockSpec(memory_space=pltpu.SMEM)]
        + [pl.BlockSpec(memory_space=pltpu.VMEM)] * 2
        + [pl.BlockSpec(memory_space=pl.ANY)] * 8,
        out_specs=pl.BlockSpec(memory_space=pltpu.VMEM),
        scratch_shapes=[
            pltpu.VMEM((8 * ROWS, HEADS * HEAD), BF16),
            pltpu.SemaphoreType.DMA((8,)),
        ],
        compiler_params=pltpu.CompilerParams(vmem_limit_bytes=VMEM_LIMIT),
        cost_estimate=pl.CostEstimate(flops=10**9, bytes_accessed=0, transcendentals=0),
        name="weight_terms",
    )(places, mine, got, *grads)


def swap(x, axis, size, apart):
    return lax.ppermute(x, axis, [(i, i ^ apart) for i in range(size)])


def local(queries, keys, values, out_grad, out_weight, extents):
    me = lax.axis_index("seq")
    part = lax.axis_index("dp")

    sent = pack(queries, keys, values, out_grad, out_weight)
    received = lax.all_to_all(sent, "seq", 0, 0, tiled=True)
    late, received = lax.optimization_barrier((out_grad, received))
    far = [out_grad] + [swap(late, "seq", HEADS, apart) for apart in (2, 8, 10)]
    near = [swap(x, "seq", HEADS, 1) for x in far]
    out_grads = [x for pair in zip(far, near) for x in pair]

    grads, attended = attend(me[None].astype(jnp.int32), extents, received)
    got = swap(attended[8:], "seq", HEADS, 4)
    returned = lax.all_to_all(grads, "seq", 0, 0, tiled=True)

    x_lo, y = part // 4, part % 4
    tile = jnp.arange(8, dtype=jnp.int32)
    places = ((tile // 4) ^ x_lo) + 2 * ((tile % 4) ^ y)
    terms = weight_terms(places.astype(jnp.int32), attended[:8], got, out_grads)
    total = terms[:2].astype(F32)
    for apart in (1, 2, 3):
        total = total + swap(terms[2 * apart : 2 * apart + 2], "dp", 8, apart).astype(F32)
    weight_grad = total[0, :HEAD]
    for x_apart, z_apart in ((1, 0), (0, 1), (1, 1)):
        give = total[x_apart, z_apart * HEAD : (z_apart + 1) * HEAD].astype(BF16)
        pairs = [(i, i ^ (64 * x_apart + 4 * z_apart)) for i in range(128)]
        weight_grad = weight_grad + lax.ppermute(give, ("dp", "seq"), pairs).astype(F32)

    query_grad, key_grad, value_grad = unpack(returned)
    return query_grad, key_grad, value_grad, weight_grad


def solution(mesh):
    tokens = P(("dp", "seq"), None)
    return jax.shard_map(
        local,
        mesh=mesh,
        in_specs=(tokens, tokens, tokens, tokens, P(), P("dp", None)),
        out_specs=(tokens, tokens, tokens, P("seq", "dp")),
        check_vma=False,
    )
```

time: 105 us -> 80.5 us (0.77)
  blocking collectives: 27.2 us -> 0 us
  starting transfers between devices: 13.1 us -> 29.4 us
  Pallas kernels: 25.9 us -> 16.5 us
  local copies, waits for them, and re-layouts: 8.46 us -> 0.74 us
  waiting for transfers between devices: 24 us -> 31.3 us
  matrix products: 4.41 us -> 0 us
    all_to_all x1 -> x0, blocking collectives: 27.2 us -> none  [local(): received = lax.all_to_all(sent, 'seq', 0, 0, tiled=True)]
    ppermute x2 -> x14, starting transfers between devices: 0.45 us -> 16.4 us  [the longest x11 12.8 us: swap(): return lax.ppermute(x, axis, [(i, i ^ apart) for i in range(size)])]
    pallas_call x1, Pallas kernels: 23.9 us -> 9.14 us  [attend(): pl.pallas_call(attend_body, out_shape=(jax.ShapeDtypeStruct((HEADS, 3 * H...]
    ppermute x2 -> x14, waiting for transfers between devices: 0.01 us -> 12.3 us  [the longest x11 9.53 us: swap(): return lax.ppermute(x, axis, [(i, i ^ apart) for i in range(size)])]
    all_to_all x1, waiting for transfers between devices: 10.2 us -> 0.01 us  [local(): returned = lax.all_to_all(grads, 'seq', 0, 0, tiled=True)]
    unnamed x12 -> x4, local copies, waits for them, and re-layouts: 5.59 us -> 0.01 us
    all_to_all x2 -> x1, waiting for transfers between devices: 13.8 us -> 19 us  [local(): received = lax.all_to_all(sent, 'seq', 0, 0, tiled=True)]
    dot_general x2 -> x0, matrix products: 4.41 us -> none  [term(): return jnp.einsum('shr,srd->hd', rows, grad_all, preferred_element_type=F32)]
  transfers between devices with their start and end apart: 5 -> 16, of which waited for: 3 -> 9; matrix products, arithmetic and copies ran while one was open for 5% -> 2% of each run, Pallas kernels for 24% -> 14%
where the time goes in v2:
time: 80.5 us; the launch traced here: 79.4 us
  waiting for transfers between devices  31.3 us (39%)
  starting transfers between devices  29.4 us (37%)
  Pallas kernels  16.5 us (20%)
    all_to_all x1, waiting for transfers between devices, local(): received = lax.all_to_all(sent, 'seq', 0, 0, tiled=True)  19 us
    ppermute x11, starting transfers between devices, swap(): return lax.ppermute(x, axis, [(i, i ^ apart) for i in range(size)])  12.8 us
    ppermute x11, waiting for transfers between devices, swap(): return lax.ppermute(x, axis, [(i, i ^ apart) for i in range(size)])  9.53 us
    pallas_call x1, Pallas kernels, attend(): pl.pallas_call(attend_body, out_shape=(jax.ShapeDtypeStruct((HEADS, 3 * H...  9.14 us
    all_to_all x1, starting transfers between devices, local(): received = lax.all_to_all(sent, 'seq', 0, 0, tiled=True)  8.11 us
    all_to_all x1, starting transfers between devices, local(): returned = lax.all_to_all(grads, 'seq', 0, 0, tiled=True)  4.96 us
    pallas_call x1, Pallas kernels, pack(): pl.pallas_call(pack_body, out_shape=jax.ShapeDtypeStruct((HEADS, 4 * HEAD...  4.09 us
    ppermute x3, starting transfers between devices, local(): lax.ppermute(give, ('dp', 'seq'), pairs).astype(F32)  3.57 us
  transfers between devices with their start and end apart: 16, of which 9 were waited for; matrix products, arithmetic and copies ran while one was open for 2% of the time, Pallas kernels for 14%

profile of v2, /device:TPU:0, one launch (start us, length us, event | category | flops | bytes accessed | tf_op | source)
XLA Modules:
  0.0 79.4 jit_solution(5506607043143241712)
XLA Ops:
  0.6 4.1 %pack.1 = bf16[16,288,128]{2,1,0:T(8,128)(2,1)} custom-call(bf16[128,1152]{1,0:T(8,128)(2,1)} %q_hbm.1, bf16[128,1152]{1,0:T(8,128)(2,1)} %k_hbm.1, bf16[128,1152]{1,0:T(8,128)(2,1)} %v_hbm.1, bf16[128,1152]{1,0:T(8,128)(2,1)} %refs_0_.1, bf16[1152,1152]{1,0:T(8,128)(2,1)} %w_hbm.1), custom_call_target="tpu_custom_call" | custom-call | flops 10000000000 | tf_op jit(solution)/shard_map/pack/pallas_call | solution.py:58
  4.7 0.0 copy-start
  4.7 0.0 copy-start.1
  4.8 8.1 %all-to-all-start = ((bf16[16,288,128]{2,1,0:T(8,128)(2,1)}), bf16[16,288,128]{2,1,0:T(8,128)(2,1)S(1)}, u32[]{:S(2)}, u32[]{:S(2)}) async-start(bf16[16,288,128]{2,1,0:T(8,128)(2,1)} %pack.1), calls=%async_computation | async-start | bytes 2359296 | tf_op jit(solution)/shard_map/all_to_all | solution.py:319
  12.9 0.0 copy-done
  12.9 0.5 collective-permute-start.1
  13.4 19.0 %all-to-all-done.r_ref = bf16[16,288,128]{2,1,0:T(8,128)(2,1)S(1)} async-done(((bf16[16,288,128]{2,1,0:T(8,128)(2,1)}), bf16[16,288,128]{2,1,0:T(8,128)(2,1)S(1)}, u32[]{:S(2)}, u32[]{:S(2)}) %all-to-all-start) | async-done | bytes 1179680 | tf_op jit(solution)/shard_map/all_to_all | solution.py:319
  32.3 0.9 %collective-permute-start.6 = (bf16[128,1152]{1,0:T(8,128)(2,1)S(1)}, bf16[128,1152]{1,0:T(8,128)(2,1)S(1)}, u32[]{:S(2)}, u32[]{:S(2)}) collective-permute-start(bf16[128,1152]{1,0:T(8,128)(2,1)S(1)} %copy-done), channel_id=1, source_target_pairs={{0,10},{1,11},{2,8},{3,9},{4,14},{5,15},{6,12},{7,13},{8,2},{9,3},... | collective-permute-start | bytes 884744 | tf_op jit(solution)/shard_map/ppermute | solution.py:311
  33.3 2.7 %collective-permute-start.4 = (bf16[128,1152]{1,0:T(8,128)(2,1)S(1)}, bf16[128,1152]{1,0:T(8,128)(2,1)S(1)}, u32[]{:S(2)}, u32[]{:S(2)}) collective-permute-start(bf16[128,1152]{1,0:T(8,128)(2,1)S(1)} %copy-done), channel_id=1, source_target_pairs={{0,8},{1,9},{2,10},{3,11},{4,12},{5,13},{6,14},{7,15},{8,0},{9,1},... | collective-permute-start | bytes 884744 | tf_op jit(solution)/shard_map/ppermute | solution.py:311
  36.0 2.8 %collective-permute-start.2 = (bf16[128,1152]{1,0:T(8,128)(2,1)S(1)}, bf16[128,1152]{1,0:T(8,128)(2,1)S(1)}, u32[]{:S(2)}, u32[]{:S(2)}) collective-permute-start(bf16[128,1152]{1,0:T(8,128)(2,1)S(1)} %copy-done), channel_id=1, source_target_pairs={{0,2},{1,3},{2,0},{3,1},{4,6},{5,7},{6,4},{7,5},{8,10},{9,11},{10,... | collective-permute-start | bytes 884744 | tf_op jit(solution)/shard_map/ppermute | solution.py:311
  38.8 0.0 copy-done.1
  38.8 9.1 %attend.1 = (bf16[16,216,128]{2,1,0:T(8,128)(2,1)}, bf16[16,72,128]{2,1,0:T(8,128)(2,1)S(1)}) custom-call(s32[1]{0:T(128)} %bitcast.me_ref, s32[1,8]{1,0:T(1,128)S(1)} %copy-done.1, bf16[16,288,128]{2,1,0:T(8,128)(2,1)S(1)} %all-to-all-done.r_ref), custom_call_target="tpu_custom_call" | custom-call | flops 10000000000 | tf_op jit(solution)/shard_map/attend/pallas_call | solution.py:214
  48.0 0.0 collective-permute-done.6.refs_6_
  48.0 0.0 collective-permute-start.7
  48.0 2.0 %collective-permute-done.4.refs_4_ = bf16[128,1152]{1,0:T(8,128)(2,1)S(1)} collective-permute-done((bf16[128,1152]{1,0:T(8,128)(2,1)S(1)}, bf16[128,1152]{1,0:T(8,128)(2,1)S(1)}, u32[]{:S(2)}, u32[]{:S(2)}) %collective-permute-start.4) | collective-permute-done | bytes 294944 | tf_op jit(solution)/shard_map/ppermute | solution.py:311
  50.0 0.0 collective-permute-start.5
  50.0 0.0 collective-permute-done.2.refs_2_
  50.1 0.5 collective-permute-start.3
  50.6 0.7 fusion.9
  51.2 0.0 collective-permute-start
  51.3 5.0 %all-to-all-start.1 = ((bf16[16,216,128]{2,1,0:T(8,128)(2,1)}), bf16[16,216,128]{2,1,0:T(8,128)(2,1)S(1)}, u32[]{:S(2)}, u32[]{:S(2)}) async-start(bf16[16,216,128]{2,1,0:T(8,128)(2,1)} %get-tuple-element.12), calls=%async_computation.1 | async-start | bytes 1769472 | tf_op jit(solution)/shard_map/all_to_all | solution.py:327
  56.3 0.0 collective-permute-done.1.refs_1_
  56.3 0.9 %collective-permute-done.got_ref = bf16[8,72,128]{2,1,0:T(8,128)(2,1)S(1)} collective-permute-done((bf16[8,72,128]{2,1,0:T(8,128)(2,1)}, bf16[8,72,128]{2,1,0:T(8,128)(2,1)S(1)}, u32[]{:S(2)}, u32[]{:S(2)}) %collective-permute-start) | collective-permute-done | bytes 147488 | tf_op jit(solution)/shard_map/ppermute | solution.py:311
  57.2 0.0 collective-permute-done.7.refs_7_
  57.2 0.0 collective-permute-done.5.refs_5_
  57.2 0.0 collective-permute-done.3.refs_3_
  57.2 2.2 %weight_terms.1 = bf16[8,144,144]{2,1,0:T(8,128)(2,1)S(1)} custom-call(s32[8]{0:T(128)S(1)} %fusion.5.tile_ref, bf16[8,72,128]{2,1,0:T(8,128)(2,1)S(1)} %get-tuple-element.24.mine_ref, bf16[8,72,128]{2,1,0:T(8,128)(2,1)S(1)} %collective-permute-done.got_ref, bf16[128,1152]{1,0:T(8,128)(2,1)S(1)} %copy-done, ...), custom_call_target="tpu_custom_call" | custom-call | flops 1000000000 | tf_op jit(solution)/shard_map/weight_terms/pallas_call | solution.py:293
  59.4 1.7 %collective-permute-start.8 = (bf16[2,144,144]{2,1,0:T(8,128)(2,1)S(1)}, bf16[2,144,144]{2,1,0:T(8,128)(2,1)S(1)}, u32[]{:S(2)}, u32[]{:S(2)}) collective-permute-start(bf16[2,144,144]{2,1,0:T(8,128)(2,1)S(1)} %get-tuple-element.20), channel_id=1, source_target_pairs={{0,16},{16,0},{32,48},{48,32},{64,80},{80,64},{96,112},{112,96},{1... | collective-permute-start | bytes 248840 | tf_op jit(solution)/shard_map/ppermute | solution.py:311
  61.1 2.2 %collective-permute-start.10 = (bf16[2,144,144]{2,1,0:T(8,128)(2,1)S(1)}, bf16[2,144,144]{2,1,0:T(8,128)(2,1)S(1)}, u32[]{:S(2)}, u32[]{:S(2)}) collective-permute-start(bf16[2,144,144]{2,1,0:T(8,128)(2,1)S(1)} %get-tuple-element.21), channel_id=1, source_target_pairs={{0,48},{16,32},{32,16},{48,0},{64,112},{80,96},{96,80},{112,64},{1... | collective-permute-start | bytes 248840 | tf_op jit(solution)/shard_map/ppermute | solution.py:311
  63.3 1.4 %collective-permute-start.9 = (bf16[2,144,144]{2,1,0:T(8,128)(2,1)S(1)}, bf16[2,144,144]{2,1,0:T(8,128)(2,1)S(1)}, u32[]{:S(2)}, u32[]{:S(2)}) collective-permute-start(bf16[2,144,144]{2,1,0:T(8,128)(2,1)S(1)} %get-tuple-element.22), channel_id=1, source_target_pairs={{0,32},{16,48},{32,0},{48,16},{64,96},{80,112},{96,64},{112,80},{1... | collective-permute-start | bytes 248840 | tf_op jit(solution)/shard_map/ppermute | solution.py:311
  64.7 0.1 collective-permute-done.8
  64.8 4.6 %collective-permute-done.10 = bf16[2,144,144]{2,1,0:T(8,128)(2,1)S(1)} collective-permute-done((bf16[2,144,144]{2,1,0:T(8,128)(2,1)S(1)}, bf16[2,144,144]{2,1,0:T(8,128)(2,1)S(1)}, u32[]{:S(2)}, u32[]{:S(2)}) %collective-permute-start.10) | collective-permute-done | bytes 82976 | tf_op jit(solution)/shard_map/ppermute | solution.py:311
  69.4 1.8 %collective-permute-done.9 = bf16[2,144,144]{2,1,0:T(8,128)(2,1)S(1)} collective-permute-done((bf16[2,144,144]{2,1,0:T(8,128)(2,1)S(1)}, bf16[2,144,144]{2,1,0:T(8,128)(2,1)S(1)}, u32[]{:S(2)}, u32[]{:S(2)}) %collective-permute-start.9) | collective-permute-done | bytes 82976 | tf_op jit(solution)/shard_map/ppermute | solution.py:311
  71.2 0.1 fusion.7
  71.3 0.8 collective-permute-start.11
  72.1 1.6 %collective-permute-start.13 = (bf16[72,144]{1,0:T(8,128)(2,1)S(1)}, bf16[72,144]{1,0:T(8,128)(2,1)S(1)}, u32[]{:S(2)}, u32[]{:S(2)}) collective-permute-start(bf16[72,144]{1,0:T(8,128)(2,1)S(1)} %get-tuple-element.26), channel_id=1, source_target_pairs={{0,68},{1,69},{2,70},{3,71},{4,64},{5,65},{6,66},{7,67},{8,76},{9,... | collective-permute-start | bytes 62216 | tf_op jit(solution)/shard_map/ppermute | solution.py:340
  73.8 1.2 %collective-permute-start.12 = (bf16[72,144]{1,0:T(8,128)(2,1)S(1)}, bf16[72,144]{1,0:T(8,128)(2,1)S(1)}, u32[]{:S(2)}, u32[]{:S(2)}) collective-permute-start(bf16[72,144]{1,0:T(8,128)(2,1)S(1)} %get-tuple-element.27), channel_id=1, source_target_pairs={{0,4},{1,5},{2,6},{3,7},{4,0},{5,1},{6,2},{7,3},{8,12},{9,13},{10,... | collective-permute-start | bytes 62216 | tf_op jit(solution)/shard_map/ppermute | solution.py:340
  74.9 0.5 collective-permute-done.11
  75.4 1.6 %collective-permute-done.13 = bf16[72,144]{1,0:T(8,128)(2,1)S(1)} collective-permute-done((bf16[72,144]{1,0:T(8,128)(2,1)S(1)}, bf16[72,144]{1,0:T(8,128)(2,1)S(1)}, u32[]{:S(2)}, u32[]{:S(2)}) %collective-permute-start.13) | collective-permute-done | bytes 20768 | tf_op jit(solution)/shard_map/ppermute | solution.py:340
  77.0 0.7 collective-permute-done.12
  77.7 0.7 fusion.2
  78.4 0.0 all-to-all-done.1.y_ref
  78.4 1.1 %unpack.1 = (bf16[128,1152]{1,0:T(8,128)(2,1)}, bf16[128,1152]{1,0:T(8,128)(2,1)}, bf16[128,1152]{1,0:T(8,128)(2,1)}) custom-call(bf16[16,216,128]{2,1,0:T(8,128)(2,1)S(1)} %all-to-all-done.1.y_ref), custom_call_target="tpu_custom_call" | custom-call | flops 99999997952 | tf_op jit(solution)/shard_map/unpack/pallas_call | solution.py:260
  (3 shorter events, 0.0 us)
Async XLA Ops:
  4.7 8.1 %copy-start = (bf16[128,1152]{1,0:T(8,128)(2,1)S(1)}, bf16[128,1152]{1,0:T(8,128)(2,1)}, u32[]{:S(2)}) copy-start(bf16[128,1152]{1,0:T(8,128)(2,1)} %refs_0_.1) | copy-start | bytes 884740
  4.7 34.1 %copy-start.1 = (s32[1,8]{1,0:T(1,128)S(1)}, s32[1,8]{1,0:T(1,128)}, u32[]{:S(2)}) copy-start(s32[1,8]{1,0:T(1,128)} %ext_ref.1) | copy-start | bytes 100
  4.8 27.6 %all-to-all-start = ((bf16[16,288,128]{2,1,0:T(8,128)(2,1)}), bf16[16,288,128]{2,1,0:T(8,128)(2,1)S(1)}, u32[]{:S(2)}, u32[]{:S(2)}) async-start(bf16[16,288,128]{2,1,0:T(8,128)(2,1)} %pack.1), calls=%async_computation | async-start | bytes 2359296 | tf_op jit(solution)/shard_map/all_to_all | solution.py:319
  12.9 43.4 %collective-permute-start.1 = (bf16[128,1152]{1,0:T(8,128)(2,1)S(1)}, bf16[128,1152]{1,0:T(8,128)(2,1)S(1)}, u32[]{:S(2)}, u32[]{:S(2)}) collective-permute-start(bf16[128,1152]{1,0:T(8,128)(2,1)S(1)} %copy-done), channel_id=1, source_target_pairs={{0,1},{1,0},{2,3},{3,2},{4,5},{5,4},{6,7},{7,6},{8,9},{9,8},{10,11... | collective-permute-start | bytes 884744 | tf_op jit(solution)/shard_map/ppermute | solution.py:311
  32.3 15.6 %collective-permute-start.6 = (bf16[128,1152]{1,0:T(8,128)(2,1)S(1)}, bf16[128,1152]{1,0:T(8,128)(2,1)S(1)}, u32[]{:S(2)}, u32[]{:S(2)}) collective-permute-start(bf16[128,1152]{1,0:T(8,128)(2,1)S(1)} %copy-done), channel_id=1, source_target_pairs={{0,10},{1,11},{2,8},{3,9},{4,14},{5,15},{6,12},{7,13},{8,2},{9,3},... | collective-permute-start | bytes 884744 | tf_op jit(solution)/shard_map/ppermute | solution.py:311
  33.3 16.8 %collective-permute-start.4 = (bf16[128,1152]{1,0:T(8,128)(2,1)S(1)}, bf16[128,1152]{1,0:T(8,128)(2,1)S(1)}, u32[]{:S(2)}, u32[]{:S(2)}) collective-permute-start(bf16[128,1152]{1,0:T(8,128)(2,1)S(1)} %copy-done), channel_id=1, source_target_pairs={{0,8},{1,9},{2,10},{3,11},{4,12},{5,13},{6,14},{7,15},{8,0},{9,1},... | collective-permute-start | bytes 884744 | tf_op jit(solution)/shard_map/ppermute | solution.py:311
  36.0 14.0 %collective-permute-start.2 = (bf16[128,1152]{1,0:T(8,128)(2,1)S(1)}, bf16[128,1152]{1,0:T(8,128)(2,1)S(1)}, u32[]{:S(2)}, u32[]{:S(2)}) collective-permute-start(bf16[128,1152]{1,0:T(8,128)(2,1)S(1)} %copy-done), channel_id=1, source_target_pairs={{0,2},{1,3},{2,0},{3,1},{4,6},{5,7},{6,4},{7,5},{8,10},{9,11},{10,... | collective-permute-start | bytes 884744 | tf_op jit(solution)/shard_map/ppermute | solution.py:311
  48.0 9.2 %collective-permute-start.7 = (bf16[128,1152]{1,0:T(8,128)(2,1)S(1)}, bf16[128,1152]{1,0:T(8,128)(2,1)S(1)}, u32[]{:S(2)}, u32[]{:S(2)}) collective-permute-start(bf16[128,1152]{1,0:T(8,128)(2,1)S(1)} %collective-permute-done.6.refs_6_), channel_id=1, source_target_pairs={{0,1},{1,0},{2,3},{3,2},{4,5},{5,4},{6,7},{7,6},{8,9},{9,8},{10,11... | collective-permute-start | bytes 884744 | tf_op jit(solution)/shard_map/ppermute | solution.py:311
  50.0 7.2 %collective-permute-start.5 = (bf16[128,1152]{1,0:T(8,128)(2,1)S(1)}, bf16[128,1152]{1,0:T(8,128)(2,1)S(1)}, u32[]{:S(2)}, u32[]{:S(2)}) collective-permute-start(bf16[128,1152]{1,0:T(8,128)(2,1)S(1)} %collective-permute-done.4.refs_4_), channel_id=1, source_target_pairs={{0,1},{1,0},{2,3},{3,2},{4,5},{5,4},{6,7},{7,6},{8,9},{9,8},{10,11... | collective-permute-start | bytes 884744 | tf_op jit(solution)/shard_map/ppermute | solution.py:311
  50.1 7.2 %collective-permute-start.3 = (bf16[128,1152]{1,0:T(8,128)(2,1)S(1)}, bf16[128,1152]{1,0:T(8,128)(2,1)S(1)}, u32[]{:S(2)}, u32[]{:S(2)}) collective-permute-start(bf16[128,1152]{1,0:T(8,128)(2,1)S(1)} %collective-permute-done.2.refs_2_), channel_id=1, source_target_pairs={{0,1},{1,0},{2,3},{3,2},{4,5},{5,4},{6,7},{7,6},{8,9},{9,8},{10,11... | collective-permute-start | bytes 884744 | tf_op jit(solution)/shard_map/ppermute | solution.py:311
  51.2 6.0 %collective-permute-start = (bf16[8,72,128]{2,1,0:T(8,128)(2,1)}, bf16[8,72,128]{2,1,0:T(8,128)(2,1)S(1)}, u32[]{:S(2)}, u32[]{:S(2)}) collective-permute-start(bf16[8,72,128]{2,1,0:T(8,128)(2,1)} %get-tuple-element.23), channel_id=1, source_target_pairs={{0,4},{1,5},{2,6},{3,7},{4,0},{5,1},{6,2},{7,3},{8,12},{9,13},{10,... | collective-permute-start | bytes 442376 | tf_op jit(solution)/shard_map/ppermute | solution.py:311
  51.3 27.1 %all-to-all-start.1 = ((bf16[16,216,128]{2,1,0:T(8,128)(2,1)}), bf16[16,216,128]{2,1,0:T(8,128)(2,1)S(1)}, u32[]{:S(2)}, u32[]{:S(2)}) async-start(bf16[16,216,128]{2,1,0:T(8,128)(2,1)} %get-tuple-element.12), calls=%async_computation.1 | async-start | bytes 1769472 | tf_op jit(solution)/shard_map/all_to_all | solution.py:327
  59.4 5.3 %collective-permute-start.8 = (bf16[2,144,144]{2,1,0:T(8,128)(2,1)S(1)}, bf16[2,144,144]{2,1,0:T(8,128)(2,1)S(1)}, u32[]{:S(2)}, u32[]{:S(2)}) collective-permute-start(bf16[2,144,144]{2,1,0:T(8,128)(2,1)S(1)} %get-tuple-element.20), channel_id=1, source_target_pairs={{0,16},{16,0},{32,48},{48,32},{64,80},{80,64},{96,112},{112,96},{1... | collective-permute-start | bytes 248840 | tf_op jit(solution)/shard_map/ppermute | solution.py:311
  61.1 8.3 %collective-permute-start.10 = (bf16[2,144,144]{2,1,0:T(8,128)(2,1)S(1)}, bf16[2,144,144]{2,1,0:T(8,128)(2,1)S(1)}, u32[]{:S(2)}, u32[]{:S(2)}) collective-permute-start(bf16[2,144,144]{2,1,0:T(8,128)(2,1)S(1)} %get-tuple-element.21), channel_id=1, source_target_pairs={{0,48},{16,32},{32,16},{48,0},{64,112},{80,96},{96,80},{112,64},{1... | collective-permute-start | bytes 248840 | tf_op jit(solution)/shard_map/ppermute | solution.py:311
  63.3 7.9 %collective-permute-start.9 = (bf16[2,144,144]{2,1,0:T(8,128)(2,1)S(1)}, bf16[2,144,144]{2,1,0:T(8,128)(2,1)S(1)}, u32[]{:S(2)}, u32[]{:S(2)}) collective-permute-start(bf16[2,144,144]{2,1,0:T(8,128)(2,1)S(1)} %get-tuple-element.22), channel_id=1, source_target_pairs={{0,32},{16,48},{32,0},{48,16},{64,96},{80,112},{96,64},{112,80},{1... | collective-permute-start | bytes 248840 | tf_op jit(solution)/shard_map/ppermute | solution.py:311
  71.3 4.0 %collective-permute-start.11 = (bf16[72,144]{1,0:T(8,128)(2,1)S(1)}, bf16[72,144]{1,0:T(8,128)(2,1)S(1)}, u32[]{:S(2)}, u32[]{:S(2)}) collective-permute-start(bf16[72,144]{1,0:T(8,128)(2,1)S(1)} %get-tuple-element.25), channel_id=1, source_target_pairs={{0,64},{1,65},{2,66},{3,67},{4,68},{5,69},{6,70},{7,71},{8,72},{9,... | collective-permute-start | bytes 62216 | tf_op jit(solution)/shard_map/ppermute | solution.py:340
  72.1 4.9 %collective-permute-start.13 = (bf16[72,144]{1,0:T(8,128)(2,1)S(1)}, bf16[72,144]{1,0:T(8,128)(2,1)S(1)}, u32[]{:S(2)}, u32[]{:S(2)}) collective-permute-start(bf16[72,144]{1,0:T(8,128)(2,1)S(1)} %get-tuple-element.26), channel_id=1, source_target_pairs={{0,68},{1,69},{2,70},{3,71},{4,64},{5,65},{6,66},{7,67},{8,76},{9,... | collective-permute-start | bytes 62216 | tf_op jit(solution)/shard_map/ppermute | solution.py:340
  73.8 4.0 %collective-permute-start.12 = (bf16[72,144]{1,0:T(8,128)(2,1)S(1)}, bf16[72,144]{1,0:T(8,128)(2,1)S(1)}, u32[]{:S(2)}, u32[]{:S(2)}) collective-permute-start(bf16[72,144]{1,0:T(8,128)(2,1)S(1)} %get-tuple-element.27), channel_id=1, source_target_pairs={{0,4},{1,5},{2,6},{3,7},{4,0},{5,1},{6,2},{7,3},{8,12},{9,13},{10,... | collective-permute-start | bytes 62216 | tf_op jit(solution)/shard_map/ppermute | solution.py:340

commit v3 on v2

--- a/solution.py
+++ b/solution.py
@@ -14,14 +14,20 @@
 ROWS = 128
 BLOCK = 256
 BLOCKS = 8
-PAIRS = BLOCKS * BLOCKS + 8
+GROUP = 4
+PAIRS = BLOCKS * BLOCKS + 3 * GROUP
+TILE = 144
+REST = TILE - ROWS
+STRIP = 24
+PARTS = 4
 PAD = 80
 SCALE = HEAD**-0.5
 LOG2E = 1.4426950408889634
 FAR = 16384.0
 F32 = jnp.float32
 BF16 = jnp.bfloat16
-VMEM_LIMIT = 48 << 20
+VMEM_SOME = 12 << 20
+VMEM_MORE = 36 << 20
 VMEM_MOST = (64 << 20) - (128 << 10)
 
 NN = (((1,), (0,)), ((), ()))
@@ -32,36 +38,56 @@
     return lax.dot_general(a, b, dims, preferred_element_type=F32)
 
 
-def pack_body(q_hbm, k_hbm, v_hbm, g_hbm, w_hbm, out_ref, q_ref, k_ref, v_ref, g_ref, w_ref, sems):
-    copies = [
+def pack_body(
+    q_hbm, k_hbm, v_hbm, g_hbm, w_hbm, out_hbm, q_ref, k_ref, v_ref, g_ref, w_ref, out_ref, sems, out_sems
+):
+    width = HEADS * HEAD // PARTS
+    heads = HEADS // PARTS
+    ins = [
         pltpu.make_async_copy(source, target, sems.at[i])
         for i, (source, target) in enumerate(
-            [(q_hbm, q_ref), (k_hbm, k_ref), (v_hbm, v_ref), (g_hbm, g_ref), (w_hbm, w_ref)]
+            [(q_hbm, q_ref), (k_hbm, k_ref), (v_hbm, v_ref), (g_hbm, g_ref)]
+            + [(w_hbm.at[pl.ds(p * width, width)], w_ref.at[p]) for p in range(PARTS)]
         )
     ]
-    for copy in copies:
+    for copy in ins:
         copy.start()
-    parts = []
+    turned = []
     for i, ref in enumerate((q_ref, k_ref, v_ref)):
-        copies[i].wait()
-        parts.append(ref[...].astype(F32).T)
-    copies[3].wait()
-    copies[4].wait()
-    parts.append(dot(w_ref[...], g_ref[...], NT).astype(BF16).astype(F32))
-    for h in range(HEADS):
-        rows = slice(h * HEAD, (h + 1) * HEAD)
-        out_ref[h] = jnp.concatenate([part[rows] for part in parts], axis=0).astype(BF16)
+        ins[i].wait()
+        turned.append(ref[...].astype(F32).T)
+    ins[3].wait()
+    outs = []
+    for p in range(PARTS):
+        ins[4 + p].wait()
+        back = dot(w_ref[p], g_ref[...], NT).astype(BF16).astype(F32)
+        for i in range(heads):
+            h = p * heads + i
+            rows = [x[h * HEAD : (h + 1) * HEAD] for x in turned]
+            rows.append(back[i * HEAD : (i + 1) * HEAD])
+            out_ref[h] = jnp.concatenate(rows, axis=0).astype(BF16)
+        part = pl.ds(p * heads, heads)
+        outs.append(pltpu.make_async_copy(out_ref.at[part], out_hbm.at[part], out_sems.at[p]))
+        outs[p].start()
+    for copy in outs:
+        copy.wait()
 
 
 def pack(queries, keys, values, out_grad, out_weight):
     width = HEADS * HEAD
+    shape = (HEADS, 4 * HEAD, ROWS)
     return pl.pallas_call(
         pack_body,
-        out_shape=jax.ShapeDtypeStruct((HEADS, 4 * HEAD, ROWS), BF16),
+        out_shape=jax.ShapeDtypeStruct(shape, BF16),
         in_specs=[pl.BlockSpec(memory_space=pltpu.HBM)] * 5,
-        out_specs=pl.BlockSpec(memory_space=pltpu.VMEM),
+        out_specs=pl.BlockSpec(memory_space=pl.ANY),
         scratch_shapes=[pltpu.VMEM((ROWS, width), BF16)] * 4
-        + [pltpu.VMEM((width, width), BF16), pltpu.SemaphoreType.DMA((5,))],
+        + [
+            pltpu.VMEM((PARTS, width // PARTS, width), BF16),
+            pltpu.VMEM(shape, BF16),
+            pltpu.SemaphoreType.DMA((4 + PARTS,)),
+            pltpu.SemaphoreType.DMA((PARTS,)),
+        ],
         compiler_params=pltpu.CompilerParams(vmem_limit_bytes=VMEM_MOST),
         cost_estimate=pl.CostEstimate(flops=10**10, bytes_accessed=0, transcendentals=0),
         name="pack",
@@ -73,8 +99,9 @@
 
 
 def attend_body(
-    me_ref, ext_ref, r_ref, g_ref, att_ref, q_s, b_s, k_s, v_s, kn_s, vn_s, e_s, acc_s, dq_s, dk_s, dv_s,
-    top_s, pair_top_s, delta_s, inverse_s, qb_s, kb_s, later_q_s, later_k_s
+    me_ref, ext_ref, r_ref, g_ref, mine_ref, give_ref, q_s, b_s, k_s, v_s, kn_s, vn_s, e_s, acc_s, dq_s, dk_s, dv_s,
+    top_s, pair_top_s, delta_s, inverse_s, qb_s, kb_s, later_q_s, later_k_s,
+    even_s, odd_s, ds_even_s, ds_odd_s, back_even_s, back_odd_s
 ):
     ends = []
     total = jnp.int32(0)
@@ -128,38 +155,46 @@
         lax.fori_loop(0, size, add_pair, 0)
         count = count + size
         reached = lo + size
-    for u in range(8):
+    for u in range(3 * GROUP):
         qb_s[count + u] = BLOCKS
         kb_s[count + u] = BLOCKS
         later_q_s[count + u] = 0
         later_k_s[count + u] = 0
 
+    def score(at, ref, u):
+        scores = dot(kn_s[kb_s[at]][:, :PAD], q_s[qb_s[at]][:PAD], NN)
+        ref[u] = scores
+        top = jnp.max(scores.reshape(BLOCK // 8, 8, BLOCK), axis=0)
+        pair_top_s[at] = jnp.max(top, axis=0, keepdims=True)
+
+    def soften(at, ref, u):
+        e = jnp.exp2((ref[u] - pair_top_s[at]) * (SCALE * LOG2E))
+        e_s[at] = e
+        return dot(v_s[kb_s[at]], e.astype(BF16), NN)
+
+    def gather(at, term):
+        qb, top = qb_s[at], pair_top_s[at]
+        before = top_s[qb]
+        after = jnp.maximum(before, top)
+        top_s[qb] = after
+        acc_s[qb] = kept(acc_s[qb], later_q_s[at]) * jnp.exp2(
+            (before - after) * (SCALE * LOG2E)
+        ) + term * jnp.exp2((top - after) * (SCALE * LOG2E))
+
     def forward(i, carry):
-        ats = [8 * i + u for u in range(8)]
-        qbs = [qb_s[at] for at in ats]
-        kbs = [kb_s[at] for at in ats]
-        tops = []
-        for at, qb, kb in zip(ats, qbs, kbs):
-            scores = dot(kn_s[kb], q_s[qb], NN)
-            e_s[at] = scores
-            top = jnp.max(scores.reshape(BLOCK // 8, 8, BLOCK), axis=0)
-            tops.append(jnp.max(top, axis=0, keepdims=True))
-        terms = []
-        for at, kb, top in zip(ats, kbs, tops):
-            e = jnp.exp2((e_s[at] - top) * (SCALE * LOG2E))
-            e_s[at] = e
-            pair_top_s[at] = top
-            terms.append(dot(v_s[kb], e.astype(BF16), NN))
-        for at, qb, top, term in zip(ats, qbs, tops, terms):
-            before = top_s[qb]
-            after = jnp.maximum(before, top)
-            top_s[qb] = after
-            acc_s[qb] = kept(acc_s[qb], later_q_s[at]) * jnp.exp2((before - after) * (SCALE * LOG2E)) + term * jnp.exp2(
-                (top - after) * (SCALE * LOG2E)
-            )
+        for first, now, ahead in ((2 * i, even_s, odd_s), (2 * i + 1, odd_s, even_s)):
+            terms = []
+            for u in range(GROUP):
+                score((first + 1) * GROUP + u, ahead, u)
+                terms.append(soften(first * GROUP + u, now, u))
+            for u in range(GROUP):
+                gather(first * GROUP + u, terms[u])
         return carry
 
-    lax.fori_loop(0, (count + 8 - 1) // 8 if True else 0, forward, 0)
+    rounds = (count + 2 * GROUP - 1) // (2 * GROUP)
+    for u in range(GROUP):
+        score(u, even_s, u)
+    lax.fori_loop(0, rounds, forward, 0)
 
     for qb in range(BLOCKS):
         acc = acc_s[qb]
@@ -167,35 +202,55 @@
         attended = (acc[:HEAD] * inverse).astype(BF16)
         for half in range(2):
             apart = (2 * qb + half) ^ me_ref[0]
-            place = (apart & 3) + ((apart >> 3) << 2) + ((apart & 4) << 1)
-            att_ref[place] = attended[:, half * ROWS : (half + 1) * ROWS]
+            place = (apart & 3) + ((apart >> 3) << 2)
+            rows = attended[:, half * ROWS : (half + 1) * ROWS]
+
+            @pl.when(apart & 4 == 0)
+            def _(place=place, rows=rows):
+                mine_ref[place] = rows
+
+            @pl.when(apart & 4 != 0)
+            def _(place=place, rows=rows):
+                give_ref[place] = rows
+
         back = b_s[qb].astype(F32)
         delta_s[qb] = jnp.sum(back[:HEAD] * attended.astype(F32), axis=0, keepdims=True)
         inverse_s[qb] = inverse
 
+    def differ(at, ds_ref, back_ref, u):
+        qb = qb_s[at]
+        factor = jnp.exp2((pair_top_s[at] - top_s[qb]) * (SCALE * LOG2E)) * inverse_s[qb]
+        back = (b_s[qb].astype(F32) * factor).astype(BF16)
+        back_ref[u] = back
+        dprobs = dot(vn_s[kb_s[at]][:, :PAD], back, NN)
+        ds_ref[u] = (e_s[at] * (dprobs - delta_s[qb] * factor)).astype(BF16)
+
+    def products(at, ds_ref, back_ref, u):
+        dv = dot(back_ref[u], e_s[at].astype(BF16), NT)
+        dk = dot(q_s[qb_s[at]][:PAD], ds_ref[u], NT)
+        dq = dot(k_s[kb_s[at]], ds_ref[u], NN)
+        return dv, dk, dq
+
+    def collect(at, dv, dk, dq):
+        qb, kb = qb_s[at], kb_s[at]
+        dv_s[kb] = kept(dv_s[kb], later_k_s[at]) + dv
+        dk_s[kb] = kept(dk_s[kb], later_k_s[at]) + dk
+        dq_s[qb] = kept(dq_s[qb], later_q_s[at]) + dq
+
     def backward(i, carry):
-        ats = [8 * i + u for u in range(8)]
-        qbs = [qb_s[at] for at in ats]
-        kbs = [kb_s[at] for at in ats]
-        backs, dss = [], []
-        for at, qb, kb in zip(ats, qbs, kbs):
-            factor = jnp.exp2((pair_top_s[at] - top_s[qb]) * (SCALE * LOG2E)) * inverse_s[qb]
-            back = (b_s[qb].astype(F32) * factor).astype(BF16)
-            back_wide = jnp.concatenate([back, jnp.zeros((128 - PAD, BLOCK), BF16)], axis=0)
-            backs.append(back)
-            dss.append((e_s[at] * (dot(vn_s[kb], back_wide, NN) - delta_s[qb] * factor)).astype(BF16))
-        dvs, dks, dqs = [], [], []
-        for at, qb, kb, back, ds in zip(ats, qbs, kbs, backs, dss):
-            dvs.append(dot(back, e_s[at].astype(BF16), NT))
-            dks.append(dot(q_s[qb][:PAD], ds, NT))
-            dqs.append(dot(k_s[kb], ds, NN))
-        for at, qb, kb, dv, dk, dq in zip(ats, qbs, kbs, dvs, dks, dqs):
-            dv_s[kb] = kept(dv_s[kb], later_k_s[at]) + dv
-            dk_s[kb] = kept(dk_s[kb], later_k_s[at]) + dk
-            dq_s[qb] = kept(dq_s[qb], later_q_s[at]) + dq
+        for first, now, ahead in ((2 * i, even, odd), (2 * i + 1, odd, even)):
+            terms = []
+            for u in range(GROUP):
+                differ((first + 1) * GROUP + u, *ahead, u)
+                terms.append(products(first * GROUP + u, *now, u))
+            for u in range(GROUP):
+                collect(first * GROUP + u, *terms[u])
         return carry
 
-    lax.fori_loop(0, (count + 8 - 1) // 8 if True else 0, backward, 0)
+    even, odd = (ds_even_s, back_even_s), (ds_odd_s, back_odd_s)
+    for u in range(GROUP):
+        differ(u, *even, u)
+    lax.fori_loop(0, rounds, backward, 0)
 
     for s in range(HEADS):
         b, half = s // 2, s % 2
@@ -215,7 +270,8 @@
         attend_body,
         out_shape=(
             jax.ShapeDtypeStruct((HEADS, 3 * HEAD, ROWS), BF16),
-            jax.ShapeDtypeStruct((HEADS, HEAD, ROWS), BF16),
+            jax.ShapeDtypeStruct((HEADS // 2, HEAD, ROWS), BF16),
+            jax.ShapeDtypeStruct((HEADS // 2, HEAD, ROWS), BF16),
         ),
         in_specs=[
             pl.BlockSpec(memory_space=pltpu.SMEM),
@@ -242,8 +298,14 @@
             pltpu.SMEM((PAIRS,), jnp.int32),
             pltpu.SMEM((PAIRS,), jnp.int32),
             pltpu.SMEM((PAIRS,), jnp.int32),
+            pltpu.VMEM((GROUP, BLOCK, BLOCK), F32),
+            pltpu.VMEM((GROUP, BLOCK, BLOCK), F32),
+            pltpu.VMEM((GROUP, BLOCK, BLOCK), BF16),
+            pltpu.VMEM((GROUP, BLOCK, BLOCK), BF16),
+            pltpu.VMEM((GROUP, PAD, BLOCK), BF16),
+            pltpu.VMEM((GROUP, PAD, BLOCK), BF16),
         ],
-        compiler_params=pltpu.CompilerParams(vmem_limit_bytes=VMEM_LIMIT),
+        compiler_params=pltpu.CompilerParams(vmem_limit_bytes=VMEM_MORE),
         cost_estimate=pl.CostEstimate(flops=10**10, bytes_accessed=0, transcendentals=0),
         name="attend",
     )(me, extents, received)
@@ -260,7 +322,7 @@
     return pl.pallas_call(
         unpack_body,
         out_shape=(shape, shape, shape),
-        compiler_params=pltpu.CompilerParams(vmem_limit_bytes=VMEM_LIMIT),
+        compiler_params=pltpu.CompilerParams(vmem_limit_bytes=VMEM_SOME),
         cost_estimate=pl.CostEstimate(flops=10**11, bytes_accessed=0, transcendentals=0),
         name="unpack",
     )(returned)
@@ -285,14 +347,19 @@
         copies[i].wait()
         copies[i + 1].wait()
         total = total + dot(left, grads[i * ROWS : (i + 2) * ROWS], NN)
+    empty = jnp.zeros((STRIP, ROWS - 3 * REST), F32)
     for tile in range(8):
-        out_ref[tile_ref[tile]] = total[:, tile * 144 : (tile + 1) * 144].astype(BF16)
+        for head in range(2):
+            part = total[head * HEAD : (head + 1) * HEAD, tile * TILE : (tile + 1) * TILE]
+            rest = [part[i * STRIP : (i + 1) * STRIP, ROWS:] for i in range(3)]
+            rest = jnp.concatenate(rest + [empty], axis=1)
+            out_ref[tile_ref[tile], head] = jnp.concatenate([part[:, :ROWS], rest], axis=0).astype(BF16)
 
 
 def weight_terms(places, mine, got, grads):
     return pl.pallas_call(
         weight_body,
-        out_shape=jax.ShapeDtypeStruct((8, 2 * HEAD, 144), BF16),
+        out_shape=jax.ShapeDtypeStruct((8, 2, HEAD + STRIP, ROWS), BF16),
         in_specs=[pl.BlockSpec(memory_space=pltpu.SMEM)]
         + [pl.BlockSpec(memory_space=pltpu.VMEM)] * 2
         + [pl.BlockSpec(memory_space=pl.ANY)] * 8,
@@ -301,10 +368,27 @@
             pltpu.VMEM((8 * ROWS, HEADS * HEAD), BF16),
             pltpu.SemaphoreType.DMA((8,)),
         ],
-        compiler_params=pltpu.CompilerParams(vmem_limit_bytes=VMEM_LIMIT),
+        compiler_params=pltpu.CompilerParams(vmem_limit_bytes=VMEM_SOME),
         cost_estimate=pl.CostEstimate(flops=10**9, bytes_accessed=0, transcendentals=0),
         name="weight_terms",
     )(places, mine, got, *grads)
+
+
+def finish_body(own_ref, *refs):
+    total = own_ref[...]
+    for ref in refs[:-1]:
+        total = total + ref[...].astype(F32)
+    rest = [total[HEAD:, i * REST : (i + 1) * REST] for i in range(3)]
+    refs[-1][...] = jnp.concatenate([total[:HEAD], jnp.concatenate(rest, axis=0)], axis=1)
+
+
+def finish(own, others):
+    return pl.pallas_call(
+        finish_body,
+        out_shape=jax.ShapeDtypeStruct((HEAD, TILE), F32),
+        compiler_params=pltpu.CompilerParams(vmem_limit_bytes=VMEM_SOME),
+        name="finish",
+    )(own, *others)
 
 
 def swap(x, axis, size, apart):
@@ -319,27 +403,27 @@
     received = lax.all_to_all(sent, "seq", 0, 0, tiled=True)
     late, received = lax.optimization_barrier((out_grad, received))
     far = [out_grad] + [swap(late, "seq", HEADS, apart) for apart in (2, 8, 10)]
+    grads, mine, give = attend(me[None].astype(jnp.int32), extents, received)
+    got = swap(give, "seq", HEADS, 4)
+    _, *far = lax.optimization_barrier((give, *far))
     near = [swap(x, "seq", HEADS, 1) for x in far]
     out_grads = [x for pair in zip(far, near) for x in pair]
-
-    grads, attended = attend(me[None].astype(jnp.int32), extents, received)
-    got = swap(attended[8:], "seq", HEADS, 4)
     returned = lax.all_to_all(grads, "seq", 0, 0, tiled=True)
 
     x_lo, y = part // 4, part % 4
     tile = jnp.arange(8, dtype=jnp.int32)
     places = ((tile // 4) ^ x_lo) + 2 * ((tile % 4) ^ y)
-    terms = weight_terms(places.astype(jnp.int32), attended[:8], got, out_grads)
+    terms = weight_terms(places.astype(jnp.int32), mine, got, out_grads)
     total = terms[:2].astype(F32)
     for apart in (1, 2, 3):
         total = total + swap(terms[2 * apart : 2 * apart + 2], "dp", 8, apart).astype(F32)
-    weight_grad = total[0, :HEAD]
+    last = []
     for x_apart, z_apart in ((1, 0), (0, 1), (1, 1)):
-        give = total[x_apart, z_apart * HEAD : (z_apart + 1) * HEAD].astype(BF16)
         pairs = [(i, i ^ (64 * x_apart + 4 * z_apart)) for i in range(128)]
-        weight_grad = weight_grad + lax.ppermute(give, ("dp", "seq"), pairs).astype(F32)
-
+        last.append(lax.ppermute(total[x_apart, z_apart].astype(BF16), ("dp", "seq"), pairs))
     query_grad, key_grad, value_grad = unpack(returned)
+    value_grad, *last = lax.optimization_barrier((value_grad, *last))
+    weight_grad = finish(total[0, 0], last)
     return query_grad, key_grad, value_grad, weight_grad
 
 

time: 80.5 us -> 78.5 us (0.975); the launches traced: 79.4 us -> 78.6 us
  waiting for transfers between devices: 31.3 us -> 28.4 us
  Pallas kernels: 16.5 us -> 19.2 us
  local copies, waits for them, and re-layouts: 0.74 us -> 1.61 us
    ppermute x11, waiting for transfers between devices: 9.53 us -> 6.49 us  [swap(): return lax.ppermute(x, axis, [(i, i ^ apart) for i in range(size)])]
    unnamed x4 -> x8, local copies, waits for them, and re-layouts: 0.01 us -> 1.58 us
    pallas_call x1, Pallas kernels: 9.14 us -> 10.5 us  [attend(): pl.pallas_call(attend_body, out_shape=(jax.ShapeDtypeStruct((HEADS, 3 * H...]
    pallas_call x2 -> x3, Pallas kernels: 6.26 us -> 7.57 us  [the longest x1 4.13 us: pack(): pl.pallas_call(pack_body, out_shape=jax.ShapeDtypeStruct(shape, BF16), in...]
    ppermute x11, starting transfers between devices: 12.8 us -> 12 us  [swap(): return lax.ppermute(x, axis, [(i, i ^ apart) for i in range(size)])]
  transfers between devices with their start and end apart: 16 -> 16, of which waited for: 9 -> 8; matrix products, arithmetic and copies ran while one was open for 2% -> 0% of each run, Pallas kernels for 14% -> 18%
where the time goes in v3:
time: 78.5 us; the launch traced here: 78.6 us
  starting transfers between devices  28.6 us (36%)
  waiting for transfers between devices  28.4 us (36%)
  Pallas kernels  19.2 us (24%)
  local copies, waits for them, and re-layouts  1.61 us (2%)
    all_to_all x1, waiting for transfers between devices, local(): received = lax.all_to_all(sent, 'seq', 0, 0, tiled=True)  19.5 us
    ppermute x11, starting transfers between devices, swap(): return lax.ppermute(x, axis, [(i, i ^ apart) for i in range(size)])  12 us
    pallas_call x1, Pallas kernels, attend(): pl.pallas_call(attend_body, out_shape=(jax.ShapeDtypeStruct((HEADS, 3 * H...  10.5 us
    all_to_all x1, starting transfers between devices, local(): received = lax.all_to_all(sent, 'seq', 0, 0, tiled=True)  8.1 us
    ppermute x11, waiting for transfers between devices, swap(): return lax.ppermute(x, axis, [(i, i ^ apart) for i in range(size)])  6.49 us
    all_to_all x1, starting transfers between devices, local(): returned = lax.all_to_all(grads, 'seq', 0, 0, tiled=True)  4.95 us
    pallas_call x1, Pallas kernels, pack(): pl.pallas_call(pack_body, out_shape=jax.ShapeDtypeStruct(shape, BF16), in...  4.13 us
    ppermute x3, starting transfers between devices, local(): lax.ppermute(total[x_apart, z_apart].astype(BF16), ('dp', 'seq'), pairs)  3.57 us
  transfers between devices with their start and end apart: 16, of which 8 were waited for; matrix products, arithmetic and copies ran while one was open for 0% of the time, Pallas kernels for 18%

profile of v3, /device:TPU:0, one launch (start us, length us, event | category | flops | bytes accessed | tf_op | source)
XLA Modules:
  0.0 78.6 jit_solution(17723455385634356304)
XLA Ops:
  0.6 4.1 %pack.1 = bf16[16,288,128]{2,1,0:T(8,128)(2,1)} custom-call(bf16[128,1152]{1,0:T(8,128)(2,1)} %q_hbm.1, bf16[128,1152]{1,0:T(8,128)(2,1)} %k_hbm.1, bf16[128,1152]{1,0:T(8,128)(2,1)} %v_hbm.1, bf16[128,1152]{1,0:T(8,128)(2,1)} %refs_0_, bf16[1152,1152]{1,0:T(8,128)(2,1)} %w_hbm.1), custom_call_target="tpu_custom_call" | custom-call | flops 10000000000 | tf_op jit(solution)/shard_map/pack/pallas_call | solution.py:79
  4.8 0.0 copy-start
  4.8 0.0 copy-start.1
  4.8 8.1 %all-to-all-start = ((bf16[16,288,128]{2,1,0:T(8,128)(2,1)}), bf16[16,288,128]{2,1,0:T(8,128)(2,1)S(1)}, u32[]{:S(2)}, u32[]{:S(2)}) async-start(bf16[16,288,128]{2,1,0:T(8,128)(2,1)} %pack.1), calls=%async_computation | async-start | bytes 2359296 | tf_op jit(solution)/shard_map/all_to_all | solution.py:403
  12.9 19.5 %all-to-all-done.r_ref = bf16[16,288,128]{2,1,0:T(8,128)(2,1)S(1)} async-done(((bf16[16,288,128]{2,1,0:T(8,128)(2,1)}), bf16[16,288,128]{2,1,0:T(8,128)(2,1)S(1)}, u32[]{:S(2)}, u32[]{:S(2)}) %all-to-all-start) | async-done | bytes 1179680 | tf_op jit(solution)/shard_map/all_to_all | solution.py:403
  32.4 0.0 copy-done
  32.4 0.9 %collective-permute-start.3 = (bf16[128,1152]{1,0:T(8,128)(2,1)S(1)}, bf16[128,1152]{1,0:T(8,128)(2,1)S(1)}, u32[]{:S(2)}, u32[]{:S(2)}) collective-permute-start(bf16[128,1152]{1,0:T(8,128)(2,1)S(1)} %copy-done), channel_id=1, source_target_pairs={{0,10},{1,11},{2,8},{3,9},{4,14},{5,15},{6,12},{7,13},{8,2},{9,3},... | collective-permute-start | bytes 884744 | tf_op jit(solution)/shard_map/ppermute | solution.py:395
  33.3 2.7 %collective-permute-start.2 = (bf16[128,1152]{1,0:T(8,128)(2,1)S(1)}, bf16[128,1152]{1,0:T(8,128)(2,1)S(1)}, u32[]{:S(2)}, u32[]{:S(2)}) collective-permute-start(bf16[128,1152]{1,0:T(8,128)(2,1)S(1)} %copy-done), channel_id=1, source_target_pairs={{0,8},{1,9},{2,10},{3,11},{4,12},{5,13},{6,14},{7,15},{8,0},{9,1},... | collective-permute-start | bytes 884744 | tf_op jit(solution)/shard_map/ppermute | solution.py:395
  36.1 2.8 %collective-permute-start.1 = (bf16[128,1152]{1,0:T(8,128)(2,1)S(1)}, bf16[128,1152]{1,0:T(8,128)(2,1)S(1)}, u32[]{:S(2)}, u32[]{:S(2)}) collective-permute-start(bf16[128,1152]{1,0:T(8,128)(2,1)S(1)} %copy-done), channel_id=1, source_target_pairs={{0,2},{1,3},{2,0},{3,1},{4,6},{5,7},{6,4},{7,5},{8,10},{9,11},{10,... | collective-permute-start | bytes 884744 | tf_op jit(solution)/shard_map/ppermute | solution.py:395
  38.9 0.0 copy-done.1
  38.9 10.5 %attend.1 = (bf16[16,216,128]{2,1,0:T(8,128)(2,1)}, bf16[8,72,128]{2,1,0:T(8,128)(2,1)S(1)}, bf16[8,72,128]{2,1,0:T(8,128)(2,1)S(1)}) custom-call(s32[1]{0:T(128)} %bitcast.me_ref, s32[1,8]{1,0:T(1,128)S(1)} %copy-done.1, bf16[16,288,128]{2,1,0:T(8,128)(2,1)S(1)} %all-to-all-done.r_ref), custom_call_target="tpu_custom_call" | custom-call | flops 10000000000 | tf_op jit(solution)/shard_map/attend/pallas_call | solution.py:269
  49.4 0.0 copy-start.2
  49.4 0.7 copy-done.2
  50.0 0.0 collective-permute-done.3.refs_6_
  50.0 0.0 collective-permute-done.2.refs_4_
  50.1 0.0 collective-permute-done.1.refs_2_
  50.1 0.1 collective-permute-start.4
  50.1 0.5 collective-permute-start.5
  50.6 0.1 collective-permute-start.6
  50.7 0.4 collective-permute-start.7
  51.2 0.0 collective-permute-start
  51.2 5.0 %all-to-all-start.1 = ((bf16[16,216,128]{2,1,0:T(8,128)(2,1)}), bf16[16,216,128]{2,1,0:T(8,128)(2,1)S(1)}, u32[]{:S(2)}, u32[]{:S(2)}) async-start(bf16[16,216,128]{2,1,0:T(8,128)(2,1)} %get-tuple-element.21), calls=%async_computation.1 | async-start | bytes 1769472 | tf_op jit(solution)/shard_map/all_to_all | solution.py:411
  56.1 0.9 %collective-permute-done.got_ref = bf16[8,72,128]{2,1,0:T(8,128)(2,1)S(1)} collective-permute-done((bf16[8,72,128]{2,1,0:T(8,128)(2,1)S(1)}, bf16[8,72,128]{2,1,0:T(8,128)(2,1)S(1)}, u32[]{:S(2)}, u32[]{:S(2)}) %collective-permute-start) | collective-permute-done | bytes 147488 | tf_op jit(solution)/shard_map/ppermute | solution.py:395
  57.0 0.0 collective-permute-done.4.refs_1_
  57.0 0.0 collective-permute-done.5.refs_3_
  57.0 0.0 collective-permute-done.6.refs_5_
  57.0 0.0 collective-permute-done.7.refs_7_
  57.0 0.0 copy-start.3
  57.0 0.9 %copy-done.3 = bf16[8,72,128]{2,1,0:T(8,128)(2,1)S(1)} copy-done((bf16[8,72,128]{2,1,0:T(8,128)(2,1)S(1)}, bf16[8,72,128]{2,1,0:T(8,128)(2,1)}, u32[]{:S(2)}) %copy-start.3) | copy-done | bytes 147480
  57.9 2.7 %weight_terms.1 = bf16[8,2,96,128]{3,2,1,0:T(8,128)(2,1)S(1)} custom-call(s32[8]{0:T(128)S(1)} %fusion.2.tile_ref, bf16[8,72,128]{2,1,0:T(8,128)(2,1)S(1)} %copy-done.3, bf16[8,72,128]{2,1,0:T(8,128)(2,1)S(1)} %collective-permute-done.got_ref, bf16[128,1152]{1,0:T(8,128)(2,1)S(1)} %copy-done, bf16[128,1152]{1,0:T(8,128)(2,1)S(1)} %collective-permute-done.4.refs_1_, ...), custom_call_target="tpu_custom_call" | custom-call | flops 1000000000 | tf_op jit(solution)/shard_map/weight_terms/pallas_call | solution.py:360
  60.7 1.7 %collective-permute-start.8 = (bf16[2,2,96,128]{3,2,1,0:T(8,128)(2,1)S(1)}, bf16[2,2,96,128]{3,2,1,0:T(8,128)(2,1)S(1)}, u32[]{:S(2)}, u32[]{:S(2)}) collective-permute-start(bf16[2,2,96,128]{3,2,1,0:T(8,128)(2,1)S(1)} %get-tuple-element.38), channel_id=1, source_target_pairs={{0,16},{16,0},{32,48},{48,32},{64,80},{80,64},{96,112},{112,96},{1... | collective-permute-start | bytes 294920 | tf_op jit(solution)/shard_map/ppermute | solution.py:395
  62.4 2.2 %collective-permute-start.10 = (bf16[2,2,96,128]{3,2,1,0:T(8,128)(2,1)S(1)}, bf16[2,2,96,128]{3,2,1,0:T(8,128)(2,1)S(1)}, u32[]{:S(2)}, u32[]{:S(2)}) collective-permute-start(bf16[2,2,96,128]{3,2,1,0:T(8,128)(2,1)S(1)} %get-tuple-element.39), channel_id=1, source_target_pairs={{0,48},{16,32},{32,16},{48,0},{64,112},{80,96},{96,80},{112,64},{1... | collective-permute-start | bytes 294920 | tf_op jit(solution)/shard_map/ppermute | solution.py:395
  64.6 0.6 collective-permute-start.9
  65.1 0.3 collective-permute-done.8
  65.4 3.8 %collective-permute-done.10 = bf16[2,2,96,128]{3,2,1,0:T(8,128)(2,1)S(1)} collective-permute-done((bf16[2,2,96,128]{3,2,1,0:T(8,128)(2,1)S(1)}, bf16[2,2,96,128]{3,2,1,0:T(8,128)(2,1)S(1)}, u32[]{:S(2)}, u32[]{:S(2)}) %collective-permute-start.10) | collective-permute-done | bytes 98336 | tf_op jit(solution)/shard_map/ppermute | solution.py:395
  69.2 1.4 %collective-permute-done.9 = bf16[2,2,96,128]{3,2,1,0:T(8,128)(2,1)S(1)} collective-permute-done((bf16[2,2,96,128]{3,2,1,0:T(8,128)(2,1)S(1)}, bf16[2,2,96,128]{3,2,1,0:T(8,128)(2,1)S(1)}, u32[]{:S(2)}, u32[]{:S(2)}) %collective-permute-start.9) | collective-permute-done | bytes 98336 | tf_op jit(solution)/shard_map/ppermute | solution.py:395
  70.7 0.1 fusion.4
  70.8 1.5 %collective-permute-start.13 = (bf16[96,128]{1,0:T(8,128)(2,1)S(1)}, bf16[96,128]{1,0:T(8,128)(2,1)S(1)}, u32[]{:S(2)}, u32[]{:S(2)}) collective-permute-start(bf16[96,128]{1,0:T(8,128)(2,1)S(1)} %get-tuple-element.41), channel_id=1, source_target_pairs={{0,68},{1,69},{2,70},{3,71},{4,64},{5,65},{6,66},{7,67},{8,76},{9,... | collective-permute-start | bytes 73736 | tf_op jit(solution)/shard_map/ppermute | solution.py:423
  72.3 1.7 %collective-permute-start.12 = (bf16[96,128]{1,0:T(8,128)(2,1)S(1)}, bf16[96,128]{1,0:T(8,128)(2,1)S(1)}, u32[]{:S(2)}, u32[]{:S(2)}) collective-permute-start(bf16[96,128]{1,0:T(8,128)(2,1)S(1)} %get-tuple-element.42), channel_id=1, source_target_pairs={{0,4},{1,5},{2,6},{3,7},{4,0},{5,1},{6,2},{7,3},{8,12},{9,13},{10,... | collective-permute-start | bytes 73736 | tf_op jit(solution)/shard_map/ppermute | solution.py:423
  74.0 0.3 collective-permute-start.11
  74.3 0.0 all-to-all-done.1.y_ref
  74.3 1.1 %unpack.1 = (bf16[128,1152]{1,0:T(8,128)(2,1)}, bf16[128,1152]{1,0:T(8,128)(2,1)}, bf16[128,1152]{1,0:T(8,128)(2,1)}) custom-call(bf16[16,216,128]{2,1,0:T(8,128)(2,1)S(1)} %all-to-all-done.1.y_ref), custom_call_target="tpu_custom_call" | custom-call | flops 99999997952 | tf_op jit(solution)/shard_map/unpack/pallas_call | solution.py:322
  75.4 0.1 collective-permute-done.13.refs_2_
  75.6 0.5 collective-permute-done.12.refs_1_
  76.1 1.7 %collective-permute-done.11.refs_0_ = bf16[96,128]{1,0:T(8,128)(2,1)S(1)} collective-permute-done((bf16[96,128]{1,0:T(8,128)(2,1)S(1)}, bf16[96,128]{1,0:T(8,128)(2,1)S(1)}, u32[]{:S(2)}, u32[]{:S(2)}) %collective-permute-start.11) | collective-permute-done | bytes 24608 | tf_op jit(solution)/shard_map/ppermute | solution.py:423
  77.8 0.7 finish.1
  (4 shorter events, 0.0 us)
Async XLA Ops:
  4.8 27.6 %copy-start = (bf16[128,1152]{1,0:T(8,128)(2,1)S(1)}, bf16[128,1152]{1,0:T(8,128)(2,1)}, u32[]{:S(2)}) copy-start(bf16[128,1152]{1,0:T(8,128)(2,1)} %refs_0_) | copy-start | bytes 884740
  4.8 34.1 %copy-start.1 = (s32[1,8]{1,0:T(1,128)S(1)}, s32[1,8]{1,0:T(1,128)}, u32[]{:S(2)}) copy-start(s32[1,8]{1,0:T(1,128)} %ext_ref.1) | copy-start | bytes 100
  4.8 27.6 %all-to-all-start = ((bf16[16,288,128]{2,1,0:T(8,128)(2,1)}), bf16[16,288,128]{2,1,0:T(8,128)(2,1)S(1)}, u32[]{:S(2)}, u32[]{:S(2)}) async-start(bf16[16,288,128]{2,1,0:T(8,128)(2,1)} %pack.1), calls=%async_computation | async-start | bytes 2359296 | tf_op jit(solution)/shard_map/all_to_all | solution.py:403
  32.4 17.7 %collective-permute-start.3 = (bf16[128,1152]{1,0:T(8,128)(2,1)S(1)}, bf16[128,1152]{1,0:T(8,128)(2,1)S(1)}, u32[]{:S(2)}, u32[]{:S(2)}) collective-permute-start(bf16[128,1152]{1,0:T(8,128)(2,1)S(1)} %copy-done), channel_id=1, source_target_pairs={{0,10},{1,11},{2,8},{3,9},{4,14},{5,15},{6,12},{7,13},{8,2},{9,3},... | collective-permute-start | bytes 884744 | tf_op jit(solution)/shard_map/ppermute | solution.py:395
  33.3 16.8 %collective-permute-start.2 = (bf16[128,1152]{1,0:T(8,128)(2,1)S(1)}, bf16[128,1152]{1,0:T(8,128)(2,1)S(1)}, u32[]{:S(2)}, u32[]{:S(2)}) collective-permute-start(bf16[128,1152]{1,0:T(8,128)(2,1)S(1)} %copy-done), channel_id=1, source_target_pairs={{0,8},{1,9},{2,10},{3,11},{4,12},{5,13},{6,14},{7,15},{8,0},{9,1},... | collective-permute-start | bytes 884744 | tf_op jit(solution)/shard_map/ppermute | solution.py:395
  36.1 14.0 %collective-permute-start.1 = (bf16[128,1152]{1,0:T(8,128)(2,1)S(1)}, bf16[128,1152]{1,0:T(8,128)(2,1)S(1)}, u32[]{:S(2)}, u32[]{:S(2)}) collective-permute-start(bf16[128,1152]{1,0:T(8,128)(2,1)S(1)} %copy-done), channel_id=1, source_target_pairs={{0,2},{1,3},{2,0},{3,1},{4,6},{5,7},{6,4},{7,5},{8,10},{9,11},{10,... | collective-permute-start | bytes 884744 | tf_op jit(solution)/shard_map/ppermute | solution.py:395
  49.4 0.7 copy-start.2
  50.1 6.9 %collective-permute-start.4 = (bf16[128,1152]{1,0:T(8,128)(2,1)S(1)}, bf16[128,1152]{1,0:T(8,128)(2,1)S(1)}, u32[]{:S(2)}, u32[]{:S(2)}) collective-permute-start(bf16[128,1152]{1,0:T(8,128)(2,1)S(1)} %copy-done), channel_id=1, source_target_pairs={{0,1},{1,0},{2,3},{3,2},{4,5},{5,4},{6,7},{7,6},{8,9},{9,8},{10,11... | collective-permute-start | bytes 884744 | tf_op jit(solution)/shard_map/ppermute | solution.py:395
  50.1 6.9 %collective-permute-start.5 = (bf16[128,1152]{1,0:T(8,128)(2,1)S(1)}, bf16[128,1152]{1,0:T(8,128)(2,1)S(1)}, u32[]{:S(2)}, u32[]{:S(2)}) collective-permute-start(bf16[128,1152]{1,0:T(8,128)(2,1)S(1)} %collective-permute-done.1.refs_2_), channel_id=1, source_target_pairs={{0,1},{1,0},{2,3},{3,2},{4,5},{5,4},{6,7},{7,6},{8,9},{9,8},{10,11... | collective-permute-start | bytes 884744 | tf_op jit(solution)/shard_map/ppermute | solution.py:395
  50.6 6.4 %collective-permute-start.6 = (bf16[128,1152]{1,0:T(8,128)(2,1)S(1)}, bf16[128,1152]{1,0:T(8,128)(2,1)S(1)}, u32[]{:S(2)}, u32[]{:S(2)}) collective-permute-start(bf16[128,1152]{1,0:T(8,128)(2,1)S(1)} %collective-permute-done.2.refs_4_), channel_id=1, source_target_pairs={{0,1},{1,0},{2,3},{3,2},{4,5},{5,4},{6,7},{7,6},{8,9},{9,8},{10,11... | collective-permute-start | bytes 884744 | tf_op jit(solution)/shard_map/ppermute | solution.py:395
  50.7 6.3 %collective-permute-start.7 = (bf16[128,1152]{1,0:T(8,128)(2,1)S(1)}, bf16[128,1152]{1,0:T(8,128)(2,1)S(1)}, u32[]{:S(2)}, u32[]{:S(2)}) collective-permute-start(bf16[128,1152]{1,0:T(8,128)(2,1)S(1)} %collective-permute-done.3.refs_6_), channel_id=1, source_target_pairs={{0,1},{1,0},{2,3},{3,2},{4,5},{5,4},{6,7},{7,6},{8,9},{9,8},{10,11... | collective-permute-start | bytes 884744 | tf_op jit(solution)/shard_map/ppermute | solution.py:395
  51.2 5.8 %collective-permute-start = (bf16[8,72,128]{2,1,0:T(8,128)(2,1)S(1)}, bf16[8,72,128]{2,1,0:T(8,128)(2,1)S(1)}, u32[]{:S(2)}, u32[]{:S(2)}) collective-permute-start(bf16[8,72,128]{2,1,0:T(8,128)(2,1)S(1)} %get-tuple-element.26), channel_id=1, source_target_pairs={{0,4},{1,5},{2,6},{3,7},{4,0},{5,1},{6,2},{7,3},{8,12},{9,13},{10,... | collective-permute-start | bytes 442376 | tf_op jit(solution)/shard_map/ppermute | solution.py:395
  51.2 23.2 %all-to-all-start.1 = ((bf16[16,216,128]{2,1,0:T(8,128)(2,1)}), bf16[16,216,128]{2,1,0:T(8,128)(2,1)S(1)}, u32[]{:S(2)}, u32[]{:S(2)}) async-start(bf16[16,216,128]{2,1,0:T(8,128)(2,1)} %get-tuple-element.21), calls=%async_computation.1 | async-start | bytes 1769472 | tf_op jit(solution)/shard_map/all_to_all | solution.py:411
  57.0 0.9 %copy-start.3 = (bf16[8,72,128]{2,1,0:T(8,128)(2,1)S(1)}, bf16[8,72,128]{2,1,0:T(8,128)(2,1)}, u32[]{:S(2)}) copy-start(bf16[8,72,128]{2,1,0:T(8,128)(2,1)} %copy-done.2) | copy-start | bytes 442372
  60.7 4.7 %collective-permute-start.8 = (bf16[2,2,96,128]{3,2,1,0:T(8,128)(2,1)S(1)}, bf16[2,2,96,128]{3,2,1,0:T(8,128)(2,1)S(1)}, u32[]{:S(2)}, u32[]{:S(2)}) collective-permute-start(bf16[2,2,96,128]{3,2,1,0:T(8,128)(2,1)S(1)} %get-tuple-element.38), channel_id=1, source_target_pairs={{0,16},{16,0},{32,48},{48,32},{64,80},{80,64},{96,112},{112,96},{1... | collective-permute-start | bytes 294920 | tf_op jit(solution)/shard_map/ppermute | solution.py:395
  62.4 6.9 %collective-permute-start.10 = (bf16[2,2,96,128]{3,2,1,0:T(8,128)(2,1)S(1)}, bf16[2,2,96,128]{3,2,1,0:T(8,128)(2,1)S(1)}, u32[]{:S(2)}, u32[]{:S(2)}) collective-permute-start(bf16[2,2,96,128]{3,2,1,0:T(8,128)(2,1)S(1)} %get-tuple-element.39), channel_id=1, source_target_pairs={{0,48},{16,32},{32,16},{48,0},{64,112},{80,96},{96,80},{112,64},{1... | collective-permute-start | bytes 294920 | tf_op jit(solution)/shard_map/ppermute | solution.py:395
  64.6 6.1 %collective-permute-start.9 = (bf16[2,2,96,128]{3,2,1,0:T(8,128)(2,1)S(1)}, bf16[2,2,96,128]{3,2,1,0:T(8,128)(2,1)S(1)}, u32[]{:S(2)}, u32[]{:S(2)}) collective-permute-start(bf16[2,2,96,128]{3,2,1,0:T(8,128)(2,1)S(1)} %get-tuple-element.40), channel_id=1, source_target_pairs={{0,32},{16,48},{32,0},{48,16},{64,96},{80,112},{96,64},{112,80},{1... | collective-permute-start | bytes 294920 | tf_op jit(solution)/shard_map/ppermute | solution.py:395
  70.8 4.8 %collective-permute-start.13 = (bf16[96,128]{1,0:T(8,128)(2,1)S(1)}, bf16[96,128]{1,0:T(8,128)(2,1)S(1)}, u32[]{:S(2)}, u32[]{:S(2)}) collective-permute-start(bf16[96,128]{1,0:T(8,128)(2,1)S(1)} %get-tuple-element.41), channel_id=1, source_target_pairs={{0,68},{1,69},{2,70},{3,71},{4,64},{5,65},{6,66},{7,67},{8,76},{9,... | collective-permute-start | bytes 73736 | tf_op jit(solution)/shard_map/ppermute | solution.py:423
  72.3 3.8 %collective-permute-start.12 = (bf16[96,128]{1,0:T(8,128)(2,1)S(1)}, bf16[96,128]{1,0:T(8,128)(2,1)S(1)}, u32[]{:S(2)}, u32[]{:S(2)}) collective-permute-start(bf16[96,128]{1,0:T(8,128)(2,1)S(1)} %get-tuple-element.42), channel_id=1, source_target_pairs={{0,4},{1,5},{2,6},{3,7},{4,0},{5,1},{6,2},{7,3},{8,12},{9,13},{10,... | collective-permute-start | bytes 73736 | tf_op jit(solution)/shard_map/ppermute | solution.py:423
  74.0 3.8 %collective-permute-start.11 = (bf16[96,128]{1,0:T(8,128)(2,1)S(1)}, bf16[96,128]{1,0:T(8,128)(2,1)S(1)}, u32[]{:S(2)}, u32[]{:S(2)}) collective-permute-start(bf16[96,128]{1,0:T(8,128)(2,1)S(1)} %get-tuple-element.43), channel_id=1, source_target_pairs={{0,64},{1,65},{2,66},{3,67},{4,68},{5,69},{6,70},{7,71},{8,72},{9,... | collective-permute-start | bytes 73736 | tf_op jit(solution)/shard_map/ppermute | solution.py:423

commit v4 on v3

--- a/solution.py
+++ b/solution.py
@@ -99,9 +99,9 @@
 
 
 def attend_body(
-    me_ref, ext_ref, r_ref, g_ref, mine_ref, give_ref, q_s, b_s, k_s, v_s, kn_s, vn_s, e_s, acc_s, dq_s, dk_s, dv_s,
+    me_ref, ext_ref, r_ref, g_ref, mine_hbm, give_ref, q_s, b_s, k_s, v_s, kn_s, vn_s, e_s, acc_s, dq_s, dk_s, dv_s,
     top_s, pair_top_s, delta_s, inverse_s, qb_s, kb_s, later_q_s, later_k_s,
-    even_s, odd_s, ds_even_s, ds_odd_s, back_even_s, back_odd_s
+    even_s, odd_s, ds_even_s, ds_odd_s, back_even_s, back_odd_s, mine_ref, mine_sem
 ):
     ends = []
     total = jnp.int32(0)
@@ -217,6 +217,9 @@
         delta_s[qb] = jnp.sum(back[:HEAD] * attended.astype(F32), axis=0, keepdims=True)
         inverse_s[qb] = inverse
 
+    keep = pltpu.make_async_copy(mine_ref, mine_hbm, mine_sem)
+    keep.start()
+
     def differ(at, ds_ref, back_ref, u):
         qb = qb_s[at]
         factor = jnp.exp2((pair_top_s[at] - top_s[qb]) * (SCALE * LOG2E)) * inverse_s[qb]
@@ -263,6 +266,7 @@
             ],
             axis=0,
         ).astype(BF16)
+    keep.wait()
 
 
 def attend(me, extents, received):
@@ -278,6 +282,11 @@
             pl.BlockSpec(memory_space=pltpu.SMEM),
             pl.BlockSpec(memory_space=pltpu.VMEM),
         ],
+        out_specs=(
+            pl.BlockSpec(memory_space=pltpu.VMEM),
+            pl.BlockSpec(memory_space=pltpu.HBM),
+            pl.BlockSpec(memory_space=pltpu.VMEM),
+        ),
         scratch_shapes=[
             pltpu.VMEM((BLOCKS + 1, 128, BLOCK), BF16),
             pltpu.VMEM((BLOCKS + 1, PAD, BLOCK), BF16),
@@ -304,6 +313,8 @@
             pltpu.VMEM((GROUP, BLOCK, BLOCK), BF16),
             pltpu.VMEM((GROUP, PAD, BLOCK), BF16),
             pltpu.VMEM((GROUP, PAD, BLOCK), BF16),
+            pltpu.VMEM((HEADS // 2, HEAD, ROWS), BF16),
+            pltpu.SemaphoreType.DMA,
         ],
         compiler_params=pltpu.CompilerParams(vmem_limit_bytes=VMEM_MORE),
         cost_estimate=pl.CostEstimate(flops=10**10, bytes_accessed=0, transcendentals=0),
@@ -329,24 +340,12 @@
 
 
 def weight_body(tile_ref, mine_ref, got_ref, *refs):
-    sources, out_ref, grads, sems = refs[:8], refs[8], refs[9], refs[10]
-    copies = [
-        pltpu.make_async_copy(source, grads.at[pl.ds(i * ROWS, ROWS)], sems.at[i])
-        for i, source in enumerate(sources)
-    ]
-    for copy in copies:
-        copy.start()
+    grads, out_ref = refs[:8], refs[8]
     total = jnp.zeros((2 * HEAD, HEADS * HEAD), F32)
     for i in range(0, 8, 2):
-        left = jnp.concatenate(
-            [
-                jnp.concatenate([mine_ref[j], got_ref[j]], axis=0) for j in (i, i + 1)
-            ],
-            axis=1,
-        )
-        copies[i].wait()
-        copies[i + 1].wait()
-        total = total + dot(left, grads[i * ROWS : (i + 2) * ROWS], NN)
+        left = [jnp.concatenate([mine_ref[j], got_ref[j]], axis=0) for j in (i, i + 1)]
+        right = jnp.concatenate([grads[i][...], grads[i + 1][...]], axis=0)
+        total = total + dot(jnp.concatenate(left, axis=1), right, NN)
     empty = jnp.zeros((STRIP, ROWS - 3 * REST), F32)
     for tile in range(8):
         for head in range(2):
@@ -361,13 +360,8 @@
         weight_body,
         out_shape=jax.ShapeDtypeStruct((8, 2, HEAD + STRIP, ROWS), BF16),
         in_specs=[pl.BlockSpec(memory_space=pltpu.SMEM)]
-        + [pl.BlockSpec(memory_space=pltpu.VMEM)] * 2
-        + [pl.BlockSpec(memory_space=pl.ANY)] * 8,
+        + [pl.BlockSpec(memory_space=pltpu.VMEM)] * 10,
         out_specs=pl.BlockSpec(memory_space=pltpu.VMEM),
-        scratch_shapes=[
-            pltpu.VMEM((8 * ROWS, HEADS * HEAD), BF16),
-            pltpu.SemaphoreType.DMA((8,)),
-        ],
         compiler_params=pltpu.CompilerParams(vmem_limit_bytes=VMEM_SOME),
         cost_estimate=pl.CostEstimate(flops=10**9, bytes_accessed=0, transcendentals=0),
         name="weight_terms",

time: 78.5 us -> 77 us (0.981)
  Pallas kernels: 19.2 us -> 16.6 us
    pallas_call x1, Pallas kernels: 10.5 us -> 8.85 us  [attend(): pl.pallas_call(attend_body, out_shape=(jax.ShapeDtypeStruct((HEADS, 3 * H...]
    ppermute x11, waiting for transfers between devices: 6.49 us -> 7.57 us  [swap(): return lax.ppermute(x, axis, [(i, i ^ apart) for i in range(size)])]
    pallas_call x1, Pallas kernels: 2.73 us -> 1.82 us  [weight_terms(): pl.pallas_call(weight_body, out_shape=jax.ShapeDtypeStruct((8, 2, HEAD +...]
  transfers between devices with their start and end apart: 16 -> 16, of which waited for: 8 -> 8; matrix products, arithmetic and copies ran while one was open for 0% -> 0% of each run, Pallas kernels for 18% -> 15%
where the time goes in v4:
time: 77 us; the launch traced here: 76.7 us
  starting transfers between devices  29 us (38%)
  waiting for transfers between devices  28.7 us (37%)
  Pallas kernels  16.6 us (22%)
  local copies, waits for them, and re-layouts  1.61 us (2%)
    all_to_all x1, waiting for transfers between devices, local(): received = lax.all_to_all(sent, 'seq', 0, 0, tiled=True)  19.5 us
    ppermute x11, starting transfers between devices, swap(): return lax.ppermute(x, axis, [(i, i ^ apart) for i in range(size)])  12.4 us
    pallas_call x1, Pallas kernels, attend(): pl.pallas_call(attend_body, out_shape=(jax.ShapeDtypeStruct((HEADS, 3 * H...  8.85 us
    all_to_all x1, starting transfers between devices, local(): received = lax.all_to_all(sent, 'seq', 0, 0, tiled=True)  8.1 us
    ppermute x11, waiting for transfers between devices, swap(): return lax.ppermute(x, axis, [(i, i ^ apart) for i in range(size)])  7.57 us
    all_to_all x1, starting transfers between devices, local(): returned = lax.all_to_all(grads, 'seq', 0, 0, tiled=True)  4.96 us
    pallas_call x1, Pallas kernels, pack(): pl.pallas_call(pack_body, out_shape=jax.ShapeDtypeStruct(shape, BF16), in...  4.13 us
    ppermute x3, starting transfers between devices, local(): lax.ppermute(total[x_apart, z_apart].astype(BF16), ('dp', 'seq'), pairs)  3.57 us
  transfers between devices with their start and end apart: 16, of which 8 were waited for; matrix products, arithmetic and copies ran while one was open for 0% of the time, Pallas kernels for 15%

profile of v4, /device:TPU:0, one launch (start us, length us, event | category | flops | bytes accessed | tf_op | source)
XLA Modules:
  0.0 76.7 jit_solution(9196875201415491558)
XLA Ops:
  0.6 4.1 %pack.1 = bf16[16,288,128]{2,1,0:T(8,128)(2,1)} custom-call(bf16[128,1152]{1,0:T(8,128)(2,1)} %q_hbm.1, bf16[128,1152]{1,0:T(8,128)(2,1)} %k_hbm.1, bf16[128,1152]{1,0:T(8,128)(2,1)} %v_hbm.1, bf16[128,1152]{1,0:T(8,128)(2,1)} %refs_0_, bf16[1152,1152]{1,0:T(8,128)(2,1)} %w_hbm.1), custom_call_target="tpu_custom_call" | custom-call | flops 10000000000 | tf_op jit(solution)/shard_map/pack/pallas_call | solution.py:79
  4.8 0.0 copy-start
  4.8 0.0 copy-start.1
  4.8 8.1 %all-to-all-start = ((bf16[16,288,128]{2,1,0:T(8,128)(2,1)}), bf16[16,288,128]{2,1,0:T(8,128)(2,1)S(1)}, u32[]{:S(2)}, u32[]{:S(2)}) async-start(bf16[16,288,128]{2,1,0:T(8,128)(2,1)} %pack.1), calls=%async_computation | async-start | bytes 2359296 | tf_op jit(solution)/shard_map/all_to_all | solution.py:397
  12.9 19.5 %all-to-all-done.r_ref = bf16[16,288,128]{2,1,0:T(8,128)(2,1)S(1)} async-done(((bf16[16,288,128]{2,1,0:T(8,128)(2,1)}), bf16[16,288,128]{2,1,0:T(8,128)(2,1)S(1)}, u32[]{:S(2)}, u32[]{:S(2)}) %all-to-all-start) | async-done | bytes 1179680 | tf_op jit(solution)/shard_map/all_to_all | solution.py:397
  32.4 0.0 copy-done
  32.4 0.9 %collective-permute-start.3 = (bf16[128,1152]{1,0:T(8,128)(2,1)S(1)}, bf16[128,1152]{1,0:T(8,128)(2,1)S(1)}, u32[]{:S(2)}, u32[]{:S(2)}) collective-permute-start(bf16[128,1152]{1,0:T(8,128)(2,1)S(1)} %copy-done), channel_id=1, source_target_pairs={{0,10},{1,11},{2,8},{3,9},{4,14},{5,15},{6,12},{7,13},{8,2},{9,3},... | collective-permute-start | bytes 884744 | tf_op jit(solution)/shard_map/ppermute | solution.py:389
  33.3 2.7 %collective-permute-start.2 = (bf16[128,1152]{1,0:T(8,128)(2,1)S(1)}, bf16[128,1152]{1,0:T(8,128)(2,1)S(1)}, u32[]{:S(2)}, u32[]{:S(2)}) collective-permute-start(bf16[128,1152]{1,0:T(8,128)(2,1)S(1)} %copy-done), channel_id=1, source_target_pairs={{0,8},{1,9},{2,10},{3,11},{4,12},{5,13},{6,14},{7,15},{8,0},{9,1},... | collective-permute-start | bytes 884744 | tf_op jit(solution)/shard_map/ppermute | solution.py:389
  36.1 2.8 %collective-permute-start.1 = (bf16[128,1152]{1,0:T(8,128)(2,1)S(1)}, bf16[128,1152]{1,0:T(8,128)(2,1)S(1)}, u32[]{:S(2)}, u32[]{:S(2)}) collective-permute-start(bf16[128,1152]{1,0:T(8,128)(2,1)S(1)} %copy-done), channel_id=1, source_target_pairs={{0,2},{1,3},{2,0},{3,1},{4,6},{5,7},{6,4},{7,5},{8,10},{9,11},{10,... | collective-permute-start | bytes 884744 | tf_op jit(solution)/shard_map/ppermute | solution.py:389
  38.9 0.0 copy-done.1
  38.9 8.8 %attend.1 = (bf16[16,216,128]{2,1,0:T(8,128)(2,1)}, bf16[8,72,128]{2,1,0:T(8,128)(2,1)S(1)}, bf16[8,72,128]{2,1,0:T(8,128)(2,1)S(1)}) custom-call(s32[1]{0:T(128)} %bitcast.me_ref, s32[1,8]{1,0:T(1,128)S(1)} %copy-done.1, bf16[16,288,128]{2,1,0:T(8,128)(2,1)S(1)} %all-to-all-done.r_ref), custom_call_target="tpu_custom_call" | custom-call | flops 10000000000 | tf_op jit(solution)/shard_map/attend/pallas_call | solution.py:273
  47.7 0.0 copy-start.2
  47.7 0.7 copy-done.2
  48.4 0.0 collective-permute-done.3.refs_6_
  48.4 1.7 %collective-permute-done.2.refs_4_ = bf16[128,1152]{1,0:T(8,128)(2,1)S(1)} collective-permute-done((bf16[128,1152]{1,0:T(8,128)(2,1)S(1)}, bf16[128,1152]{1,0:T(8,128)(2,1)S(1)}, u32[]{:S(2)}, u32[]{:S(2)}) %collective-permute-start.2) | collective-permute-done | bytes 294944 | tf_op jit(solution)/shard_map/ppermute | solution.py:389
  50.1 0.0 collective-permute-done.1.refs_2_
  50.1 0.0 collective-permute-start.4
  50.1 0.5 collective-permute-start.5
  50.6 0.0 collective-permute-start.6
  50.6 0.5 collective-permute-start.7
  51.1 0.0 collective-permute-start
  51.2 5.0 %all-to-all-start.1 = ((bf16[16,216,128]{2,1,0:T(8,128)(2,1)}), bf16[16,216,128]{2,1,0:T(8,128)(2,1)S(1)}, u32[]{:S(2)}, u32[]{:S(2)}) async-start(bf16[16,216,128]{2,1,0:T(8,128)(2,1)} %get-tuple-element.21), calls=%async_computation.1 | async-start | bytes 1769472 | tf_op jit(solution)/shard_map/all_to_all | solution.py:405
  56.1 0.7 collective-permute-done.got_ref
  56.9 0.0 collective-permute-done.4.refs_1_
  56.9 0.0 collective-permute-done.5.refs_3_
  56.9 0.0 collective-permute-done.6.refs_5_
  56.9 0.0 collective-permute-done.7.refs_7_
  56.9 0.0 copy-start.3
  56.9 0.9 %copy-done.3 = bf16[8,72,128]{2,1,0:T(8,128)(2,1)S(1)} copy-done((bf16[8,72,128]{2,1,0:T(8,128)(2,1)S(1)}, bf16[8,72,128]{2,1,0:T(8,128)(2,1)}, u32[]{:S(2)}) %copy-start.3) | copy-done | bytes 147480
  57.8 1.8 %weight_terms.1 = bf16[8,2,96,128]{3,2,1,0:T(8,128)(2,1)S(1)} custom-call(s32[8]{0:T(128)S(1)} %fusion.2.tile_ref, bf16[8,72,128]{2,1,0:T(8,128)(2,1)S(1)} %copy-done.3, bf16[8,72,128]{2,1,0:T(8,128)(2,1)S(1)} %collective-permute-done.got_ref, bf16[128,1152]{1,0:T(8,128)(2,1)S(1)} %copy-done, bf16[128,1152]{1,0:T(8,128)(2,1)S(1)} %collective-permute-done.4.refs_1_, ...), custom_call_target="tpu_custom_call" | custom-call | flops 1000000000 | tf_op jit(solution)/shard_map/weight_terms/pallas_call | solution.py:359
  59.7 1.7 %collective-permute-start.8 = (bf16[2,2,96,128]{3,2,1,0:T(8,128)(2,1)S(1)}, bf16[2,2,96,128]{3,2,1,0:T(8,128)(2,1)S(1)}, u32[]{:S(2)}, u32[]{:S(2)}) collective-permute-start(bf16[2,2,96,128]{3,2,1,0:T(8,128)(2,1)S(1)} %get-tuple-element.38), channel_id=1, source_target_pairs={{0,16},{16,0},{32,48},{48,32},{64,80},{80,64},{96,112},{112,96},{1... | collective-permute-start | bytes 294920 | tf_op jit(solution)/shard_map/ppermute | solution.py:389
  61.3 2.2 %collective-permute-start.10 = (bf16[2,2,96,128]{3,2,1,0:T(8,128)(2,1)S(1)}, bf16[2,2,96,128]{3,2,1,0:T(8,128)(2,1)S(1)}, u32[]{:S(2)}, u32[]{:S(2)}) collective-permute-start(bf16[2,2,96,128]{3,2,1,0:T(8,128)(2,1)S(1)} %get-tuple-element.39), channel_id=1, source_target_pairs={{0,48},{16,32},{32,16},{48,0},{64,112},{80,96},{96,80},{112,64},{1... | collective-permute-start | bytes 294920 | tf_op jit(solution)/shard_map/ppermute | solution.py:389
  63.5 1.0 %collective-permute-start.9 = (bf16[2,2,96,128]{3,2,1,0:T(8,128)(2,1)S(1)}, bf16[2,2,96,128]{3,2,1,0:T(8,128)(2,1)S(1)}, u32[]{:S(2)}, u32[]{:S(2)}) collective-permute-start(bf16[2,2,96,128]{3,2,1,0:T(8,128)(2,1)S(1)} %get-tuple-element.40), channel_id=1, source_target_pairs={{0,32},{16,48},{32,0},{48,16},{64,96},{80,112},{96,64},{112,80},{1... | collective-permute-start | bytes 294920 | tf_op jit(solution)/shard_map/ppermute | solution.py:389
  64.5 0.0 collective-permute-done.8
  64.5 3.7 %collective-permute-done.10 = bf16[2,2,96,128]{3,2,1,0:T(8,128)(2,1)S(1)} collective-permute-done((bf16[2,2,96,128]{3,2,1,0:T(8,128)(2,1)S(1)}, bf16[2,2,96,128]{3,2,1,0:T(8,128)(2,1)S(1)}, u32[]{:S(2)}, u32[]{:S(2)}) %collective-permute-start.10) | collective-permute-done | bytes 98336 | tf_op jit(solution)/shard_map/ppermute | solution.py:389
  68.2 1.4 %collective-permute-done.9 = bf16[2,2,96,128]{3,2,1,0:T(8,128)(2,1)S(1)} collective-permute-done((bf16[2,2,96,128]{3,2,1,0:T(8,128)(2,1)S(1)}, bf16[2,2,96,128]{3,2,1,0:T(8,128)(2,1)S(1)}, u32[]{:S(2)}, u32[]{:S(2)}) %collective-permute-start.9) | collective-permute-done | bytes 98336 | tf_op jit(solution)/shard_map/ppermute | solution.py:389
  69.6 0.1 fusion.4
  69.7 1.3 %collective-permute-start.13 = (bf16[96,128]{1,0:T(8,128)(2,1)S(1)}, bf16[96,128]{1,0:T(8,128)(2,1)S(1)}, u32[]{:S(2)}, u32[]{:S(2)}) collective-permute-start(bf16[96,128]{1,0:T(8,128)(2,1)S(1)} %get-tuple-element.41), channel_id=1, source_target_pairs={{0,68},{1,69},{2,70},{3,71},{4,64},{5,65},{6,66},{7,67},{8,76},{9,... | collective-permute-start | bytes 73736 | tf_op jit(solution)/shard_map/ppermute | solution.py:417
  71.0 1.2 %collective-permute-start.12 = (bf16[96,128]{1,0:T(8,128)(2,1)S(1)}, bf16[96,128]{1,0:T(8,128)(2,1)S(1)}, u32[]{:S(2)}, u32[]{:S(2)}) collective-permute-start(bf16[96,128]{1,0:T(8,128)(2,1)S(1)} %get-tuple-element.42), channel_id=1, source_target_pairs={{0,4},{1,5},{2,6},{3,7},{4,0},{5,1},{6,2},{7,3},{8,12},{9,13},{10,... | collective-permute-start | bytes 73736 | tf_op jit(solution)/shard_map/ppermute | solution.py:417
  72.2 1.1 %collective-permute-start.11 = (bf16[96,128]{1,0:T(8,128)(2,1)S(1)}, bf16[96,128]{1,0:T(8,128)(2,1)S(1)}, u32[]{:S(2)}, u32[]{:S(2)}) collective-permute-start(bf16[96,128]{1,0:T(8,128)(2,1)S(1)} %get-tuple-element.43), channel_id=1, source_target_pairs={{0,64},{1,65},{2,66},{3,67},{4,68},{5,69},{6,70},{7,71},{8,72},{9,... | collective-permute-start | bytes 73736 | tf_op jit(solution)/shard_map/ppermute | solution.py:417
  73.3 0.0 all-to-all-done.1.y_ref
  73.3 1.1 %unpack.1 = (bf16[128,1152]{1,0:T(8,128)(2,1)}, bf16[128,1152]{1,0:T(8,128)(2,1)}, bf16[128,1152]{1,0:T(8,128)(2,1)}) custom-call(bf16[16,216,128]{2,1,0:T(8,128)(2,1)S(1)} %all-to-all-done.1.y_ref), custom_call_target="tpu_custom_call" | custom-call | flops 99999997952 | tf_op jit(solution)/shard_map/unpack/pallas_call | solution.py:333
  74.3 0.1 collective-permute-done.13.refs_2_
  74.5 0.4 collective-permute-done.12.refs_1_
  74.8 1.2 %collective-permute-done.11.refs_0_ = bf16[96,128]{1,0:T(8,128)(2,1)S(1)} collective-permute-done((bf16[96,128]{1,0:T(8,128)(2,1)S(1)}, bf16[96,128]{1,0:T(8,128)(2,1)S(1)}, u32[]{:S(2)}, u32[]{:S(2)}) %collective-permute-start.11) | collective-permute-done | bytes 24608 | tf_op jit(solution)/shard_map/ppermute | solution.py:417
  76.0 0.7 finish.1
  (4 shorter events, 0.0 us)
Async XLA Ops:
  4.8 27.6 %copy-start = (bf16[128,1152]{1,0:T(8,128)(2,1)S(1)}, bf16[128,1152]{1,0:T(8,128)(2,1)}, u32[]{:S(2)}) copy-start(bf16[128,1152]{1,0:T(8,128)(2,1)} %refs_0_) | copy-start | bytes 884740
  4.8 34.1 %copy-start.1 = (s32[1,8]{1,0:T(1,128)S(1)}, s32[1,8]{1,0:T(1,128)}, u32[]{:S(2)}) copy-start(s32[1,8]{1,0:T(1,128)} %ext_ref.1) | copy-start | bytes 100
  4.8 27.6 %all-to-all-start = ((bf16[16,288,128]{2,1,0:T(8,128)(2,1)}), bf16[16,288,128]{2,1,0:T(8,128)(2,1)S(1)}, u32[]{:S(2)}, u32[]{:S(2)}) async-start(bf16[16,288,128]{2,1,0:T(8,128)(2,1)} %pack.1), calls=%async_computation | async-start | bytes 2359296 | tf_op jit(solution)/shard_map/all_to_all | solution.py:397
  32.4 16.0 %collective-permute-start.3 = (bf16[128,1152]{1,0:T(8,128)(2,1)S(1)}, bf16[128,1152]{1,0:T(8,128)(2,1)S(1)}, u32[]{:S(2)}, u32[]{:S(2)}) collective-permute-start(bf16[128,1152]{1,0:T(8,128)(2,1)S(1)} %copy-done), channel_id=1, source_target_pairs={{0,10},{1,11},{2,8},{3,9},{4,14},{5,15},{6,12},{7,13},{8,2},{9,3},... | collective-permute-start | bytes 884744 | tf_op jit(solution)/shard_map/ppermute | solution.py:389
  33.3 16.8 %collective-permute-start.2 = (bf16[128,1152]{1,0:T(8,128)(2,1)S(1)}, bf16[128,1152]{1,0:T(8,128)(2,1)S(1)}, u32[]{:S(2)}, u32[]{:S(2)}) collective-permute-start(bf16[128,1152]{1,0:T(8,128)(2,1)S(1)} %copy-done), channel_id=1, source_target_pairs={{0,8},{1,9},{2,10},{3,11},{4,12},{5,13},{6,14},{7,15},{8,0},{9,1},... | collective-permute-start | bytes 884744 | tf_op jit(solution)/shard_map/ppermute | solution.py:389
  36.1 14.0 %collective-permute-start.1 = (bf16[128,1152]{1,0:T(8,128)(2,1)S(1)}, bf16[128,1152]{1,0:T(8,128)(2,1)S(1)}, u32[]{:S(2)}, u32[]{:S(2)}) collective-permute-start(bf16[128,1152]{1,0:T(8,128)(2,1)S(1)} %copy-done), channel_id=1, source_target_pairs={{0,2},{1,3},{2,0},{3,1},{4,6},{5,7},{6,4},{7,5},{8,10},{9,11},{10,... | collective-permute-start | bytes 884744 | tf_op jit(solution)/shard_map/ppermute | solution.py:389
  47.7 0.7 copy-start.2
  50.1 6.8 %collective-permute-start.4 = (bf16[128,1152]{1,0:T(8,128)(2,1)S(1)}, bf16[128,1152]{1,0:T(8,128)(2,1)S(1)}, u32[]{:S(2)}, u32[]{:S(2)}) collective-permute-start(bf16[128,1152]{1,0:T(8,128)(2,1)S(1)} %copy-done), channel_id=1, source_target_pairs={{0,1},{1,0},{2,3},{3,2},{4,5},{5,4},{6,7},{7,6},{8,9},{9,8},{10,11... | collective-permute-start | bytes 884744 | tf_op jit(solution)/shard_map/ppermute | solution.py:389
  50.1 6.8 %collective-permute-start.5 = (bf16[128,1152]{1,0:T(8,128)(2,1)S(1)}, bf16[128,1152]{1,0:T(8,128)(2,1)S(1)}, u32[]{:S(2)}, u32[]{:S(2)}) collective-permute-start(bf16[128,1152]{1,0:T(8,128)(2,1)S(1)} %collective-permute-done.1.refs_2_), channel_id=1, source_target_pairs={{0,1},{1,0},{2,3},{3,2},{4,5},{5,4},{6,7},{7,6},{8,9},{9,8},{10,11... | collective-permute-start | bytes 884744 | tf_op jit(solution)/shard_map/ppermute | solution.py:389
  50.6 6.3 %collective-permute-start.6 = (bf16[128,1152]{1,0:T(8,128)(2,1)S(1)}, bf16[128,1152]{1,0:T(8,128)(2,1)S(1)}, u32[]{:S(2)}, u32[]{:S(2)}) collective-permute-start(bf16[128,1152]{1,0:T(8,128)(2,1)S(1)} %collective-permute-done.2.refs_4_), channel_id=1, source_target_pairs={{0,1},{1,0},{2,3},{3,2},{4,5},{5,4},{6,7},{7,6},{8,9},{9,8},{10,11... | collective-permute-start | bytes 884744 | tf_op jit(solution)/shard_map/ppermute | solution.py:389
  50.6 6.3 %collective-permute-start.7 = (bf16[128,1152]{1,0:T(8,128)(2,1)S(1)}, bf16[128,1152]{1,0:T(8,128)(2,1)S(1)}, u32[]{:S(2)}, u32[]{:S(2)}) collective-permute-start(bf16[128,1152]{1,0:T(8,128)(2,1)S(1)} %collective-permute-done.3.refs_6_), channel_id=1, source_target_pairs={{0,1},{1,0},{2,3},{3,2},{4,5},{5,4},{6,7},{7,6},{8,9},{9,8},{10,11... | collective-permute-start | bytes 884744 | tf_op jit(solution)/shard_map/ppermute | solution.py:389
  51.1 5.8 %collective-permute-start = (bf16[8,72,128]{2,1,0:T(8,128)(2,1)S(1)}, bf16[8,72,128]{2,1,0:T(8,128)(2,1)S(1)}, u32[]{:S(2)}, u32[]{:S(2)}) collective-permute-start(bf16[8,72,128]{2,1,0:T(8,128)(2,1)S(1)} %get-tuple-element.26), channel_id=1, source_target_pairs={{0,4},{1,5},{2,6},{3,7},{4,0},{5,1},{6,2},{7,3},{8,12},{9,13},{10,... | collective-permute-start | bytes 442376 | tf_op jit(solution)/shard_map/ppermute | solution.py:389
  51.2 22.1 %all-to-all-start.1 = ((bf16[16,216,128]{2,1,0:T(8,128)(2,1)}), bf16[16,216,128]{2,1,0:T(8,128)(2,1)S(1)}, u32[]{:S(2)}, u32[]{:S(2)}) async-start(bf16[16,216,128]{2,1,0:T(8,128)(2,1)} %get-tuple-element.21), calls=%async_computation.1 | async-start | bytes 1769472 | tf_op jit(solution)/shard_map/all_to_all | solution.py:405
  56.9 0.9 %copy-start.3 = (bf16[8,72,128]{2,1,0:T(8,128)(2,1)S(1)}, bf16[8,72,128]{2,1,0:T(8,128)(2,1)}, u32[]{:S(2)}) copy-start(bf16[8,72,128]{2,1,0:T(8,128)(2,1)} %copy-done.2) | copy-start | bytes 442372
  59.7 4.8 %collective-permute-start.8 = (bf16[2,2,96,128]{3,2,1,0:T(8,128)(2,1)S(1)}, bf16[2,2,96,128]{3,2,1,0:T(8,128)(2,1)S(1)}, u32[]{:S(2)}, u32[]{:S(2)}) collective-permute-start(bf16[2,2,96,128]{3,2,1,0:T(8,128)(2,1)S(1)} %get-tuple-element.38), channel_id=1, source_target_pairs={{0,16},{16,0},{32,48},{48,32},{64,80},{80,64},{96,112},{112,96},{1... | collective-permute-start | bytes 294920 | tf_op jit(solution)/shard_map/ppermute | solution.py:389
  61.3 6.9 %collective-permute-start.10 = (bf16[2,2,96,128]{3,2,1,0:T(8,128)(2,1)S(1)}, bf16[2,2,96,128]{3,2,1,0:T(8,128)(2,1)S(1)}, u32[]{:S(2)}, u32[]{:S(2)}) collective-permute-start(bf16[2,2,96,128]{3,2,1,0:T(8,128)(2,1)S(1)} %get-tuple-element.39), channel_id=1, source_target_pairs={{0,48},{16,32},{32,16},{48,0},{64,112},{80,96},{96,80},{112,64},{1... | collective-permute-start | bytes 294920 | tf_op jit(solution)/shard_map/ppermute | solution.py:389
  63.5 6.1 %collective-permute-start.9 = (bf16[2,2,96,128]{3,2,1,0:T(8,128)(2,1)S(1)}, bf16[2,2,96,128]{3,2,1,0:T(8,128)(2,1)S(1)}, u32[]{:S(2)}, u32[]{:S(2)}) collective-permute-start(bf16[2,2,96,128]{3,2,1,0:T(8,128)(2,1)S(1)} %get-tuple-element.40), channel_id=1, source_target_pairs={{0,32},{16,48},{32,0},{48,16},{64,96},{80,112},{96,64},{112,80},{1... | collective-permute-start | bytes 294920 | tf_op jit(solution)/shard_map/ppermute | solution.py:389
  69.7 4.8 %collective-permute-start.13 = (bf16[96,128]{1,0:T(8,128)(2,1)S(1)}, bf16[96,128]{1,0:T(8,128)(2,1)S(1)}, u32[]{:S(2)}, u32[]{:S(2)}) collective-permute-start(bf16[96,128]{1,0:T(8,128)(2,1)S(1)} %get-tuple-element.41), channel_id=1, source_target_pairs={{0,68},{1,69},{2,70},{3,71},{4,64},{5,65},{6,66},{7,67},{8,76},{9,... | collective-permute-start | bytes 73736 | tf_op jit(solution)/shard_map/ppermute | solution.py:417
  71.0 3.8 %collective-permute-start.12 = (bf16[96,128]{1,0:T(8,128)(2,1)S(1)}, bf16[96,128]{1,0:T(8,128)(2,1)S(1)}, u32[]{:S(2)}, u32[]{:S(2)}) collective-permute-start(bf16[96,128]{1,0:T(8,128)(2,1)S(1)} %get-tuple-element.42), channel_id=1, source_target_pairs={{0,4},{1,5},{2,6},{3,7},{4,0},{5,1},{6,2},{7,3},{8,12},{9,13},{10,... | collective-permute-start | bytes 73736 | tf_op jit(solution)/shard_map/ppermute | solution.py:417
  72.2 3.8 %collective-permute-start.11 = (bf16[96,128]{1,0:T(8,128)(2,1)S(1)}, bf16[96,128]{1,0:T(8,128)(2,1)S(1)}, u32[]{:S(2)}, u32[]{:S(2)}) collective-permute-start(bf16[96,128]{1,0:T(8,128)(2,1)S(1)} %get-tuple-element.43), channel_id=1, source_target_pairs={{0,64},{1,65},{2,66},{3,67},{4,68},{5,69},{6,70},{7,71},{8,72},{9,... | collective-permute-start | bytes 73736 | tf_op jit(solution)/shard_map/ppermute | solution.py:417

commit v5 on v4

--- a/solution.py
+++ b/solution.py
@@ -399,8 +399,11 @@
     far = [out_grad] + [swap(late, "seq", HEADS, apart) for apart in (2, 8, 10)]
     grads, mine, give = attend(me[None].astype(jnp.int32), extents, received)
     got = swap(give, "seq", HEADS, 4)
-    _, *far = lax.optimization_barrier((give, *far))
-    near = [swap(x, "seq", HEADS, 1) for x in far]
+    near = [swap(out_grad, "seq", HEADS, 1)]
+    _, *far[1:] = lax.optimization_barrier((got, *far[1:]))
+    for x in far[1:]:
+        halves = [swap(x[i : i + 64], "seq", HEADS, 1) for i in (0, 64)]
+        near.append(jnp.concatenate(halves, axis=0))
     out_grads = [x for pair in zip(far, near) for x in pair]
     returned = lax.all_to_all(grads, "seq", 0, 0, tiled=True)
 

time: 77 us -> 78.6 us (1.021)
  waiting for transfers between devices: 28.7 us -> 30.7 us
  local copies, waits for them, and re-layouts: 1.61 us -> 0.12 us
  starting transfers between devices: 29 us -> 29.9 us
    ppermute x11 -> x14, starting transfers between devices: 12.4 us -> 14 us  [swap(): return lax.ppermute(x, axis, [(i, i ^ apart) for i in range(size)])]
    unnamed x8 -> x4, local copies, waits for them, and re-layouts: 1.57 us -> 0.01 us
    all_to_all x1, starting transfers between devices: 4.96 us -> 3.64 us  [local(): returned = lax.all_to_all(grads, 'seq', 0, 0, tiled=True)]
    ppermute x3, waiting for transfers between devices: 1.67 us -> 2.73 us  [local(): lax.ppermute(total[x_apart, z_apart].astype(BF16), ('dp', 'seq'), pairs)]
    ppermute x11 -> x14, waiting for transfers between devices: 7.57 us -> 8.54 us  [swap(): return lax.ppermute(x, axis, [(i, i ^ apart) for i in range(size)])]
  transfers between devices with their start and end apart: 16 -> 19, of which waited for: 8 -> 12; matrix products, arithmetic and copies ran while one was open for 0% -> 0% of each run, Pallas kernels for 15% -> 15%
where the time goes in v5:
time: 78.6 us; the launch traced here: 78.3 us
  waiting for transfers between devices  30.7 us (39%)
  starting transfers between devices  29.9 us (38%)
  Pallas kernels  16.6 us (21%)
  between operations  0.82 us (1%)
    all_to_all x1, waiting for transfers between devices, local(): received = lax.all_to_all(sent, 'seq', 0, 0, tiled=True)  19.5 us
    ppermute x14, starting transfers between devices, swap(): return lax.ppermute(x, axis, [(i, i ^ apart) for i in range(size)])  14 us
    pallas_call x1, Pallas kernels, attend(): pl.pallas_call(attend_body, out_shape=(jax.ShapeDtypeStruct((HEADS, 3 * H...  8.84 us
    ppermute x14, waiting for transfers between devices, swap(): return lax.ppermute(x, axis, [(i, i ^ apart) for i in range(size)])  8.54 us
    all_to_all x1, starting transfers between devices, local(): received = lax.all_to_all(sent, 'seq', 0, 0, tiled=True)  8.1 us
    ppermute x3, starting transfers between devices, local(): lax.ppermute(total[x_apart, z_apart].astype(BF16), ('dp', 'seq'), pairs)  4.18 us
    pallas_call x1, Pallas kernels, pack(): pl.pallas_call(pack_body, out_shape=jax.ShapeDtypeStruct(shape, BF16), in...  4.12 us
    all_to_all x1, starting transfers between devices, local(): returned = lax.all_to_all(grads, 'seq', 0, 0, tiled=True)  3.64 us
  transfers between devices with their start and end apart: 19, of which 12 were waited for; matrix products, arithmetic and copies ran while one was open for 0% of the time, Pallas kernels for 15%

profile of v5, /device:TPU:0, one launch (start us, length us, event | category | flops | bytes accessed | tf_op | source)
XLA Modules:
  0.0 78.3 jit_solution(17587249912644264883)
XLA Ops:
  0.6 4.1 %pack.1 = bf16[16,288,128]{2,1,0:T(8,128)(2,1)} custom-call(bf16[128,1152]{1,0:T(8,128)(2,1)} %q_hbm.1, bf16[128,1152]{1,0:T(8,128)(2,1)} %k_hbm.1, bf16[128,1152]{1,0:T(8,128)(2,1)} %v_hbm.1, bf16[128,1152]{1,0:T(8,128)(2,1)} %refs_0_.1, bf16[1152,1152]{1,0:T(8,128)(2,1)} %w_hbm.1), custom_call_target="tpu_custom_call" | custom-call | flops 10000000000 | tf_op jit(solution)/shard_map/pack/pallas_call | solution.py:79
  4.8 0.0 copy-start
  4.8 0.0 copy-start.1
  4.8 8.1 %all-to-all-start = ((bf16[16,288,128]{2,1,0:T(8,128)(2,1)}), bf16[16,288,128]{2,1,0:T(8,128)(2,1)S(1)}, u32[]{:S(2)}, u32[]{:S(2)}) async-start(bf16[16,288,128]{2,1,0:T(8,128)(2,1)} %pack.1), calls=%async_computation | async-start | bytes 2359296 | tf_op jit(solution)/shard_map/all_to_all | solution.py:397
  12.9 19.5 %all-to-all-done.r_ref = bf16[16,288,128]{2,1,0:T(8,128)(2,1)S(1)} async-done(((bf16[16,288,128]{2,1,0:T(8,128)(2,1)}), bf16[16,288,128]{2,1,0:T(8,128)(2,1)S(1)}, u32[]{:S(2)}, u32[]{:S(2)}) %all-to-all-start) | async-done | bytes 1179680 | tf_op jit(solution)/shard_map/all_to_all | solution.py:397
  32.4 0.0 copy-done
  32.4 0.9 %collective-permute-start.4 = (bf16[128,1152]{1,0:T(8,128)(2,1)S(1)}, bf16[128,1152]{1,0:T(8,128)(2,1)S(1)}, u32[]{:S(2)}, u32[]{:S(2)}) collective-permute-start(bf16[128,1152]{1,0:T(8,128)(2,1)S(1)} %copy-done), channel_id=1, source_target_pairs={{0,10},{1,11},{2,8},{3,9},{4,14},{5,15},{6,12},{7,13},{8,2},{9,3},... | collective-permute-start | bytes 884744 | tf_op jit(solution)/shard_map/ppermute | solution.py:389
  33.3 2.7 %collective-permute-start.3 = (bf16[128,1152]{1,0:T(8,128)(2,1)S(1)}, bf16[128,1152]{1,0:T(8,128)(2,1)S(1)}, u32[]{:S(2)}, u32[]{:S(2)}) collective-permute-start(bf16[128,1152]{1,0:T(8,128)(2,1)S(1)} %copy-done), channel_id=1, source_target_pairs={{0,8},{1,9},{2,10},{3,11},{4,12},{5,13},{6,14},{7,15},{8,0},{9,1},... | collective-permute-start | bytes 884744 | tf_op jit(solution)/shard_map/ppermute | solution.py:389
  36.1 2.8 %collective-permute-start.2 = (bf16[128,1152]{1,0:T(8,128)(2,1)S(1)}, bf16[128,1152]{1,0:T(8,128)(2,1)S(1)}, u32[]{:S(2)}, u32[]{:S(2)}) collective-permute-start(bf16[128,1152]{1,0:T(8,128)(2,1)S(1)} %copy-done), channel_id=1, source_target_pairs={{0,2},{1,3},{2,0},{3,1},{4,6},{5,7},{6,4},{7,5},{8,10},{9,11},{10,... | collective-permute-start | bytes 884744 | tf_op jit(solution)/shard_map/ppermute | solution.py:389
  38.9 0.0 copy-done.1
  38.9 8.8 %attend.1 = (bf16[16,216,128]{2,1,0:T(8,128)(2,1)}, bf16[8,72,128]{2,1,0:T(8,128)(2,1)S(1)}, bf16[8,72,128]{2,1,0:T(8,128)(2,1)S(1)}) custom-call(s32[1]{0:T(128)} %bitcast.me_ref, s32[1,8]{1,0:T(1,128)S(1)} %copy-done.1, bf16[16,288,128]{2,1,0:T(8,128)(2,1)S(1)} %all-to-all-done.r_ref), custom_call_target="tpu_custom_call" | custom-call | flops 10000000000 | tf_op jit(solution)/shard_map/attend/pallas_call | solution.py:273
  47.7 0.1 collective-permute-start
  47.8 0.1 collective-permute-start.1
  47.9 3.6 %all-to-all-start.1 = ((bf16[16,216,128]{2,1,0:T(8,128)(2,1)}), bf16[16,216,128]{2,1,0:T(8,128)(2,1)S(1)}, u32[]{:S(2)}, u32[]{:S(2)}) async-start(bf16[16,216,128]{2,1,0:T(8,128)(2,1)} %get-tuple-element.20), calls=%async_computation.1 | async-start | bytes 1769472 | tf_op jit(solution)/shard_map/all_to_all | solution.py:408
  51.6 1.4 %collective-permute-done.got_ref = bf16[8,72,128]{2,1,0:T(8,128)(2,1)S(1)} collective-permute-done((bf16[8,72,128]{2,1,0:T(8,128)(2,1)S(1)}, bf16[8,72,128]{2,1,0:T(8,128)(2,1)S(1)}, u32[]{:S(2)}, u32[]{:S(2)}) %collective-permute-start) | collective-permute-done | bytes 147488 | tf_op jit(solution)/shard_map/ppermute | solution.py:389
  52.9 0.0 collective-permute-done.4.refs_6_
  52.9 0.0 collective-permute-done.3.refs_4_
  53.0 0.0 collective-permute-done.2.refs_2_
  53.0 0.1 collective-permute-start.5
  53.1 0.5 collective-permute-start.6
  53.6 0.2 collective-permute-start.7
  53.8 0.4 collective-permute-start.8
  54.2 0.2 collective-permute-done.5
  54.4 0.1 collective-permute-start.9
  54.6 0.1 collective-permute-done.6
  54.7 0.3 collective-permute-start.10
  55.0 0.1 collective-permute-done.7
  55.1 0.2 collective-permute-done.8
  55.3 0.5 collective-permute-done.9
  55.8 0.2 collective-permute-done.10
  56.1 0.0 collective-permute-done.1.refs_1_
  56.1 1.8 %weight_terms.1 = bf16[8,2,96,128]{3,2,1,0:T(8,128)(2,1)S(1)} custom-call(s32[8]{0:T(128)S(1)} %fusion.2.tile_ref, bf16[8,72,128]{2,1,0:T(8,128)(2,1)S(1)} %get-tuple-element.24.mine_ref, bf16[8,72,128]{2,1,0:T(8,128)(2,1)S(1)} %collective-permute-done.got_ref, bf16[128,1152]{1,0:T(8,128)(2,1)S(1)} %copy-done, ...), custom_call_target="tpu_custom_call" | custom-call | flops 1000000000 | tf_op jit(solution)/shard_map/weight_terms/pallas_call | solution.py:359
  57.9 3.5 %collective-permute-start.11 = (bf16[2,2,96,128]{3,2,1,0:T(8,128)(2,1)S(1)}, bf16[2,2,96,128]{3,2,1,0:T(8,128)(2,1)S(1)}, u32[]{:S(2)}, u32[]{:S(2)}) collective-permute-start(bf16[2,2,96,128]{3,2,1,0:T(8,128)(2,1)S(1)} %get-tuple-element.36), channel_id=1, source_target_pairs={{0,16},{16,0},{32,48},{48,32},{64,80},{80,64},{96,112},{112,96},{1... | collective-permute-start | bytes 294920 | tf_op jit(solution)/shard_map/ppermute | solution.py:389
  61.4 0.3 collective-permute-start.13
  61.8 1.8 %collective-permute-start.12 = (bf16[2,2,96,128]{3,2,1,0:T(8,128)(2,1)S(1)}, bf16[2,2,96,128]{3,2,1,0:T(8,128)(2,1)S(1)}, u32[]{:S(2)}, u32[]{:S(2)}) collective-permute-start(bf16[2,2,96,128]{3,2,1,0:T(8,128)(2,1)S(1)} %get-tuple-element.38), channel_id=1, source_target_pairs={{0,32},{16,48},{32,0},{48,16},{64,96},{80,112},{96,64},{112,80},{1... | collective-permute-start | bytes 294920 | tf_op jit(solution)/shard_map/ppermute | solution.py:389
  63.6 1.1 %collective-permute-done.11 = bf16[2,2,96,128]{3,2,1,0:T(8,128)(2,1)S(1)} collective-permute-done((bf16[2,2,96,128]{3,2,1,0:T(8,128)(2,1)S(1)}, bf16[2,2,96,128]{3,2,1,0:T(8,128)(2,1)S(1)}, u32[]{:S(2)}, u32[]{:S(2)}) %collective-permute-start.11) | collective-permute-done | bytes 98336 | tf_op jit(solution)/shard_map/ppermute | solution.py:389
  64.7 4.8 %collective-permute-done.13 = bf16[2,2,96,128]{3,2,1,0:T(8,128)(2,1)S(1)} collective-permute-done((bf16[2,2,96,128]{3,2,1,0:T(8,128)(2,1)S(1)}, bf16[2,2,96,128]{3,2,1,0:T(8,128)(2,1)S(1)}, u32[]{:S(2)}, u32[]{:S(2)}) %collective-permute-start.13) | collective-permute-done | bytes 98336 | tf_op jit(solution)/shard_map/ppermute | solution.py:389
  69.5 0.0 collective-permute-done.12
  69.5 0.1 fusion.4
  69.6 2.9 %collective-permute-start.16 = (bf16[96,128]{1,0:T(8,128)(2,1)S(1)}, bf16[96,128]{1,0:T(8,128)(2,1)S(1)}, u32[]{:S(2)}, u32[]{:S(2)}) collective-permute-start(bf16[96,128]{1,0:T(8,128)(2,1)S(1)} %get-tuple-element.45), channel_id=1, source_target_pairs={{0,68},{1,69},{2,70},{3,71},{4,64},{5,65},{6,66},{7,67},{8,76},{9,... | collective-permute-start | bytes 73736 | tf_op jit(solution)/shard_map/ppermute | solution.py:420
  72.5 1.3 %collective-permute-start.15 = (bf16[96,128]{1,0:T(8,128)(2,1)S(1)}, bf16[96,128]{1,0:T(8,128)(2,1)S(1)}, u32[]{:S(2)}, u32[]{:S(2)}) collective-permute-start(bf16[96,128]{1,0:T(8,128)(2,1)S(1)} %get-tuple-element.46), channel_id=1, source_target_pairs={{0,4},{1,5},{2,6},{3,7},{4,0},{5,1},{6,2},{7,3},{8,12},{9,13},{10,... | collective-permute-start | bytes 73736 | tf_op jit(solution)/shard_map/ppermute | solution.py:420
  73.7 0.0 collective-permute-start.14
  73.7 0.0 all-to-all-done.1.y_ref
  73.8 1.1 %unpack.1 = (bf16[128,1152]{1,0:T(8,128)(2,1)}, bf16[128,1152]{1,0:T(8,128)(2,1)}, bf16[128,1152]{1,0:T(8,128)(2,1)}) custom-call(bf16[16,216,128]{2,1,0:T(8,128)(2,1)S(1)} %all-to-all-done.1.y_ref), custom_call_target="tpu_custom_call" | custom-call | flops 99999997952 | tf_op jit(solution)/shard_map/unpack/pallas_call | solution.py:333
  74.8 0.0 collective-permute-done.16.refs_2_
  74.8 1.5 %collective-permute-done.15.refs_1_ = bf16[96,128]{1,0:T(8,128)(2,1)S(1)} collective-permute-done((bf16[96,128]{1,0:T(8,128)(2,1)S(1)}, bf16[96,128]{1,0:T(8,128)(2,1)S(1)}, u32[]{:S(2)}, u32[]{:S(2)}) %collective-permute-start.15) | collective-permute-done | bytes 24608 | tf_op jit(solution)/shard_map/ppermute | solution.py:420
  76.3 1.3 %collective-permute-done.14.refs_0_ = bf16[96,128]{1,0:T(8,128)(2,1)S(1)} collective-permute-done((bf16[96,128]{1,0:T(8,128)(2,1)S(1)}, bf16[96,128]{1,0:T(8,128)(2,1)S(1)}, u32[]{:S(2)}, u32[]{:S(2)}) %collective-permute-start.14) | collective-permute-done | bytes 24608 | tf_op jit(solution)/shard_map/ppermute | solution.py:420
  77.6 0.7 finish.1
  (10 shorter events, 0.2 us)
Async XLA Ops:
  4.8 27.6 %copy-start = (bf16[128,1152]{1,0:T(8,128)(2,1)S(1)}, bf16[128,1152]{1,0:T(8,128)(2,1)}, u32[]{:S(2)}) copy-start(bf16[128,1152]{1,0:T(8,128)(2,1)} %refs_0_.1) | copy-start | bytes 884740
  4.8 34.1 %copy-start.1 = (s32[1,8]{1,0:T(1,128)S(1)}, s32[1,8]{1,0:T(1,128)}, u32[]{:S(2)}) copy-start(s32[1,8]{1,0:T(1,128)} %ext_ref.1) | copy-start | bytes 100
  4.8 27.6 %all-to-all-start = ((bf16[16,288,128]{2,1,0:T(8,128)(2,1)}), bf16[16,288,128]{2,1,0:T(8,128)(2,1)S(1)}, u32[]{:S(2)}, u32[]{:S(2)}) async-start(bf16[16,288,128]{2,1,0:T(8,128)(2,1)} %pack.1), calls=%async_computation | async-start | bytes 2359296 | tf_op jit(solution)/shard_map/all_to_all | solution.py:397
  32.4 20.6 %collective-permute-start.4 = (bf16[128,1152]{1,0:T(8,128)(2,1)S(1)}, bf16[128,1152]{1,0:T(8,128)(2,1)S(1)}, u32[]{:S(2)}, u32[]{:S(2)}) collective-permute-start(bf16[128,1152]{1,0:T(8,128)(2,1)S(1)} %copy-done), channel_id=1, source_target_pairs={{0,10},{1,11},{2,8},{3,9},{4,14},{5,15},{6,12},{7,13},{8,2},{9,3},... | collective-permute-start | bytes 884744 | tf_op jit(solution)/shard_map/ppermute | solution.py:389
  33.3 19.6 %collective-permute-start.3 = (bf16[128,1152]{1,0:T(8,128)(2,1)S(1)}, bf16[128,1152]{1,0:T(8,128)(2,1)S(1)}, u32[]{:S(2)}, u32[]{:S(2)}) collective-permute-start(bf16[128,1152]{1,0:T(8,128)(2,1)S(1)} %copy-done), channel_id=1, source_target_pairs={{0,8},{1,9},{2,10},{3,11},{4,12},{5,13},{6,14},{7,15},{8,0},{9,1},... | collective-permute-start | bytes 884744 | tf_op jit(solution)/shard_map/ppermute | solution.py:389
  36.1 16.9 %collective-permute-start.2 = (bf16[128,1152]{1,0:T(8,128)(2,1)S(1)}, bf16[128,1152]{1,0:T(8,128)(2,1)S(1)}, u32[]{:S(2)}, u32[]{:S(2)}) collective-permute-start(bf16[128,1152]{1,0:T(8,128)(2,1)S(1)} %copy-done), channel_id=1, source_target_pairs={{0,2},{1,3},{2,0},{3,1},{4,6},{5,7},{6,4},{7,5},{8,10},{9,11},{10,... | collective-permute-start | bytes 884744 | tf_op jit(solution)/shard_map/ppermute | solution.py:389
  47.7 5.2 %collective-permute-start = (bf16[8,72,128]{2,1,0:T(8,128)(2,1)S(1)}, bf16[8,72,128]{2,1,0:T(8,128)(2,1)S(1)}, u32[]{:S(2)}, u32[]{:S(2)}) collective-permute-start(bf16[8,72,128]{2,1,0:T(8,128)(2,1)S(1)} %get-tuple-element.25), channel_id=1, source_target_pairs={{0,4},{1,5},{2,6},{3,7},{4,0},{5,1},{6,2},{7,3},{8,12},{9,13},{10,... | collective-permute-start | bytes 442376 | tf_op jit(solution)/shard_map/ppermute | solution.py:389
  47.8 8.2 %collective-permute-start.1 = (bf16[128,1152]{1,0:T(8,128)(2,1)S(1)}, bf16[128,1152]{1,0:T(8,128)(2,1)S(1)}, u32[]{:S(2)}, u32[]{:S(2)}) collective-permute-start(bf16[128,1152]{1,0:T(8,128)(2,1)S(1)} %copy-done), channel_id=1, source_target_pairs={{0,1},{1,0},{2,3},{3,2},{4,5},{5,4},{6,7},{7,6},{8,9},{9,8},{10,11... | collective-permute-start | bytes 884744 | tf_op jit(solution)/shard_map/ppermute | solution.py:389
  47.9 25.8 %all-to-all-start.1 = ((bf16[16,216,128]{2,1,0:T(8,128)(2,1)}), bf16[16,216,128]{2,1,0:T(8,128)(2,1)S(1)}, u32[]{:S(2)}, u32[]{:S(2)}) async-start(bf16[16,216,128]{2,1,0:T(8,128)(2,1)} %get-tuple-element.20), calls=%async_computation.1 | async-start | bytes 1769472 | tf_op jit(solution)/shard_map/all_to_all | solution.py:408
  53.0 1.5 %collective-permute-start.5 = (bf16[64,1152]{1,0:T(8,128)(2,1)S(1)}, bf16[64,1152]{1,0:T(8,128)(2,1)S(1)}, u32[]{:S(2)}, u32[]{:S(2)}) collective-permute-start(bf16[64,1152]{1,0:T(8,128)(2,1)S(1)} %get-tuple-element.43), channel_id=1, source_target_pairs={{0,1},{1,0},{2,3},{3,2},{4,5},{5,4},{6,7},{7,6},{8,9},{9,8},{10,11... | collective-permute-start | bytes 442376 | tf_op jit(solution)/shard_map/ppermute | solution.py:389
  53.1 1.6 %collective-permute-start.6 = (bf16[64,1152]{1,0:T(8,128)(2,1)S(1)}, bf16[64,1152]{1,0:T(8,128)(2,1)S(1)}, u32[]{:S(2)}, u32[]{:S(2)}) collective-permute-start(bf16[64,1152]{1,0:T(8,128)(2,1)S(1)} %get-tuple-element.44), channel_id=1, source_target_pairs={{0,1},{1,0},{2,3},{3,2},{4,5},{5,4},{6,7},{7,6},{8,9},{9,8},{10,11... | collective-permute-start | bytes 442376 | tf_op jit(solution)/shard_map/ppermute | solution.py:389
  53.6 1.5 %collective-permute-start.7 = (bf16[64,1152]{1,0:T(8,128)(2,1)S(1)}, bf16[64,1152]{1,0:T(8,128)(2,1)S(1)}, u32[]{:S(2)}, u32[]{:S(2)}) collective-permute-start(bf16[64,1152]{1,0:T(8,128)(2,1)S(1)} %get-tuple-element.41), channel_id=1, source_target_pairs={{0,1},{1,0},{2,3},{3,2},{4,5},{5,4},{6,7},{7,6},{8,9},{9,8},{10,11... | collective-permute-start | bytes 442376 | tf_op jit(solution)/shard_map/ppermute | solution.py:389
  53.8 1.5 %collective-permute-start.8 = (bf16[64,1152]{1,0:T(8,128)(2,1)S(1)}, bf16[64,1152]{1,0:T(8,128)(2,1)S(1)}, u32[]{:S(2)}, u32[]{:S(2)}) collective-permute-start(bf16[64,1152]{1,0:T(8,128)(2,1)S(1)} %get-tuple-element.42), channel_id=1, source_target_pairs={{0,1},{1,0},{2,3},{3,2},{4,5},{5,4},{6,7},{7,6},{8,9},{9,8},{10,11... | collective-permute-start | bytes 442376 | tf_op jit(solution)/shard_map/ppermute | solution.py:389
  54.4 1.4 %collective-permute-start.9 = (bf16[64,1152]{1,0:T(8,128)(2,1)S(1)}, bf16[64,1152]{1,0:T(8,128)(2,1)S(1)}, u32[]{:S(2)}, u32[]{:S(2)}) collective-permute-start(bf16[64,1152]{1,0:T(8,128)(2,1)S(1)} %get-tuple-element.39), channel_id=1, source_target_pairs={{0,1},{1,0},{2,3},{3,2},{4,5},{5,4},{6,7},{7,6},{8,9},{9,8},{10,11... | collective-permute-start | bytes 442376 | tf_op jit(solution)/shard_map/ppermute | solution.py:389
  54.7 1.4 %collective-permute-start.10 = (bf16[64,1152]{1,0:T(8,128)(2,1)S(1)}, bf16[64,1152]{1,0:T(8,128)(2,1)S(1)}, u32[]{:S(2)}, u32[]{:S(2)}) collective-permute-start(bf16[64,1152]{1,0:T(8,128)(2,1)S(1)} %get-tuple-element.40), channel_id=1, source_target_pairs={{0,1},{1,0},{2,3},{3,2},{4,5},{5,4},{6,7},{7,6},{8,9},{9,8},{10,11... | collective-permute-start | bytes 442376 | tf_op jit(solution)/shard_map/ppermute | solution.py:389
  57.9 6.8 %collective-permute-start.11 = (bf16[2,2,96,128]{3,2,1,0:T(8,128)(2,1)S(1)}, bf16[2,2,96,128]{3,2,1,0:T(8,128)(2,1)S(1)}, u32[]{:S(2)}, u32[]{:S(2)}) collective-permute-start(bf16[2,2,96,128]{3,2,1,0:T(8,128)(2,1)S(1)} %get-tuple-element.36), channel_id=1, source_target_pairs={{0,16},{16,0},{32,48},{48,32},{64,80},{80,64},{96,112},{112,96},{1... | collective-permute-start | bytes 294920 | tf_op jit(solution)/shard_map/ppermute | solution.py:389
  61.4 8.0 %collective-permute-start.13 = (bf16[2,2,96,128]{3,2,1,0:T(8,128)(2,1)S(1)}, bf16[2,2,96,128]{3,2,1,0:T(8,128)(2,1)S(1)}, u32[]{:S(2)}, u32[]{:S(2)}) collective-permute-start(bf16[2,2,96,128]{3,2,1,0:T(8,128)(2,1)S(1)} %get-tuple-element.37), channel_id=1, source_target_pairs={{0,48},{16,32},{32,16},{48,0},{64,112},{80,96},{96,80},{112,64},{1... | collective-permute-start | bytes 294920 | tf_op jit(solution)/shard_map/ppermute | solution.py:389
  61.8 7.7 %collective-permute-start.12 = (bf16[2,2,96,128]{3,2,1,0:T(8,128)(2,1)S(1)}, bf16[2,2,96,128]{3,2,1,0:T(8,128)(2,1)S(1)}, u32[]{:S(2)}, u32[]{:S(2)}) collective-permute-start(bf16[2,2,96,128]{3,2,1,0:T(8,128)(2,1)S(1)} %get-tuple-element.38), channel_id=1, source_target_pairs={{0,32},{16,48},{32,0},{48,16},{64,96},{80,112},{96,64},{112,80},{1... | collective-permute-start | bytes 294920 | tf_op jit(solution)/shard_map/ppermute | solution.py:389
  69.6 5.3 %collective-permute-start.16 = (bf16[96,128]{1,0:T(8,128)(2,1)S(1)}, bf16[96,128]{1,0:T(8,128)(2,1)S(1)}, u32[]{:S(2)}, u32[]{:S(2)}) collective-permute-start(bf16[96,128]{1,0:T(8,128)(2,1)S(1)} %get-tuple-element.45), channel_id=1, source_target_pairs={{0,68},{1,69},{2,70},{3,71},{4,64},{5,65},{6,66},{7,67},{8,76},{9,... | collective-permute-start | bytes 73736 | tf_op jit(solution)/shard_map/ppermute | solution.py:420
  72.5 3.8 %collective-permute-start.15 = (bf16[96,128]{1,0:T(8,128)(2,1)S(1)}, bf16[96,128]{1,0:T(8,128)(2,1)S(1)}, u32[]{:S(2)}, u32[]{:S(2)}) collective-permute-start(bf16[96,128]{1,0:T(8,128)(2,1)S(1)} %get-tuple-element.46), channel_id=1, source_target_pairs={{0,4},{1,5},{2,6},{3,7},{4,0},{5,1},{6,2},{7,3},{8,12},{9,13},{10,... | collective-permute-start | bytes 73736 | tf_op jit(solution)/shard_map/ppermute | solution.py:420
  73.7 3.8 %collective-permute-start.14 = (bf16[96,128]{1,0:T(8,128)(2,1)S(1)}, bf16[96,128]{1,0:T(8,128)(2,1)S(1)}, u32[]{:S(2)}, u32[]{:S(2)}) collective-permute-start(bf16[96,128]{1,0:T(8,128)(2,1)S(1)} %get-tuple-element.47), channel_id=1, source_target_pairs={{0,64},{1,65},{2,66},{3,67},{4,68},{5,69},{6,70},{7,71},{8,72},{9,... | collective-permute-start | bytes 73736 | tf_op jit(solution)/shard_map/ppermute | solution.py:420
